TPU v7x, 32 devices: a whole 2x2x4 slice. The times are simulated.
32 devices in a mesh: seq: 8 (over z, y), ch: 4 (over x, core).
Axes of the slice: x: 2, y: 2, z: 4, core: 2. Of those that a mesh axis runs over, the one named last changes fastest.
Arguments:
- attn_query: bfloat16 [1024, 4096], P(('seq', 'ch')), may hold values from -6 to 6
- attn_key: bfloat16 [1024, 4096], P(('seq', 'ch')), may hold values from -6 to 6
- attn_value: bfloat16 [1024, 4096], P(('seq', 'ch')), may hold values from -6 to 6
- attn_output: bfloat16 [1024, 4096], P(('seq', 'ch')), may hold values from -1.796875 to 1.796875
- attn_grad_out: bfloat16 [1024, 4096], P(('seq', 'ch')), may hold values from -6 to 6
- conv_query: bfloat16 [1024, 8192], P(('seq', 'ch')), may hold values from -6 to 6
- conv_key: bfloat16 [1024, 8192], P(('seq', 'ch')), may hold values from -6 to 6
- conv_value: bfloat16 [1024, 8192], P(('seq', 'ch')), may hold values from -6 to 6
- conv_grad_out: bfloat16 [1024, 8192], P(('seq', 'ch')), may hold values from -6 to 6
- conv_filter: bfloat16 [512, 128], P('ch'), may hold values from -0.5 to 0.5
- doc_lengths: int32 [12], replicated, may hold values from 1 to 320, 1024 in all
Outputs:
- grad_attn_query: bfloat16 [1024, 4096], P(('seq', 'ch'))
- grad_attn_key: bfloat16 [1024, 4096], P(('seq', 'ch'))
- grad_attn_value: bfloat16 [1024, 4096], P(('seq', 'ch'))
- grad_conv_query: bfloat16 [1024, 8192], P(('seq', 'ch'))
- grad_conv_key: bfloat16 [1024, 8192], P(('seq', 'ch'))
- grad_conv_value: bfloat16 [1024, 8192], P(('seq', 'ch'))
- grad_filter: float32 [512, 128], P('ch')
Inputs may be any that keep to these rules, and one draw needn't show every extreme that they name: `doc_lengths`: the lengths of 12 documents laid end to end in the window; they sum to 1024 and the longest has exactly 320 positions.
All inputs are finite; a program needn't handle non-finite values.
Results may differ from a plain program's by a relative error of at most 0.0049.
Values may be sent and summed in bfloat16 or wider, within the bound.
No kernel may reach another device: no remote copies, remote signals or barrier semaphores. Data moves between devices by JAX's collectives and lax.ppermute only.
A program may use at most 128 MiB of HBM per device.

v0:
```python
import math

import jax
import jax.numpy as jnp
from jax import lax
from jax.sharding import PartitionSpec as P

HEAD_DIM = 128
GROUP = 16
FILTER_LEN = 128


NEG_FILL = -1e30


def passed_along(block, axis, distance):
    devices = range(lax.axis_size(axis))
    route = [(i - distance, i) for i in devices if i - distance in devices]
    return lax.ppermute(block, axis, route)


def doc_index(doc_lengths, positions):
    doc_ends = jnp.cumsum(doc_lengths)
    return jnp.sum((doc_ends[None, :] <= positions[:, None]).astype(jnp.int32), axis=1)


def split_rows(advance, carried, pieces):
    row_count = pieces[0].shape[0]

    def one_block(block_index, current):
        sub_parts = tuple(
            (
                lax.dynamic_slice_in_dim(shard_part, block_index * 512, 512, 0)
                for shard_part in pieces
            )
        )
        return advance(current, sub_parts, block_index * 512)

    return lax.fori_loop(0, row_count // 512, one_block, carried)


def banded(taps, row_count):
    group_count, tap_count = taps.shape
    span_count = row_count + tap_count - 1
    padded = jnp.pad(taps, ((0, 0), (0, row_count)))
    repeated = jnp.tile(padded, (1, row_count))[:, : row_count * span_count]
    return repeated.reshape(group_count, row_count, span_count)


def band_sums(matrix, tap_count):
    group_count, row_count, span_count = matrix.shape
    padded = jnp.pad(matrix, ((0, 0), (0, 0), (0, 1)))
    flattened = jnp.pad(
        padded.reshape(group_count, row_count * (span_count + 1)), ((0, 0), (0, row_count))
    )
    skewed = flattened.reshape(group_count, row_count, span_count + 2)
    return jnp.sum(skewed[:, :, :tap_count], axis=1)


def body(
    attn_query,
    attn_key,
    attn_value,
    attn_output,
    attn_grad_out,
    conv_query,
    conv_key,
    conv_value,
    conv_grad_out,
    conv_filter,
    doc_lengths,
):
    (
        query_rows,
        key_rows,
        value_rows,
        output_rows,
        grad_rows,
        mixer_query,
        mixer_key,
        mixer_value,
        mixer_grad,
    ) = (
        lax.all_to_all(attn_query, "ch", split_axis=1, concat_axis=0, tiled=True),
        lax.all_to_all(attn_key, "ch", split_axis=1, concat_axis=0, tiled=True),
        lax.all_to_all(attn_value, "ch", split_axis=1, concat_axis=0, tiled=True),
        lax.all_to_all(attn_output, "ch", split_axis=1, concat_axis=0, tiled=True),
        lax.all_to_all(attn_grad_out, "ch", split_axis=1, concat_axis=0, tiled=True),
        lax.all_to_all(conv_query, "ch", split_axis=1, concat_axis=0, tiled=True),
        lax.all_to_all(conv_key, "ch", split_axis=1, concat_axis=0, tiled=True),
        lax.all_to_all(conv_value, "ch", split_axis=1, concat_axis=0, tiled=True),
        lax.all_to_all(conv_grad_out, "ch", split_axis=1, concat_axis=0, tiled=True),
    )
    seq_count = lax.axis_size("seq")
    tok_rows = query_rows.shape[0]
    total_tokens = tok_rows * seq_count
    head_count = query_rows.shape[1] // HEAD_DIM
    scale_factor = 1.0 / math.sqrt(HEAD_DIM)
    row_base = lax.axis_index("seq") * tok_rows
    local_pos = row_base + jnp.arange(tok_rows, dtype=jnp.int32)
    local_doc = doc_index(doc_lengths, local_pos)
    query_heads = query_rows.reshape(tok_rows, head_count, HEAD_DIM)
    key_heads = key_rows.reshape(tok_rows, head_count, HEAD_DIM)
    value_heads = value_rows.reshape(tok_rows, head_count, HEAD_DIM)
    output_heads = output_rows.reshape(tok_rows, head_count, HEAD_DIM)
    grad_heads = grad_rows.reshape(tok_rows, head_count, HEAD_DIM)
    delta_rows = jnp.sum(grad_heads.astype(jnp.float32) * output_heads.astype(jnp.float32), axis=2)
    delta_heads = delta_rows.T

    def key_step(carried, pieces, key_start):
        key_part, value_part = pieces
        key_pos = key_start + jnp.arange(key_part.shape[0], dtype=jnp.int32)
        key_doc = doc_index(doc_lengths, key_pos)
        visible = (
            (key_doc[None, :] == local_doc[:, None])
            & (key_pos[None, :] <= local_pos[:, None])
            & (key_pos[None, :] >= 0)
        )
        running_max, running_sum, running_grad = carried
        scores = (
            jnp.einsum("thd,rhd->htr", query_heads, key_part, preferred_element_type=jnp.float32)
            * scale_factor
        )
        new_max = jnp.maximum(
            running_max, jnp.max(jnp.where(visible[None], scores, NEG_FILL), axis=2)
        )
        weights = jnp.where(visible[None], jnp.exp(scores - new_max[:, :, None]), 0.0)
        rescale = jnp.exp(running_max - new_max)
        grad_probs = jnp.einsum(
            "thd,rhd->htr", grad_heads, value_part, preferred_element_type=jnp.float32
        )
        weighted = weights * (grad_probs - delta_heads[:, :, None])
        update = jnp.einsum(
            "htr,rhd->htd", weighted, key_part.astype(jnp.float32), precision=lax.Precision.HIGHEST
        )
        return (
            new_max,
            running_sum * rescale + jnp.sum(weights, axis=2),
            running_grad * rescale[:, :, None] + update,
        )

    start_state = (
        jnp.full((head_count, tok_rows), NEG_FILL, jnp.float32),
        jnp.zeros((head_count, tok_rows), jnp.float32),
        jnp.zeros((head_count, tok_rows, HEAD_DIM), jnp.float32),
    )
    final_max, final_sum, final_grad = split_rows(
        key_step,
        start_state,
        (
            lax.all_gather(key_heads, "seq", axis=0, tiled=True),
            lax.all_gather(value_heads, "seq", axis=0, tiled=True),
        ),
    )
    lse_heads = final_max + jnp.log(final_sum)
    lse_rows = lse_heads.T
    grad_query = (final_grad * (scale_factor / final_sum)[:, :, None]).transpose(1, 0, 2)
    grad_query = grad_query.reshape(tok_rows, head_count * HEAD_DIM).astype(jnp.bfloat16)

    def query_step(carried, pieces, query_start, lse_part, delta_part):
        query_part, grad_part = pieces
        query_pos = query_start + jnp.arange(query_part.shape[0], dtype=jnp.int32)
        query_doc = doc_index(doc_lengths, query_pos)
        visible = (
            (query_doc[:, None] == local_doc[None, :])
            & (local_pos[None, :] <= query_pos[:, None])
            & (query_pos[:, None] < total_tokens)
        )
        key_grad, value_grad = carried
        scores = (
            jnp.einsum("rhd,thd->hrt", query_part, key_heads, preferred_element_type=jnp.float32)
            * scale_factor
        )
        probs = jnp.where(visible[None], jnp.exp(scores - lse_part.T[:, :, None]), 0.0)
        value_grad = value_grad + jnp.einsum(
            "hrt,rhd->thd", probs, grad_part.astype(jnp.float32), precision=lax.Precision.HIGHEST
        )
        grad_probs = jnp.einsum(
            "rhd,thd->hrt", grad_part, value_heads, preferred_element_type=jnp.float32
        )
        grad_scores = probs * (grad_probs - delta_part.T[:, :, None])
        key_grad = key_grad + scale_factor * jnp.einsum(
            "hrt,rhd->thd",
            grad_scores,
            query_part.astype(jnp.float32),
            precision=lax.Precision.HIGHEST,
        )
        return (key_grad, value_grad)

    zero_grads = (
        jnp.zeros((tok_rows, head_count, HEAD_DIM), jnp.float32),
        jnp.zeros((tok_rows, head_count, HEAD_DIM), jnp.float32),
    )
    lse_whole, delta_whole = (
        lax.all_gather(lse_rows, "seq", axis=0, tiled=True),
        lax.all_gather(delta_rows, "seq", axis=0, tiled=True),
    )

    def sliced_step(current, sub_parts, part_start):
        part_rows = sub_parts[0].shape[0]
        lse_part = lax.dynamic_slice_in_dim(lse_whole, part_start, part_rows, 0)
        delta_part = lax.dynamic_slice_in_dim(delta_whole, part_start, part_rows, 0)
        return query_step(current, sub_parts, part_start, lse_part, delta_part)

    key_grad, value_grad = split_rows(
        sliced_step,
        zero_grads,
        (
            lax.all_gather(query_heads, "seq", axis=0, tiled=True),
            lax.all_gather(grad_heads, "seq", axis=0, tiled=True),
        ),
    )
    grad_key = key_grad.reshape(tok_rows, head_count * HEAD_DIM).astype(jnp.bfloat16)
    grad_value = value_grad.reshape(tok_rows, head_count * HEAD_DIM).astype(jnp.bfloat16)
    grad_attn_query, grad_attn_key, grad_attn_value = (
        lax.all_to_all(grad_query, "ch", split_axis=0, concat_axis=1, tiled=True),
        lax.all_to_all(grad_key, "ch", split_axis=0, concat_axis=1, tiled=True),
        lax.all_to_all(grad_value, "ch", split_axis=0, concat_axis=1, tiled=True),
    )
    chan_count = mixer_query.shape[1]
    group_count = conv_filter.shape[0]
    ext_rows = tok_rows + FILTER_LEN
    mixed_input = (mixer_key.astype(jnp.float32) * mixer_value.astype(jnp.float32)).astype(
        jnp.bfloat16
    )
    prior_rows = passed_along(mixed_input[tok_rows - (FILTER_LEN - 1) :], "seq", 1)
    extended = jnp.concatenate(
        (jnp.zeros((1, chan_count), jnp.bfloat16), prior_rows, mixed_input), axis=0
    )
    ext_pos = row_base - FILTER_LEN + jnp.arange(ext_rows, dtype=jnp.int32)
    ext_doc = doc_index(doc_lengths, ext_pos)
    back_mask = ((local_doc[:, None] == ext_doc[None, :]) & (ext_pos[None, :] >= 0)).astype(
        jnp.bfloat16
    )
    reversed_taps = jnp.pad(conv_filter[:, ::-1], ((0, 0), (1, 0)))
    toeplitz = banded(reversed_taps, tok_rows) * back_mask[None]
    ext_groups = extended.reshape(ext_rows, group_count, GROUP)
    conv_out = jnp.einsum(
        "gts,sgc->tgc", toeplitz, ext_groups, preferred_element_type=jnp.float32
    ).reshape(tok_rows, chan_count)
    grad_mixer_query = (mixer_grad.astype(jnp.float32) * conv_out).astype(jnp.bfloat16)
    out_grad = (mixer_grad.astype(jnp.float32) * mixer_query.astype(jnp.float32)).astype(
        jnp.bfloat16
    )
    out_groups = out_grad.reshape(tok_rows, group_count, GROUP)
    block_size = math.gcd(group_count, 16)
    block_count = group_count // block_size
    out_blocks = out_groups.reshape(tok_rows, block_count, block_size, GROUP).transpose(1, 0, 2, 3)
    ext_blocks = ext_groups.reshape(ext_rows, block_count, block_size, GROUP).transpose(1, 0, 2, 3)

    def tap_block(block_parts):
        out_part, ext_part = block_parts
        outer = (
            jnp.einsum("tgc,sgc->gts", out_part, ext_part, preferred_element_type=jnp.float32)
            * back_mask[None]
        )
        return band_sums(outer, FILTER_LEN + 1)

    tap_sums = lax.map(tap_block, (out_blocks, ext_blocks)).reshape(group_count, FILTER_LEN + 1)
    tap_grad = tap_sums[:, 1:][:, ::-1]
    grad_filter = lax.psum(tap_grad, "seq")
    later_rows = passed_along(out_grad[: FILTER_LEN - 1], "seq", -1)
    ahead = jnp.concatenate(
        (out_grad, later_rows, jnp.zeros((1, chan_count), jnp.bfloat16)), axis=0
    ).reshape(ext_rows, group_count, GROUP)
    ahead_pos = row_base + jnp.arange(ext_rows, dtype=jnp.int32)
    ahead_doc = doc_index(doc_lengths, ahead_pos)
    front_mask = (
        (local_doc[:, None] == ahead_doc[None, :]) & (ahead_pos[None, :] < total_tokens)
    ).astype(jnp.bfloat16)
    forward_taps = banded(jnp.pad(conv_filter, ((0, 0), (0, 1))), tok_rows) * front_mask[None]
    input_grad = jnp.einsum(
        "gst,tgc->sgc", forward_taps, ahead, preferred_element_type=jnp.float32
    ).reshape(tok_rows, chan_count)
    grad_mixer_key = (input_grad * mixer_value.astype(jnp.float32)).astype(jnp.bfloat16)
    grad_mixer_value = (input_grad * mixer_key.astype(jnp.float32)).astype(jnp.bfloat16)
    grad_conv_query, grad_conv_key, grad_conv_value = (
        lax.all_to_all(grad_mixer_query, "ch", split_axis=0, concat_axis=1, tiled=True),
        lax.all_to_all(grad_mixer_key, "ch", split_axis=0, concat_axis=1, tiled=True),
        lax.all_to_all(grad_mixer_value, "ch", split_axis=0, concat_axis=1, tiled=True),
    )
    return (
        grad_attn_query,
        grad_attn_key,
        grad_attn_value,
        grad_conv_query,
        grad_conv_key,
        grad_conv_value,
        grad_filter,
    )


def solution(mesh):
    return jax.shard_map(
        body,
        mesh=mesh,
        in_specs=(
            P(("seq", "ch"), None),
            P(("seq", "ch"), None),
            P(("seq", "ch"), None),
            P(("seq", "ch"), None),
            P(("seq", "ch"), None),
            P(("seq", "ch"), None),
            P(("seq", "ch"), None),
            P(("seq", "ch"), None),
            P(("seq", "ch"), None),
            P("ch", None),
            P(),
        ),
        out_specs=(
            P(("seq", "ch"), None),
            P(("seq", "ch"), None),
            P(("seq", "ch"), None),
            P(("seq", "ch"), None),
            P(("seq", "ch"), None),
            P(("seq", "ch"), None),
            P("ch", None),
        ),
        check_vma=False,
    )
```

profile of v0, /device:TPU:0, one launch (start us, length us, event | category | flops | bytes accessed | tf_op | source)
XLA Modules:
  0.0 536.5 jit_solution(13356400532149911708)
XLA Ops:
  8.2 10.0 %all_to_all.225 = bf16[32,4,1024]{2,0,1:T(8,128)(2,1)S(1)} all-to-all(bf16[32,4,1024]{2,0,1:T(8,128)(2,1)S(1)} %bitcast.238), channel_id=1, replica_groups=mesh['seq'=8,'ch'=4] {'ch'}, dimensions={1} | all-to-all | bytes 524288 | tf_op jit(solution)/shard_map/all_to_all | solution.py:85
  20.1 8.4 %all_to_all.226 = bf16[32,4,1024]{2,0,1:T(8,128)(2,1)S(1)} all-to-all(bf16[32,4,1024]{2,0,1:T(8,128)(2,1)S(1)} %bitcast.239), channel_id=1, replica_groups=mesh['seq'=8,'ch'=4] {'ch'}, dimensions={1} | all-to-all | bytes 524288 | tf_op jit(solution)/shard_map/all_to_all | solution.py:86
  29.4 8.6 %all_to_all.227 = bf16[32,4,1024]{2,0,1:T(8,128)(2,1)S(1)} all-to-all(bf16[32,4,1024]{2,0,1:T(8,128)(2,1)S(1)} %bitcast.240), channel_id=1, replica_groups=mesh['seq'=8,'ch'=4] {'ch'}, dimensions={1} | all-to-all | bytes 524288 | tf_op jit(solution)/shard_map/all_to_all | solution.py:88
  43.9 8.0 %all-to-all-done.10 = bf16[32,4,2048]{2,0,1:T(8,128)(2,1)S(1)} async-done(((bf16[32,4,2048]{2,0,1:T(8,128)(2,1)}), bf16[32,4,2048]{2,0,1:T(8,128)(2,1)S(1)}, u32[]{:S(2)}, u32[]{:S(2)}) %all-to-all-start.10) | async-done | bytes 524320 | tf_op jit(solution)/shard_map/all_to_all | solution.py:91
  56.3 8.0 %all-to-all-done.9 = bf16[32,4,2048]{2,0,1:T(8,128)(2,1)S(1)} async-done(((bf16[32,4,2048]{2,0,1:T(8,128)(2,1)}), bf16[32,4,2048]{2,0,1:T(8,128)(2,1)S(1)}, u32[]{:S(2)}, u32[]{:S(2)}) %all-to-all-start.9) | async-done | bytes 524320 | tf_op jit(solution)/shard_map/all_to_all | solution.py:90
  69.6 7.0 %all-to-all-done.8 = bf16[32,4,2048]{2,0,1:T(8,128)(2,1)S(1)} async-done(((bf16[32,4,2048]{2,0,1:T(8,128)(2,1)}), bf16[32,4,2048]{2,0,1:T(8,128)(2,1)S(1)}, u32[]{:S(2)}, u32[]{:S(2)}) %all-to-all-start.8) | async-done | bytes 524320 | tf_op jit(solution)/shard_map/all_to_all | solution.py:92
  103.5 4.5 tile.20
  107.9 12.9 %tile.21 = bf16[128,32896]{0,1:T(8,128)(2,1)} reshape(bf16[128,128,257]{0,2,1:T(8,128)(2,1)} %tile.20) | data formatting | bytes 16842752 | tf_op jit(solution)/shard_map/tile | solution.py:46
  120.8 7.2 %slice.31 = bf16[128,32768]{0,1:T(8,128)(2,1)} slice(bf16[128,32896]{0,1:T(8,128)(2,1)} %tile.21), slice={[0:128], [0:32768]} | slice | bytes 16777216 | tf_op jit(solution)/shard_map/slice | solution.py:46
  128.0 12.6 %copy.248 = bf16[128,128,256]{2,1,0:T(8,128)(2,1)} copy(bf16[128,128,256]{0,2,1:T(8,128)(2,1)} %bitcast.213) | data formatting | bytes 16777216 | tf_op jit(solution)/shard_map/reshape | solution.py:47
  140.8 4.5 tile.8
  145.3 12.9 %tile.9 = bf16[128,32896]{0,1:T(8,128)(2,1)} reshape(bf16[128,128,257]{0,2,1:T(8,128)(2,1)} %tile.8) | data formatting | bytes 16842752 | tf_op jit(solution)/shard_map/tile | solution.py:46
  158.2 7.2 %slice.29 = bf16[128,32768]{0,1:T(8,128)(2,1)} slice(bf16[128,32896]{0,1:T(8,128)(2,1)} %tile.9), slice={[0:128], [0:32768]} | slice | bytes 16777216 | tf_op jit(solution)/shard_map/slice | solution.py:46
  165.4 12.8 %copy.242 = bf16[128,128,256]{2,1,0:T(8,128)(2,1)} copy(bf16[128,128,256]{0,2,1:T(8,128)(2,1)} %bitcast.214) | data formatting | bytes 16777216 | tf_op jit(solution)/shard_map/reshape | solution.py:47
  183.9 33.4 %all_gather.23 = f32[1024,8]{1,0:T(8,128)} all-gather(f32[128,8]{1,0:T(8,128)S(1)} %multiply_reduce_fusion), channel_id=1, replica_groups=mesh['seq'=8,'ch'=4] {'seq'}, dimensions={0}, use_global_device_ids=true | all-gather | bytes 36864 | tf_op jit(solution)/shard_map/all_gather | solution.py:196
  223.9 6.0 %fusion.61 = f32[128,128,16]{0,2,1:T(8,128)S(1)} fusion(bf16[256,128,16]{0,2,1:T(8,128)(2,1)} %bitcast.220, bf16[128,128,256]{2,1,0:T(8,128)(2,1)} %copy.248, bf16[128,256]{1,0:T(8,128)(2,1)S(1)} %copy-done.22), kind=kOutput, calls=%fused_computation.78 | convolution fusion | flops 138412032 | bytes 10551296 | tf_op jit(solution)/shard_map/gst,tgc->sgc/dot_general | solution.py:272
  244.0 6.3 %fusion.58 = f32[128,128,16]{0,2,1:T(8,128)S(1)} fusion(bf16[256,128,16]{0,2,1:T(8,128)(2,1)} %bitcast.16, bf16[128,128,256]{2,1,0:T(8,128)(2,1)} %copy.242, bf16[128,256]{1,0:T(8,128)(2,1)S(1)} %copy-done.21), kind=kOutput, calls=%fused_computation.77 | convolution fusion | flops 138412032 | bytes 10551296 | tf_op jit(solution)/shard_map/gts,sgc->tgc/dot_general | solution.py:238
  262.1 17.5 %while.52 = (s32[]{:T(128)}, f32[8,128]{1,0:T(8,128)S(1)}, f32[8,128]{1,0:T(8,128)S(1)}, f32[8,128,128]{2,1,0:T(8,128)}, s32[1,12]{1,0:T(1,128)S(1)}, /*index=5*...) while((s32[]{:T(128)}, f32[8,128]{1,0:T(8,128)S(1)}, ...), condition=%wide.region_7.8_spmd.clone, body=%wide.region_3.7_spmd.clone.sunk | while | flops 1080713344 | bytes 34423732 | solution.py:39
  285.3 30.4 %all_gather.21 = f32[1024,8]{0,1:T(8,128)S(1)} all-gather(f32[128,8]{0,1:T(8,128)S(1)} %get-tuple-element.968), channel_id=1, replica_groups=mesh['seq'=8,'ch'=4] {'seq'}, dimensions={0}, use_global_device_ids=true | all-gather | bytes 36864 | tf_op jit(solution)/shard_map/all_gather | solution.py:195
  315.7 4.3 all-to-all-start.5
  320.1 21.3 %while.53 = (s32[]{:T(128)}, f32[128,8,128]{0,2,1:T(8,128)}, f32[128,8,128]{0,2,1:T(8,128)}, bf16[1024,8,128]{2,1,0:T(8,128)(2,1)}, s32[1,12]{1,0:T(1,128)S(1)},...) while((s32[]{:T(128)}, f32[128,8,128]{0,2,1:T(8,128)}, ...), condition=%wide.region_10.11_spmd.clone, body=%wide.region_8.10_spmd.clone.sunk | while | flops 1882606720 | bytes 31175524 | solution.py:39
  357.1 99.7 %while.51 = (s32[]{:T(128)}, f32[8,16,129]{2,1,0:T(8,128)}, bf16[8,128,16,16]{1,3,2,0:T(8,128)(2,1)}, bf16[8,256,16,16]{1,3,2,0:T(8,128)(2,1)}, s32[256]{0:T(256...) while((s32[]{:T(128)}, f32[8,16,129]{2,1,0:T(8,128)}, ...), condition=%wide.region_15.16_spmd.clone, body=%wide.region_13.15_spmd.clone.sunk | while | flops 17694704 | bytes 20508132 | solution.py:259
  377.0 4.2 reshape.478
  467.2 61.3 %all-reduce.8.cloned.1.call-done = f32[128,128]{1,0:T(8,128)} async-done(((f32[128,128]{1,0:T(8,128)}), f32[128,128]{1,0:T(8,128)}) %all-reduce.8.cloned.1.call-update) | async-done | bytes 65552 | tf_op jit(solution)/shard_map/psum | solution.py:261
  (299 shorter events, 251.0 us)
Async XLA Ops:
  7.2 22.2 %copy-start.23 = (bf16[32,4096]{1,0:T(8,128)(2,1)S(1)}, bf16[32,4096]{1,0:T(8,128)(2,1)}, u32[]{:S(2)}) copy-start(bf16[32,4096]{1,0:T(8,128)(2,1)} %param.21) | copy-start | bytes 786436
  7.2 254.9 %all-gather.5.cloned.1.call-start = ((), (), s32[]{:S(2)}) async-start(), calls=%async_computation.15 | async-start | bytes 2359296 | tf_op jit(solution)/shard_map/all_gather | solution.py:151
  19.1 243.0 %all-gather.7.cloned.1.call-start = ((), (), s32[]{:S(2)}) async-start(), calls=%async_computation.16 | async-start | bytes 2359296 | tf_op jit(solution)/shard_map/all_gather | solution.py:152
  29.3 290.7 %all-gather.11.cloned.1.call-start = ((), (), s32[]{:S(2)}) async-start(), calls=%async_computation.18 | async-start | bytes 2359296 | tf_op jit(solution)/shard_map/all_gather | solution.py:210
  39.6 12.3 %all-to-all-start.10 = ((bf16[32,4,2048]{2,0,1:T(8,128)(2,1)}), bf16[32,4,2048]{2,0,1:T(8,128)(2,1)S(1)}, u32[]{:S(2)}, u32[]{:S(2)}) async-start(bf16[32,4,2048]{2,0,1:T(8,128)(2,1)} %bitcast.170), calls=%async_computation.10 | async-start | bytes 1048576 | tf_op jit(solution)/shard_map/all_to_all | solution.py:91
  43.1 24.7 %copy-start.20 = (bf16[32,8192]{1,0:T(8,128)(2,1)S(1)}, bf16[32,8192]{1,0:T(8,128)(2,1)}, u32[]{:S(2)}) copy-start(bf16[32,8192]{1,0:T(8,128)(2,1)} %param.22) | copy-start | bytes 1572868
  51.9 12.4 %all-to-all-start.9 = ((bf16[32,4,2048]{2,0,1:T(8,128)(2,1)}), bf16[32,4,2048]{2,0,1:T(8,128)(2,1)S(1)}, u32[]{:S(2)}, u32[]{:S(2)}) async-start(bf16[32,4,2048]{2,0,1:T(8,128)(2,1)} %bitcast.171), calls=%async_computation.9 | async-start | bytes 1048576 | tf_op jit(solution)/shard_map/all_to_all | solution.py:90
  64.3 12.3 %all-to-all-start.8 = ((bf16[32,4,2048]{2,0,1:T(8,128)(2,1)}), bf16[32,4,2048]{2,0,1:T(8,128)(2,1)S(1)}, u32[]{:S(2)}, u32[]{:S(2)}) async-start(bf16[32,4,2048]{2,0,1:T(8,128)(2,1)} %bitcast.172), calls=%async_computation.8 | async-start | bytes 1048576 | tf_op jit(solution)/shard_map/all_to_all | solution.py:92
  76.6 12.3 %all-to-all-start.12 = ((bf16[32,4,2048]{2,0,1:T(8,128)(2,1)}), bf16[32,4,2048]{2,0,1:T(8,128)(2,1)S(1)}, u32[]{:S(2)}, u32[]{:S(2)}) async-start(bf16[32,4,2048]{2,0,1:T(8,128)(2,1)} %bitcast.169), calls=%async_computation.12 | async-start | bytes 1048576 | tf_op jit(solution)/shard_map/all_to_all | solution.py:89
  80.2 23.0 %copy-start.27 = (bf16[128,128]{1,0:T(8,128)(2,1)S(1)}, bf16[128,128]{1,0:T(8,128)(2,1)}, u32[]{:S(2)}) copy-start(bf16[128,128]{1,0:T(8,128)(2,1)} %param.26) | copy-start | bytes 98308
  81.2 137.4 %collective-permute-start = (bf16[127,2048]{1,0:T(8,128)(2,1)}, bf16[127,2048]{1,0:T(8,128)(2,1)}, u32[]{:S(2)}, u32[]{:S(2)}) collective-permute-start(bf16[127,2048]{1,0:T(8,128)(2,1)} %slice.28), channel_id=1, source_target_pairs={{0,4},{4,8},{8,12},{12,16},{16,20},{20,24},{24,28},{1,5},{5,9},{9,... | collective-permute-start | bytes 1560584 | tf_op jit(solution)/shard_map/ppermute | solution.py:19
  88.9 9.4 %all-to-all-start.4 = ((bf16[32,4,1024]{2,0,1:T(8,128)(2,1)}), bf16[32,4,1024]{2,0,1:T(8,128)(2,1)S(1)}, u32[]{:S(2)}, u32[]{:S(2)}) async-start(bf16[32,4,1024]{2,0,1:T(8,128)(2,1)} %bitcast.173), calls=%async_computation.4 | async-start | bytes 524288 | tf_op jit(solution)/shard_map/all_to_all | solution.py:87
  92.4 126.2 %copy-start.8 = (bf16[32,4,2048]{2,0,1:T(8,128)(2,1)}, bf16[32,4,2048]{2,0,1:T(8,128)(2,1)S(1)}, u32[]{:S(2)}) copy-start(bf16[32,4,2048]{2,0,1:T(8,128)(2,1)S(1)} %fusion.71) | copy-start | bytes 1572868
  92.4 126.2 %collective-permute-start.1 = (bf16[127,2048]{1,0:T(8,128)(2,1)S(1)}, bf16[127,2048]{1,0:T(8,128)(2,1)}, u32[]{:S(2)}, u32[]{:S(2)}) collective-permute-start(bf16[127,2048]{1,0:T(8,128)(2,1)S(1)} %bitcast.215), channel_id=1, source_target_pairs={{4,0},{8,4},{12,8},{16,12},{20,16},{24,20},{28,24},{5,1},{9,5},{13... | collective-permute-start | bytes 1560584 | tf_op jit(solution)/shard_map/ppermute | solution.py:19
  98.3 83.8 %all-to-all-start.1 = ((bf16[32,4,1024]{2,0,1:T(8,128)(2,1)}), bf16[32,4,1024]{2,0,1:T(8,128)(2,1)}, u32[]{:S(2)}, u32[]{:S(2)}) async-start(bf16[32,4,1024]{2,0,1:T(8,128)(2,1)} %bitcast.176), calls=%async_computation.1 | async-start | bytes 524288 | tf_op jit(solution)/shard_map/all_to_all | solution.py:84
  102.4 217.7 %all-gather.9.cloned.1.call-start = ((), (), s32[]{:S(2)}) async-start(), calls=%async_computation.17 | async-start | bytes 2359296 | tf_op jit(solution)/shard_map/all_gather | solution.py:209
  183.1 35.4 %copy-start.12 = (bf16[16,8,8,128]{3,2,1,0:T(8,128)(2,1)}, bf16[16,8,8,128]{3,2,1,0:T(8,128)(2,1)S(1)}, u32[]{:S(2)}) copy-start(bf16[16,8,8,128]{3,2,1,0:T(8,128)(2,1)S(1)} %copy.282) | copy-start | bytes 786436
  237.9 20.0 %all-to-all-start.13 = ((bf16[4,32,2048]{2,1,0:T(8,128)(2,1)}), bf16[4,32,2048]{2,1,0:T(8,128)(2,1)S(1)}, u32[]{:S(2)}, u32[]{:S(2)}) async-start(bf16[4,32,2048]{2,1,0:T(8,128)(2,1)} %get-tuple-element.965), calls=%async_computation.13 | async-start | bytes 1048576 | tf_op jit(solution)/shard_map/all_to_all | solution.py:279
  257.9 21.7 %all-to-all-start.14 = ((bf16[4,32,2048]{2,1,0:T(8,128)(2,1)}), bf16[4,32,2048]{2,1,0:T(8,128)(2,1)}, u32[]{:S(2)}, u32[]{:S(2)}) async-start(bf16[4,32,2048]{2,1,0:T(8,128)(2,1)} %get-tuple-element.964), calls=%async_computation.14 | async-start | bytes 1048576 | tf_op jit(solution)/shard_map/all_to_all | solution.py:280
  279.6 36.1 %all-to-all-start.11 = ((bf16[4,32,2048]{2,1,0:T(8,128)(2,1)}), bf16[4,32,2048]{2,1,0:T(8,128)(2,1)S(1)}, u32[]{:S(2)}, u32[]{:S(2)}) async-start(bf16[4,32,2048]{2,1,0:T(8,128)(2,1)} %fusion.70), calls=%async_computation.11 | async-start | bytes 1048576 | tf_op jit(solution)/shard_map/all_to_all | solution.py:278
  315.7 27.8 %all-to-all-start.5 = ((bf16[4,32,1024]{2,1,0:T(8,128)(2,1)}), bf16[4,32,1024]{2,1,0:T(8,128)(2,1)}, u32[]{:S(2)}, u32[]{:S(2)}) async-start(bf16[4,32,1024]{2,1,0:T(8,128)(2,1)} %convert_element_type.199), calls=%async_computation.5 | async-start | bytes 524288 | tf_op jit(solution)/shard_map/all_to_all | solution.py:216
  343.5 9.4 %all-to-all-start.6 = ((bf16[4,32,1024]{2,1,0:T(8,128)(2,1)}), bf16[4,32,1024]{2,1,0:T(8,128)(2,1)S(1)}, u32[]{:S(2)}, u32[]{:S(2)}) async-start(bf16[4,32,1024]{2,1,0:T(8,128)(2,1)} %convert_element_type.201), calls=%async_computation.6 | async-start | bytes 524288 | tf_op jit(solution)/shard_map/all_to_all | solution.py:217
  353.0 112.6 %all-to-all-start.7 = ((bf16[4,32,1024]{2,1,0:T(8,128)(2,1)}), bf16[4,32,1024]{2,1,0:T(8,128)(2,1)}, u32[]{:S(2)}, u32[]{:S(2)}) async-start(bf16[4,32,1024]{2,1,0:T(8,128)(2,1)} %convert_element_type.203), calls=%async_computation.7 | async-start | bytes 524288 | tf_op jit(solution)/shard_map/all_to_all | solution.py:218
  357.0 171.5 %all-reduce.8.cloned.1.call-start = ((), (), s32[]{:S(2)}) async-start(), calls=%async_computation.19 | async-start | bytes 131072 | tf_op jit(solution)/shard_map/psum | solution.py:261
  (33 other events, 174.6 us)
Sparse Core Ops, SparseCore 0:
  19.2 49.5 all-gather.4
  71.5 62.2 all-gather.6
  135.9 47.5 all-gather.10
  218.7 50.8 all-gather.8
  458.7 69.7 all-reduce.7
where the time goes:
time: 541 us; the launch traced here: 537 us
  local copies, waits for them, and re-layouts  228 us (42%)
  waiting for transfers between devices  92.4 us (17%)
  blocking collectives  90.9 us (17%)
  starting transfers between devices  50.3 us (9%)
  matrix products  45.9 us (8%)
  other arithmetic  14.4 us (3%)
  between operations  14.3 us (3%)
    psum x1, waiting for transfers between devices, body(): grad_filter = lax.psum(tap_grad, 'seq')  61.3 us
    another operation x4, local copies, waits for them, and re-layouts, banded(): repeated = jnp.tile(padded, (1, row_count))[:, :row_count * span_count]  34.8 us
    reshape x8, local copies, waits for them, and re-layouts, band_sums(): skewed = flattened.reshape(group_count, row_count, span_count + 2)  33.9 us
    all_gather x1, blocking collectives, body(): lax.all_gather(delta_rows, 'seq', axis=0, tiled=True)  33.4 us
    all_gather x1, blocking collectives, body(): lax.all_gather(lse_rows, 'seq', axis=0, tiled=True)  30.4 us
    reshape x2, local copies, waits for them, and re-layouts, banded(): return repeated.reshape(group_count, row_count, span_count)  25.4 us
    pad x8, local copies, waits for them, and re-layouts, band_sums(): jnp.pad(padded.reshape(group_count, row_count * (span_count + 1)), ((0, 0...  24.6 us
    reshape x8, local copies, waits for them, and re-layouts, band_sums(): padded.reshape(group_count, row_count * (span_count + 1))  19.9 us
  transfers between devices with their start and end apart: 19, of which 7 were waited for; matrix products, arithmetic and copies ran while one was open for 52% of the time, Pallas kernels for 0%

commit v1 on v0

v1 whole, which is shorter than its diff:
```python
import functools
import math

import jax
import jax.numpy as jnp
from jax import lax
from jax.experimental import pallas as pl
from jax.experimental.pallas import tpu as pltpu
from jax.sharding import PartitionSpec as P

HEAD_DIM = 128
GROUP = 16
FILTER_LEN = 128
LANES = 128
BAND_REACH = 320
DEVICES = ("seq", "ch")
NEG_FILL = -1e30
BF16 = jnp.bfloat16
F32 = jnp.float32

NT = (((1,), (1,)), ((), ()))
NN = (((1,), (0,)), ((), ()))
TN = (((0,), (0,)), ((), ()))


def dot(a, b, dims):
    return lax.dot_general(a, b, dims, preferred_element_type=F32)


def params():
    return pltpu.CompilerParams(vmem_limit_bytes=40 * 1024 * 1024)


def cost(flops, bytes_accessed):
    return pl.CostEstimate(flops=flops, bytes_accessed=bytes_accessed, transcendentals=0)


def doc_start(lens_ref, positions):
    start = jnp.zeros_like(positions)
    end = jnp.int32(0)
    for d in range(lens_ref.shape[0]):
        end = end + lens_ref[d]
        start = jnp.where(positions >= end, end, start)
    return start


def conv_pack_kernel(cq_ref, ck_ref, cv_ref, cg_ref, out_ref):
    rows = cq_ref.shape[0]
    mixed = ck_ref[...].astype(F32) * cv_ref[...].astype(F32)
    grad = cg_ref[...].astype(F32) * cq_ref[...].astype(F32)
    out_ref[0, 0:rows, :] = mixed.astype(BF16)
    out_ref[0, rows:, :] = grad.astype(BF16)


def conv_pack(cq, ck, cv, cg, inner, ch_count):
    rows, channels = cq.shape
    members = inner * ch_count
    width = channels // members
    spec = pl.BlockSpec((rows, width), lambda k: (0, k))
    return pl.pallas_call(
        conv_pack_kernel,
        grid=(members,),
        in_specs=[spec] * 4,
        out_specs=pl.BlockSpec(
            (1, 2 * rows, width), lambda k: (lax.rem(k, inner) * ch_count + k // inner, 0, 0)
        ),
        out_shape=jax.ShapeDtypeStruct((members, 2 * rows, width), BF16),
        compiler_params=params(),
        cost_estimate=cost(4 * rows * channels, 12 * rows * channels),
        name="conv_pack",
    )(cq, ck, cv, cg)


def attn_pack_kernel(rows, q_ref, k_ref, v_ref, o_ref, g_ref, out_ref, prod_ref):
    heads = q_ref.shape[1] // HEAD_DIM
    span = LANES // rows
    offset = lax.rem(lax.axis_index("ch"), span) * rows
    prod_ref[...] = jnp.zeros_like(prod_ref)
    ones = jnp.ones((8, HEAD_DIM), F32)
    row = lax.broadcasted_iota(jnp.int32, (8, LANES), 0)
    for h in range(heads):
        cols = slice(h * HEAD_DIM, (h + 1) * HEAD_DIM)
        out_ref[h, 0:rows, :] = q_ref[:, cols]
        out_ref[h, rows : 2 * rows, :] = k_ref[:, cols]
        out_ref[h, 2 * rows : 3 * rows, :] = v_ref[:, cols]
        out_ref[h, 3 * rows : 4 * rows, :] = g_ref[:, cols]
        prod_ref[pl.ds(pl.multiple_of(offset, rows), rows), :] = g_ref[:, cols].astype(
            F32
        ) * o_ref[:, cols].astype(F32)
        delta = lax.dot_general(
            ones, prod_ref[...], NT, precision=lax.Precision.HIGHEST, preferred_element_type=F32
        )
        high = delta.astype(BF16).astype(F32)
        low = delta - high
        tile = jnp.where(row == 0, high, jnp.where(row == 1, low, 0.0))
        tile = jnp.concatenate([tile, jnp.zeros_like(tile)], axis=0)
        out_ref[h, 4 * rows : 4 * rows + 16, :] = tile.astype(BF16)


def attn_pack(q, k, v, o, g):
    rows, features = q.shape
    heads = features // HEAD_DIM
    step = math.gcd(heads, 8)
    spec = pl.BlockSpec((rows, step * HEAD_DIM), lambda j: (0, j))
    height = 4 * rows + 16
    return pl.pallas_call(
        functools.partial(attn_pack_kernel, rows),
        grid=(heads // step,),
        in_specs=[spec] * 5,
        out_specs=pl.BlockSpec((step, height, HEAD_DIM), lambda j: (j, 0, 0)),
        out_shape=jax.ShapeDtypeStruct((heads, height, HEAD_DIM), BF16),
        scratch_shapes=[pltpu.VMEM((LANES, HEAD_DIM), F32)],
        compiler_params=params(),
        cost_estimate=cost(4 * rows * features, 20 * rows * features),
        name="attn_pack",
    )(q, k, v, o, g)


def split_terms(x):
    high = x.astype(BF16)
    low = (x - high.astype(F32)).astype(BF16)
    return high, low


def attn_kernel(rows, reach, lens_ref, x_ref, out_ref, dk_ref, dv_ref):
    sources = x_ref.shape[0]
    per = LANES // rows
    blocks = sources // per
    scale = 1.0 / math.sqrt(HEAD_DIM)

    def part(first, count, which):
        return x_ref[first * per : (first + count) * per, which * rows : (which + 1) * rows, :].reshape(
            count * LANES, HEAD_DIM
        )

    dk_ref[...] = jnp.zeros_like(dk_ref)
    dv_ref[...] = jnp.zeros_like(dv_ref)
    for i in range(blocks):
        low = max(0, (i * LANES - (reach - 1)) // LANES)
        count = i + 1 - low
        query, grad = part(i, 1, 0), part(i, 1, 3)
        keys, values = part(low, count, 1), part(low, count, 2)
        delta = x_ref[i * per : (i + 1) * per, 4 * rows : 4 * rows + 16, :].astype(F32)
        delta = jnp.sum(jnp.sum(delta, axis=0), axis=0, keepdims=True)
        q_pos = i * LANES + lax.broadcasted_iota(jnp.int32, (8, LANES), 1)
        start = doc_start(lens_ref, q_pos)[0:1]
        k_pos = low * LANES + lax.broadcasted_iota(jnp.int32, (count * LANES, LANES), 0)
        visible = (k_pos >= start) & (k_pos <= q_pos[0:1])
        scores = jnp.where(visible, dot(keys, query, NT) * scale, NEG_FILL)
        top = jnp.max(scores, axis=0, keepdims=True)
        weights = jnp.where(visible, jnp.exp(scores - top), 0.0)
        probs = weights * (1.0 / jnp.sum(weights, axis=0, keepdims=True))
        grad_probs = dot(values, grad, NT)
        grad_scores = probs * (grad_probs - delta)
        span = slice(low * LANES, (i + 1) * LANES)
        p_terms = jnp.concatenate(split_terms(probs), axis=1)
        dv_ref[span, :] += dot(p_terms, jnp.concatenate([grad, grad], axis=0), NN)
        s_high, s_low = split_terms(grad_scores)
        s_terms = jnp.concatenate([s_high, s_low], axis=1)
        dk_ref[span, :] += dot(s_terms, jnp.concatenate([query, query], axis=0), NN)
        dq = dot(s_high, keys, TN) + dot(s_low, keys, TN)
        out_ref[i * per : (i + 1) * per, 0:rows, :] = (
            (dq * scale).astype(BF16).reshape(per, rows, HEAD_DIM)
        )
    for i in range(blocks):
        span = slice(i * LANES, (i + 1) * LANES)
        here = slice(i * per, (i + 1) * per)
        out_ref[here, rows : 2 * rows, :] = (
            (dk_ref[span, :] * scale).astype(BF16).reshape(per, rows, HEAD_DIM)
        )
        out_ref[here, 2 * rows : 3 * rows, :] = (
            dv_ref[span, :].astype(BF16).reshape(per, rows, HEAD_DIM)
        )


def attn_head(lens, x, rows, reach):
    sources = x.shape[0]
    tokens = sources * rows
    return pl.pallas_call(
        functools.partial(attn_kernel, rows, reach),
        in_specs=[
            pl.BlockSpec(memory_space=pltpu.SMEM),
            pl.BlockSpec(memory_space=pltpu.VMEM),
        ],
        out_specs=pl.BlockSpec(memory_space=pltpu.VMEM),
        out_shape=jax.ShapeDtypeStruct((sources, 3 * rows, HEAD_DIM), BF16),
        scratch_shapes=[
            pltpu.VMEM((tokens, HEAD_DIM), F32),
            pltpu.VMEM((tokens, HEAD_DIM), F32),
        ],
        compiler_params=params(),
        cost_estimate=cost(20 * tokens * 512 * HEAD_DIM, 4 * x.size),
        name="attn_head",
    )(lens, x)


def attn_unpack_kernel(rows, x_ref, dq_ref, dk_ref, dv_ref):
    for h in range(x_ref.shape[0]):
        cols = slice(h * HEAD_DIM, (h + 1) * HEAD_DIM)
        dq_ref[:, cols] = x_ref[h, 0:rows, :]
        dk_ref[:, cols] = x_ref[h, rows : 2 * rows, :]
        dv_ref[:, cols] = x_ref[h, 2 * rows : 3 * rows, :]


def attn_unpack(x, rows):
    heads = x.shape[0]
    step = math.gcd(heads, 8)
    spec = pl.BlockSpec((rows, step * HEAD_DIM), lambda j: (0, j))
    shape = jax.ShapeDtypeStruct((rows, heads * HEAD_DIM), BF16)
    return pl.pallas_call(
        functools.partial(attn_unpack_kernel, rows),
        grid=(heads // step,),
        in_specs=[pl.BlockSpec((step, 3 * rows, HEAD_DIM), lambda j: (j, 0, 0))],
        out_specs=[spec] * 3,
        out_shape=[shape] * 3,
        compiler_params=params(),
        cost_estimate=cost(0, 4 * x.size),
        name="attn_unpack",
    )(x)


def conv_kernel(
    rows, inner, ch_count, lens_ref, x_ref, prior_ref, later_ref, tap_ref, rev_ref, out_ref, filt_ref,
    back_ref, front_ref,
):
    sources = x_ref.shape[0]
    per = LANES // rows
    blocks = sources // per
    tile = pl.program_id(0)

    @pl.when(tile == 0)
    def _():
        base = (lax.axis_index("seq") // inner) * (sources * rows)
        shape = (LANES, 2 * LANES)
        down = lax.broadcasted_iota(jnp.int32, shape, 0)
        across = lax.broadcasted_iota(jnp.int32, shape, 1)
        for b in range(blocks):
            out_pos = base + b * LANES + down
            in_pos = base + (b - 1) * LANES + across
            gap = out_pos - in_pos
            near = (gap >= 0) & (gap < FILTER_LEN) & (in_pos >= doc_start(lens_ref, out_pos))
            back_ref[b] = near.astype(F32).astype(BF16)
            in_pos = base + b * LANES + down
            out_pos = base + b * LANES + across
            gap = out_pos - in_pos
            near = (gap >= 0) & (gap < FILTER_LEN) & (in_pos >= doc_start(lens_ref, out_pos))
            front_ref[b] = near.astype(F32).astype(BF16)

    mixed = jnp.concatenate(
        [prior_ref[...].reshape(LANES, LANES), x_ref[:, 0:rows, :].reshape(sources * rows, LANES)],
        axis=0,
    )
    grad = jnp.concatenate(
        [x_ref[:, rows : 2 * rows, :].reshape(sources * rows, LANES), later_ref[...].reshape(LANES, LANES)],
        axis=0,
    )
    lane_group = lax.broadcasted_iota(jnp.int32, (LANES, LANES), 1) // GROUP
    sub = lax.broadcasted_iota(jnp.int32, (8, LANES), 0)
    conv_out = [jnp.zeros((LANES, LANES), F32) for _ in range(blocks)]
    mixed_grad = [jnp.zeros((LANES, LANES), F32) for _ in range(blocks)]
    groups = LANES // GROUP

    def circulant(row):
        rolled = pltpu.roll(jnp.broadcast_to(row, (8, LANES)), 0, 1, stride=1, stride_axis=0)
        pieces = [rolled if a == 0 else pltpu.roll(rolled, 8 * a, 1) for a in range(LANES // 8)]
        full = jnp.concatenate(pieces, axis=0).astype(BF16)
        return jnp.concatenate([full, full], axis=1)

    for g in range(groups):
        mine = lane_group == g
        back_taps = circulant(rev_ref[g : g + 1, :])
        front_taps = circulant(tap_ref[g : g + 1, :])
        outer = jnp.zeros((LANES, LANES), F32)
        for b in range(blocks):
            window = mixed[b * LANES : (b + 2) * LANES]
            ahead = grad[b * LANES : (b + 2) * LANES]
            here = jnp.where(mine, ahead[0:LANES].astype(F32), 0.0).astype(BF16)
            conv_out[b] = jnp.where(mine, dot(back_taps * back_ref[b], window, NN), conv_out[b])
            mixed_grad[b] = jnp.where(mine, dot(front_taps * front_ref[b], ahead, NN), mixed_grad[b])
            full = dot(here, window, NT) * back_ref[b].astype(F32)
            outer = outer + full[:, 0:LANES] + full[:, LANES:]
        folded = outer[0:8]
        for a in range(1, LANES // 8):
            folded = folded + pltpu.roll(outer[8 * a : 8 * a + 8], LANES - 8 * a, 1)
        for bit in (1, 2, 4):
            folded = jnp.where((sub & bit) != 0, pltpu.roll(folded, LANES - bit, 1), folded)
        filt_ref[g : g + 1, :] = jnp.sum(folded, axis=0, keepdims=True)
    for b in range(blocks):
        here = slice(b * per, (b + 1) * per)
        out_ref[here, 0:rows, :] = conv_out[b].astype(BF16).reshape(per, rows, LANES)
        out_ref[here, rows : 2 * rows, :] = mixed_grad[b].astype(BF16).reshape(per, rows, LANES)


def conv_core(lens, x, prior, later, taps, rev_taps, rows, inner, ch_count):
    sources, _, width = x.shape
    per = LANES // rows
    blocks = sources // per
    tiles = width // LANES
    groups = LANES // GROUP
    spec = pl.BlockSpec((sources, 2 * rows, LANES), lambda j: (0, 0, j))
    halo = pl.BlockSpec((per, rows, LANES), lambda j: (0, 0, j))
    tap_spec = pl.BlockSpec((groups, FILTER_LEN), lambda j: (j, 0))
    return pl.pallas_call(
        functools.partial(conv_kernel, rows, inner, ch_count),
        grid=(tiles,),
        in_specs=[pl.BlockSpec(memory_space=pltpu.SMEM), spec, halo, halo, tap_spec, tap_spec],
        out_specs=[spec, tap_spec],
        out_shape=[
            jax.ShapeDtypeStruct(x.shape, BF16),
            jax.ShapeDtypeStruct((width // GROUP, FILTER_LEN), F32),
        ],
        scratch_shapes=[
            pltpu.VMEM((blocks, LANES, 2 * LANES), BF16),
            pltpu.VMEM((blocks, LANES, 2 * LANES), BF16),
        ],
        compiler_params=params(),
        cost_estimate=cost(12 * sources * rows * 2 * LANES * LANES * tiles, 8 * x.size),
        name="conv_core",
    )(lens, x, prior, later, taps, rev_taps)


def conv_unpack_kernel(x_ref, ck_ref, cv_ref, cg_ref, gq_ref, gk_ref, gv_ref):
    rows = ck_ref.shape[0]
    conv_out = x_ref[0, 0:rows, :].astype(F32)
    mixed_grad = x_ref[0, rows : 2 * rows, :].astype(F32)
    gq_ref[...] = (cg_ref[...].astype(F32) * conv_out).astype(BF16)
    gk_ref[...] = (mixed_grad * cv_ref[...].astype(F32)).astype(BF16)
    gv_ref[...] = (mixed_grad * ck_ref[...].astype(F32)).astype(BF16)


def conv_unpack(x, ck, cv, cg, inner, ch_count):
    rows, channels = ck.shape
    members, _, width = x.shape
    spec = pl.BlockSpec((rows, width), lambda k: (0, k))
    shape = jax.ShapeDtypeStruct((rows, channels), BF16)
    return pl.pallas_call(
        conv_unpack_kernel,
        grid=(members,),
        in_specs=[
            pl.BlockSpec(
                (1, 2 * rows, width), lambda k: (lax.rem(k, inner) * ch_count + k // inner, 0, 0)
            ),
            spec,
            spec,
            spec,
        ],
        out_specs=[spec] * 3,
        out_shape=[shape] * 3,
        compiler_params=params(),
        cost_estimate=cost(6 * rows * channels, 16 * rows * channels),
        name="conv_unpack",
    )(x, ck, cv, cg)


def doc_index(doc_lengths, positions):
    doc_ends = jnp.cumsum(doc_lengths)
    return jnp.sum((doc_ends[None, :] <= positions[:, None]).astype(jnp.int32), axis=1)


def split_rows(advance, carried, pieces):
    def one_block(block_index, current):
        sub_parts = tuple(
            lax.dynamic_slice_in_dim(part, block_index * 512, 512, 0) for part in pieces
        )
        return advance(current, sub_parts, block_index * 512)

    return lax.fori_loop(0, pieces[0].shape[0] // 512, one_block, carried)


def attn_gathered(attn_query, attn_key, attn_value, attn_output, attn_grad_out, doc_lengths):
    query_rows, key_rows, value_rows, output_rows, grad_rows = (
        lax.all_to_all(a, "ch", split_axis=1, concat_axis=0, tiled=True)
        for a in (attn_query, attn_key, attn_value, attn_output, attn_grad_out)
    )
    tok_rows = query_rows.shape[0]
    head_count = query_rows.shape[1] // HEAD_DIM
    scale_factor = 1.0 / math.sqrt(HEAD_DIM)
    local_pos = lax.axis_index("seq") * tok_rows + jnp.arange(tok_rows, dtype=jnp.int32)
    local_doc = doc_index(doc_lengths, local_pos)
    query_heads, key_heads, value_heads, output_heads, grad_heads = (
        a.reshape(tok_rows, head_count, HEAD_DIM)
        for a in (query_rows, key_rows, value_rows, output_rows, grad_rows)
    )
    delta_rows = jnp.sum(grad_heads.astype(F32) * output_heads.astype(F32), axis=2)
    delta_heads = delta_rows.T

    def key_step(carried, pieces, key_start):
        key_part, value_part = pieces
        key_pos = key_start + jnp.arange(key_part.shape[0], dtype=jnp.int32)
        key_doc = doc_index(doc_lengths, key_pos)
        visible = (key_doc[None, :] == local_doc[:, None]) & (key_pos[None, :] <= local_pos[:, None])
        running_max, running_sum, running_grad = carried
        scores = (
            jnp.einsum("thd,rhd->htr", query_heads, key_part, preferred_element_type=F32)
            * scale_factor
        )
        new_max = jnp.maximum(
            running_max, jnp.max(jnp.where(visible[None], scores, NEG_FILL), axis=2)
        )
        weights = jnp.where(visible[None], jnp.exp(scores - new_max[:, :, None]), 0.0)
        rescale = jnp.exp(running_max - new_max)
        grad_probs = jnp.einsum(
            "thd,rhd->htr", grad_heads, value_part, preferred_element_type=F32
        )
        weighted = weights * (grad_probs - delta_heads[:, :, None])
        update = jnp.einsum(
            "htr,rhd->htd", weighted, key_part.astype(F32), precision=lax.Precision.HIGHEST
        )
        return (
            new_max,
            running_sum * rescale + jnp.sum(weights, axis=2),
            running_grad * rescale[:, :, None] + update,
        )

    start_state = (
        jnp.full((head_count, tok_rows), NEG_FILL, F32),
        jnp.zeros((head_count, tok_rows), F32),
        jnp.zeros((head_count, tok_rows, HEAD_DIM), F32),
    )
    final_max, final_sum, final_grad = split_rows(
        key_step,
        start_state,
        (
            lax.all_gather(key_heads, "seq", axis=0, tiled=True),
            lax.all_gather(value_heads, "seq", axis=0, tiled=True),
        ),
    )
    lse_rows = (final_max + jnp.log(final_sum)).T
    grad_query = (final_grad * (scale_factor / final_sum)[:, :, None]).transpose(1, 0, 2)
    lse_whole = lax.all_gather(lse_rows, "seq", axis=0, tiled=True)
    delta_whole = lax.all_gather(delta_rows, "seq", axis=0, tiled=True)

    def query_step(carried, pieces, query_start):
        query_part, grad_part = pieces
        part_rows = query_part.shape[0]
        lse_part = lax.dynamic_slice_in_dim(lse_whole, query_start, part_rows, 0)
        delta_part = lax.dynamic_slice_in_dim(delta_whole, query_start, part_rows, 0)
        query_pos = query_start + jnp.arange(part_rows, dtype=jnp.int32)
        query_doc = doc_index(doc_lengths, query_pos)
        visible = (query_doc[:, None] == local_doc[None, :]) & (
            local_pos[None, :] <= query_pos[:, None]
        )
        key_grad, value_grad = carried
        scores = (
            jnp.einsum("rhd,thd->hrt", query_part, key_heads, preferred_element_type=F32)
            * scale_factor
        )
        probs = jnp.where(visible[None], jnp.exp(scores - lse_part.T[:, :, None]), 0.0)
        value_grad = value_grad + jnp.einsum(
            "hrt,rhd->thd", probs, grad_part.astype(F32), precision=lax.Precision.HIGHEST
        )
        grad_probs = jnp.einsum(
            "rhd,thd->hrt", grad_part, value_heads, preferred_element_type=F32
        )
        grad_scores = probs * (grad_probs - delta_part.T[:, :, None])
        key_grad = key_grad + scale_factor * jnp.einsum(
            "hrt,rhd->thd", grad_scores, query_part.astype(F32), precision=lax.Precision.HIGHEST
        )
        return (key_grad, value_grad)

    zero = jnp.zeros((tok_rows, head_count, HEAD_DIM), F32)
    key_grad, value_grad = split_rows(
        query_step,
        (zero, zero),
        (
            lax.all_gather(query_heads, "seq", axis=0, tiled=True),
            lax.all_gather(grad_heads, "seq", axis=0, tiled=True),
        ),
    )
    return tuple(
        lax.all_to_all(
            a.reshape(tok_rows, head_count * HEAD_DIM).astype(BF16),
            "ch",
            split_axis=0,
            concat_axis=1,
            tiled=True,
        )
        for a in (grad_query, key_grad, value_grad)
    )


def shifted(block, distance, count):
    route = [(i, i + distance) for i in range(count) if 0 <= i + distance < count]
    return lax.ppermute(block, DEVICES, route)


def exchanged(block, distance, count):
    return lax.ppermute(block, DEVICES, [(i, i ^ distance) for i in range(count)])


def body(
    attn_query, attn_key, attn_value, attn_output, attn_grad_out,
    conv_query, conv_key, conv_value, conv_grad_out, conv_filter, doc_lengths,
):
    seq_count, ch_count = lax.axis_size("seq"), lax.axis_size("ch")
    count = seq_count * ch_count
    rows, channels = conv_query.shape
    inner = 2
    members = inner * ch_count
    outer = seq_count // inner
    near = [[base + i for i in range(members)] for base in range(0, count, members)]
    heads = attn_query.shape[1] // HEAD_DIM
    head_each = heads == count

    packed = conv_pack(conv_query, conv_key, conv_value, conv_grad_out, inner, ch_count)
    conv_in = lax.all_to_all(
        packed, DEVICES, split_axis=0, concat_axis=0, tiled=True, axis_index_groups=near
    )
    if head_each:
        attn_packed = attn_pack(attn_query, attn_key, attn_value, attn_output, attn_grad_out)
        attn_packed, conv_in = lax.optimization_barrier((attn_packed, conv_in))
        attn_in = lax.all_to_all(attn_packed, DEVICES, split_axis=0, concat_axis=0, tiled=True)

    per = FILTER_LEN // rows
    prior = shifted(conv_in[members - per :, 0:rows, :], members, count)
    later = shifted(conv_in[:per, rows:, :], -members, count)
    group_count = channels // members // GROUP
    y = lax.rem(lax.axis_index("seq"), inner)
    taps = lax.dynamic_slice_in_dim(conv_filter, y * group_count, group_count, 0).astype(F32)
    rev_taps = jnp.roll(taps[:, ::-1], 1, axis=1)
    conv_back, filter_part = conv_core(
        doc_lengths, conv_in, prior, later, taps, rev_taps, rows, inner, ch_count
    )
    if head_each:
        attn_in, conv_back = lax.optimization_barrier((attn_in, conv_back))
    conv_res = lax.all_to_all(
        conv_back, DEVICES, split_axis=0, concat_axis=0, tiled=True, axis_index_groups=near
    )

    distance = members
    while distance < count:
        filter_part = filter_part + exchanged(filter_part, distance, count)
        distance *= 2
    filter_part = jnp.roll(filter_part[:, ::-1], 1, axis=1)
    other = exchanged(filter_part, ch_count, count)
    grad_filter = jnp.where(
        y == 0,
        jnp.concatenate([filter_part, other], axis=0),
        jnp.concatenate([other, filter_part], axis=0),
    )

    if head_each:
        reach = BAND_REACH if rows * count == 1024 else rows * count
        attn_back = attn_head(doc_lengths, attn_in, rows, reach)
        attn_back, conv_res = lax.optimization_barrier((attn_back, conv_res))
        attn_res = lax.all_to_all(attn_back, DEVICES, split_axis=0, concat_axis=0, tiled=True)
    grad_conv = conv_unpack(conv_res, conv_key, conv_value, conv_grad_out, inner, ch_count)
    if head_each:
        grad_attn = attn_unpack(attn_res, rows)
    else:
        grad_attn = attn_gathered(
            attn_query, attn_key, attn_value, attn_output, attn_grad_out, doc_lengths
        )
    return (*grad_attn, *grad_conv, grad_filter)


def solution(mesh):
    rows = P(("seq", "ch"), None)
    return jax.shard_map(
        body,
        mesh=mesh,
        in_specs=(rows,) * 9 + (P("ch", None), P()),
        out_specs=(rows,) * 6 + (P("ch", None),),
        check_vma=False,
    )
```

time: 541 us -> 133 us (0.25)
  local copies, waits for them, and re-layouts: 228 us -> 6.04 us
  blocking collectives: 90.9 us -> 0 us
  matrix products: 45.9 us -> 0 us
  waiting for transfers between devices: 92.4 us -> 57 us
  Pallas kernels: 0 us -> 29.5 us
  between operations: 14.3 us -> 0.8 us
  starting transfers between devices: 50.3 us -> 37.1 us
  other arithmetic: 14.4 us -> 1.66 us
    reshape x22 -> x0, local copies, waits for them, and re-layouts: 92.6 us -> none  [the longest x8 33.9 us: band_sums(): skewed = flattened.reshape(group_count, row_count, span_count + 2)]
    all_gather x2 -> x0, blocking collectives: 63.8 us -> none  [the longest x1 33.4 us: body(): lax.all_gather(delta_rows, 'seq', axis=0, tiled=True)]
    psum x1 -> x0, waiting for transfers between devices: 61.3 us -> none  [body(): grad_filter = lax.psum(tap_grad, 'seq')]
    dot_general x24 -> x0, matrix products: 45.9 us -> none  [the longest x8 11.4 us: tap_block(): jnp.einsum('tgc,sgc->gts', out_part, ext_part, preferred_element_type=jnp...]
    ppermute x2 -> x5, waiting for transfers between devices: 0.01 us -> 36.4 us  [the longest x2 19.2 us: shifted(): return lax.ppermute(block, DEVICES, route)]
    another operation x5 -> x0, local copies, waits for them, and re-layouts: 34.8 us -> none  [the longest x4 34.8 us: banded(): repeated = jnp.tile(padded, (1, row_count))[:, :row_count * span_count]]
    pallas_call x0 -> x6, Pallas kernels: none -> 29.5 us  [the longest x1 12.8 us: conv_core(): pl.pallas_call(functools.partial(conv_kernel, rows, inner, ch_count), gri...]
    pad x18 -> x0, local copies, waits for them, and re-layouts: 27.4 us -> none  [the longest x8 24.6 us: band_sums(): jnp.pad(padded.reshape(group_count, row_count * (span_count + 1)), ((0, 0...]
  transfers between devices with their start and end apart: 19 -> 9, of which waited for: 7 -> 7; matrix products, arithmetic and copies ran while one was open for 52% -> 2% of each run, Pallas kernels for 0% -> 19%
where the time goes in v1:
time: 133 us; the launch traced here: 132 us
  waiting for transfers between devices  57 us (43%)
  starting transfers between devices  37.1 us (28%)
  Pallas kernels  29.5 us (22%)
  local copies, waits for them, and re-layouts  6.04 us (5%)
  other arithmetic  1.66 us (1%)
    ppermute x2, waiting for transfers between devices, shifted(): return lax.ppermute(block, DEVICES, route)  19.2 us
    ppermute x3, waiting for transfers between devices, exchanged(): lax.ppermute(block, DEVICES, [(i, i ^ distance) for i in range(count)])  17.2 us
    pallas_call x1, Pallas kernels, conv_core(): pl.pallas_call(functools.partial(conv_kernel, rows, inner, ch_count), gri...  12.8 us
    all_to_all x1, waiting for transfers between devices, body(): lax.all_to_all(packed, DEVICES, split_axis=0, concat_axis=0, tiled=True,...  10.6 us
    all_to_all x1, waiting for transfers between devices, body(): lax.all_to_all(conv_back, DEVICES, split_axis=0, concat_axis=0, tiled=Tru...  9.93 us
    all_to_all x1, starting transfers between devices, body(): lax.all_to_all(attn_back, DEVICES, split_axis=0, concat_axis=0, tiled=True)  9.86 us
    ppermute x3, starting transfers between devices, exchanged(): lax.ppermute(block, DEVICES, [(i, i ^ distance) for i in range(count)])  7.96 us
    ppermute x2, starting transfers between devices, shifted(): return lax.ppermute(block, DEVICES, route)  5.85 us
  transfers between devices with their start and end apart: 9, of which 7 were waited for; matrix products, arithmetic and copies ran while one was open for 2% of the time, Pallas kernels for 19%

profile of v1, /device:TPU:0, one launch (start us, length us, event | category | flops | bytes accessed | tf_op | source)
XLA Modules:
  0.0 132.1 jit_solution(1922360565436498069)
XLA Ops:
  1.7 1.0 copy-done.2
  2.7 1.0 copy-done.4
  3.8 1.0 copy-done.7
  4.8 2.9 %conv_pack.1 = bf16[8,64,1024]{2,1,0:T(8,128)(2,1)} custom-call(bf16[32,8192]{1,0:T(8,128)(2,1)S(1)} %copy-done.7, bf16[32,8192]{1,0:T(8,128)(2,1)S(1)} %copy-done, bf16[32,8192]{1,0:T(8,128)(2,1)S(1)} %copy-done.2, bf16[32,8192]{1,0:T(8,128)(2,1)S(1)} %copy-done.4), custom_call_target="tpu_custom_call" | custom-call | flops 1048576 | bytes 3145728 | tf_op jit(solution)/shard_map/conv_pack/pallas_call | solution.py:60
  7.8 5.3 %all-to-all-start = ((bf16[8,64,1024]{2,1,0:T(8,128)(2,1)}), bf16[8,64,1024]{2,1,0:T(8,128)(2,1)S(1)}, u32[]{:S(2)}, u32[]{:S(2)}) async-start(bf16[8,64,1024]{2,1,0:T(8,128)(2,1)} %conv_pack.1), calls=%async_computation | async-start | bytes 2097152 | tf_op jit(solution)/shard_map/all_to_all | solution.py:506
  13.1 4.7 %attn_pack.1 = bf16[32,144,128]{2,1,0:T(8,128)(2,1)} custom-call(bf16[32,4096]{1,0:T(8,128)(2,1)S(1)} %copy-done.8, bf16[32,4096]{1,0:T(8,128)(2,1)S(1)} %copy-done.9, bf16[32,4096]{1,0:T(8,128)(2,1)S(1)} %copy-done.10, bf16[32,4096]{1,0:T(8,128)(2,1)S(1)} %copy-done.11, bf16[32,4096]{1,0:T(8,128)(2,1)S(1)} %copy-done.12), custom_call_target="tpu_custom_call" | custom-call | flops 524288 | bytes 2621440 | tf_op jit(solution)/shard_map/attn_pack/pallas_call | solution.py:106
  17.9 10.6 %all-to-all-done.x_ref = bf16[8,64,1024]{2,1,0:T(8,128)(2,1)S(1)} async-done(((bf16[8,64,1024]{2,1,0:T(8,128)(2,1)}), bf16[8,64,1024]{2,1,0:T(8,128)(2,1)S(1)}, u32[]{:S(2)}, u32[]{:S(2)}) %all-to-all-start) | async-done | bytes 1048608 | tf_op jit(solution)/shard_map/all_to_all | solution.py:506
  28.5 4.0 %all-to-all-start.1 = ((bf16[32,144,128]{2,1,0:T(8,128)(2,1)}), bf16[32,144,128]{2,1,0:T(8,128)(2,1)S(1)}, u32[]{:S(2)}, u32[]{:S(2)}) async-start(bf16[32,144,128]{2,1,0:T(8,128)(2,1)} %attn_pack.1), calls=%async_computation.1 | async-start | bytes 2359296 | tf_op jit(solution)/shard_map/all_to_all | solution.py:512
  32.6 1.3 collective-permute-start.1
  33.9 4.6 %collective-permute-start = (bf16[4,32,1024]{2,1,0:T(8,128)(2,1)S(1)}, bf16[4,32,1024]{2,1,0:T(8,128)(2,1)S(1)}, u32[]{:S(2)}, u32[]{:S(2)}) collective-permute-start(bf16[4,32,1024]{2,1,0:T(8,128)(2,1)S(1)} %get-tuple-element.36), channel_id=1, source_target_pairs={{0,8},{1,9},{2,10},{3,11},{4,12},{5,13},{6,14},{7,15},{8,16},{9,17... | collective-permute-start | bytes 786440 | tf_op jit(solution)/shard_map/ppermute | solution.py:484
  38.7 18.5 %collective-permute-done.1.later_ref = bf16[4,32,1024]{2,1,0:T(8,128)(2,1)S(1)} collective-permute-done((bf16[4,32,1024]{2,1,0:T(8,128)(2,1)S(1)}, bf16[4,32,1024]{2,1,0:T(8,128)(2,1)S(1)}, u32[]{:S(2)}, u32[]{:S(2)}) %collective-permute-start.1) | collective-permute-done | bytes 262176 | tf_op jit(solution)/shard_map/ppermute | solution.py:484
  57.9 12.8 %conv_core.1 = (bf16[8,64,1024]{2,1,0:T(8,128)(2,1)}, f32[64,128]{1,0:T(8,128)S(1)}) custom-call(s32[12]{0:T(128)S(1)} %copy-done.14, bf16[8,64,1024]{2,1,0:T(8,128)(2,1)S(1)} %all-to-all-done.x_ref, bf16[4,32,1024]{2,1,0:T(8,128)(2,1)S(1)} %collective-permute-done.prior_ref, bf16[4,32,1024]{2,1,0:T(8,128)(2,1)S(1)} %collective-permute-done.1.later_ref, ...), custom_call_target="tpu_custom_call" | custom-call | flops 805306368 | bytes 4194304 | tf_op jit(solution)/shard_map/conv_core/pallas_call | solution.py:303
  71.3 4.2 %all-to-all-start.2 = ((bf16[8,64,1024]{2,1,0:T(8,128)(2,1)}), bf16[8,64,1024]{2,1,0:T(8,128)(2,1)S(1)}, u32[]{:S(2)}, u32[]{:S(2)}) async-start(bf16[8,64,1024]{2,1,0:T(8,128)(2,1)} %get-tuple-element.25), calls=%async_computation.2 | async-start | bytes 2097152 | tf_op jit(solution)/shard_map/all_to_all | solution.py:526
  75.5 4.6 %attn_head.1 = bf16[32,96,128]{2,1,0:T(8,128)(2,1)S(1)} custom-call(s32[12]{0:T(128)S(1)} %copy-done.14, bf16[32,144,128]{2,1,0:T(8,128)(2,1)S(1)} %all-to-all-done.1.x_ref), custom_call_target="tpu_custom_call" | custom-call | flops 1342177280 | bytes 2359296 | tf_op jit(solution)/shard_map/attn_head/pallas_call | solution.py:179
  80.9 9.9 %all-to-all-done.2.x_ref = bf16[8,64,1024]{2,1,0:T(8,128)(2,1)S(1)} async-done(((bf16[8,64,1024]{2,1,0:T(8,128)(2,1)}), bf16[8,64,1024]{2,1,0:T(8,128)(2,1)S(1)}, u32[]{:S(2)}, u32[]{:S(2)}) %all-to-all-start.2) | async-done | bytes 1048608 | tf_op jit(solution)/shard_map/all_to_all | solution.py:526
  90.9 9.9 %all-to-all-start.3 = ((bf16[32,96,128]{2,1,0:T(8,128)(2,1)}), bf16[32,96,128]{2,1,0:T(8,128)(2,1)S(1)}, u32[]{:S(2)}, u32[]{:S(2)}) async-start(bf16[32,96,128]{2,1,0:T(8,128)(2,1)} %copy-done.6), calls=%async_computation.3 | async-start | bytes 1572864 | tf_op jit(solution)/shard_map/all_to_all | solution.py:546
  100.7 2.0 %collective-permute-start.2 = (f32[64,128]{1,0:T(8,128)}, f32[64,128]{1,0:T(8,128)S(1)}, u32[]{:S(2)}, u32[]{:S(2)}) collective-permute-start(f32[64,128]{1,0:T(8,128)} %copy-done.13), channel_id=1, source_target_pairs={{0,8},{1,9},{2,10},{3,11},{4,12},{5,13},{6,14},{7,15},{8,0},{9,1},... | collective-permute-start | bytes 98312 | tf_op jit(solution)/shard_map/ppermute | solution.py:488
  102.7 12.2 %collective-permute-done.2 = f32[64,128]{1,0:T(8,128)S(1)} collective-permute-done((f32[64,128]{1,0:T(8,128)}, f32[64,128]{1,0:T(8,128)S(1)}, u32[]{:S(2)}, u32[]{:S(2)}) %collective-permute-start.2) | collective-permute-done | bytes 32800 | tf_op jit(solution)/shard_map/ppermute | solution.py:488
  115.7 4.4 %collective-permute-start.3 = (f32[64,128]{1,0:T(8,128)S(1)}, f32[64,128]{1,0:T(8,128)S(1)}, u32[]{:S(2)}, u32[]{:S(2)}) collective-permute-start(f32[64,128]{1,0:T(8,128)S(1)} %add.10), channel_id=1, source_target_pairs={{0,16},{1,17},{2,18},{3,19},{4,20},{5,21},{6,22},{7,23},{8,24},{9,... | collective-permute-start | bytes 98312 | tf_op jit(solution)/shard_map/ppermute | solution.py:488
  120.1 2.6 %collective-permute-done.3 = f32[64,128]{1,0:T(8,128)S(1)} collective-permute-done((f32[64,128]{1,0:T(8,128)S(1)}, f32[64,128]{1,0:T(8,128)S(1)}, u32[]{:S(2)}, u32[]{:S(2)}) %collective-permute-start.3) | collective-permute-done | bytes 32800 | tf_op jit(solution)/shard_map/ppermute | solution.py:488
  123.0 1.5 %collective-permute-start.4 = (f32[64,128]{1,0:T(8,128)S(1)}, f32[64,128]{1,0:T(8,128)S(1)}, u32[]{:S(2)}, u32[]{:S(2)}) collective-permute-start(f32[64,128]{1,0:T(8,128)S(1)} %pad_maximum_fusion.1), channel_id=1, source_target_pairs={{0,4},{1,5},{2,6},{3,7},{4,0},{5,1},{6,2},{7,3},{8,12},{9,13},{10,... | collective-permute-start | bytes 98312 | tf_op jit(solution)/shard_map/ppermute | solution.py:488
  124.5 2.4 %collective-permute-done.4 = f32[64,128]{1,0:T(8,128)S(1)} collective-permute-done((f32[64,128]{1,0:T(8,128)S(1)}, f32[64,128]{1,0:T(8,128)S(1)}, u32[]{:S(2)}, u32[]{:S(2)}) %collective-permute-start.4) | collective-permute-done | bytes 32800 | tf_op jit(solution)/shard_map/ppermute | solution.py:488
  127.7 3.0 %conv_unpack.1 = (bf16[32,8192]{1,0:T(8,128)(2,1)}, bf16[32,8192]{1,0:T(8,128)(2,1)}, bf16[32,8192]{1,0:T(8,128)(2,1)}) custom-call(bf16[8,64,1024]{2,1,0:T(8,128)(2,1)S(1)} %all-to-all-done.2.x_ref, bf16[32,8192]{1,0:T(8,128)(2,1)S(1)} %copy-done.1, bf16[32,8192]{1,0:T(8,128)(2,1)S(1)} %copy-done.3, bf16[32,8192]{1,0:T(8,128)(2,1)S(1)} %copy-done.5), custom_call_target="tpu_custom_call" | custom-call | flops 1572864 | bytes 4194304 | tf_op jit(solution)/shard_map/conv_unpack/pallas_call | solution.py:336
  130.6 1.5 %attn_unpack.1 = (bf16[32,4096]{1,0:T(8,128)(2,1)}, bf16[32,4096]{1,0:T(8,128)(2,1)}, bf16[32,4096]{1,0:T(8,128)(2,1)}) custom-call(bf16[32,96,128]{2,1,0:T(8,128)(2,1)S(1)} %all-to-all-done.3.x_ref), custom_call_target="tpu_custom_call" | custom-call | bytes 1572864 | tf_op jit(solution)/shard_map/attn_unpack/pallas_call | solution.py:210
  (43 shorter events, 5.3 us)
Async XLA Ops:
  0.6 1.0 copy-start
  1.7 1.0 copy-start.2
  2.7 1.0 copy-start.4
  3.8 1.0 copy-start.7
  7.8 5.3 %copy-start.8 = (bf16[32,4096]{1,0:T(8,128)(2,1)S(1)}, bf16[32,4096]{1,0:T(8,128)(2,1)}, u32[]{:S(2)}) copy-start(bf16[32,4096]{1,0:T(8,128)(2,1)} %q_ref.1) | copy-start | bytes 786436
  7.8 5.3 %copy-start.9 = (bf16[32,4096]{1,0:T(8,128)(2,1)S(1)}, bf16[32,4096]{1,0:T(8,128)(2,1)}, u32[]{:S(2)}) copy-start(bf16[32,4096]{1,0:T(8,128)(2,1)} %k_ref.1) | copy-start | bytes 786436
  7.8 5.4 %copy-start.10 = (bf16[32,4096]{1,0:T(8,128)(2,1)S(1)}, bf16[32,4096]{1,0:T(8,128)(2,1)}, u32[]{:S(2)}) copy-start(bf16[32,4096]{1,0:T(8,128)(2,1)} %v_ref.1) | copy-start | bytes 786436
  7.8 5.4 %copy-start.11 = (bf16[32,4096]{1,0:T(8,128)(2,1)S(1)}, bf16[32,4096]{1,0:T(8,128)(2,1)}, u32[]{:S(2)}) copy-start(bf16[32,4096]{1,0:T(8,128)(2,1)} %o_ref.1) | copy-start | bytes 786436
  7.8 5.4 %copy-start.12 = (bf16[32,4096]{1,0:T(8,128)(2,1)S(1)}, bf16[32,4096]{1,0:T(8,128)(2,1)}, u32[]{:S(2)}) copy-start(bf16[32,4096]{1,0:T(8,128)(2,1)} %g_ref.1) | copy-start | bytes 786436
  7.8 20.7 %all-to-all-start = ((bf16[8,64,1024]{2,1,0:T(8,128)(2,1)}), bf16[8,64,1024]{2,1,0:T(8,128)(2,1)S(1)}, u32[]{:S(2)}, u32[]{:S(2)}) async-start(bf16[8,64,1024]{2,1,0:T(8,128)(2,1)} %conv_pack.1), calls=%async_computation | async-start | bytes 2097152 | tf_op jit(solution)/shard_map/all_to_all | solution.py:506
  17.9 20.6 %copy-start.15 = (bf16[128,128]{1,0:T(8,128)(2,1)S(1)}, bf16[128,128]{1,0:T(8,128)(2,1)}, u32[]{:S(2)}) copy-start(bf16[128,128]{1,0:T(8,128)(2,1)} %param.20) | copy-start | bytes 98308
  28.5 42.8 %all-to-all-start.1 = ((bf16[32,144,128]{2,1,0:T(8,128)(2,1)}), bf16[32,144,128]{2,1,0:T(8,128)(2,1)S(1)}, u32[]{:S(2)}, u32[]{:S(2)}) async-start(bf16[32,144,128]{2,1,0:T(8,128)(2,1)} %attn_pack.1), calls=%async_computation.1 | async-start | bytes 2359296 | tf_op jit(solution)/shard_map/all_to_all | solution.py:512
  32.5 25.4 %copy-start.14 = (s32[12]{0:T(128)S(1)}, s32[12]{0:T(128)}, u32[]{:S(2)}) copy-start(s32[12]{0:T(128)} %lens_ref.3) | copy-start | bytes 148
  32.6 24.6 %collective-permute-start.1 = (bf16[4,32,1024]{2,1,0:T(8,128)(2,1)S(1)}, bf16[4,32,1024]{2,1,0:T(8,128)(2,1)S(1)}, u32[]{:S(2)}, u32[]{:S(2)}) collective-permute-start(bf16[4,32,1024]{2,1,0:T(8,128)(2,1)S(1)} %get-tuple-element.35), channel_id=1, source_target_pairs={{8,0},{9,1},{10,2},{11,3},{12,4},{13,5},{14,6},{15,7},{16,8},{17,9... | collective-permute-start | bytes 786440 | tf_op jit(solution)/shard_map/ppermute | solution.py:484
  33.9 24.0 %collective-permute-start = (bf16[4,32,1024]{2,1,0:T(8,128)(2,1)S(1)}, bf16[4,32,1024]{2,1,0:T(8,128)(2,1)S(1)}, u32[]{:S(2)}, u32[]{:S(2)}) collective-permute-start(bf16[4,32,1024]{2,1,0:T(8,128)(2,1)S(1)} %get-tuple-element.36), channel_id=1, source_target_pairs={{0,8},{1,9},{2,10},{3,11},{4,12},{5,13},{6,14},{7,15},{8,16},{9,17... | collective-permute-start | bytes 786440 | tf_op jit(solution)/shard_map/ppermute | solution.py:484
  71.3 19.6 %all-to-all-start.2 = ((bf16[8,64,1024]{2,1,0:T(8,128)(2,1)}), bf16[8,64,1024]{2,1,0:T(8,128)(2,1)S(1)}, u32[]{:S(2)}, u32[]{:S(2)}) async-start(bf16[8,64,1024]{2,1,0:T(8,128)(2,1)} %get-tuple-element.25), calls=%async_computation.2 | async-start | bytes 2097152 | tf_op jit(solution)/shard_map/all_to_all | solution.py:526
  80.0 0.9 copy-start.6
  80.9 46.7 %copy-start.1 = (bf16[32,8192]{1,0:T(8,128)(2,1)S(1)}, bf16[32,8192]{1,0:T(8,128)(2,1)}, u32[]{:S(2)}) copy-start(bf16[32,8192]{1,0:T(8,128)(2,1)} %ck_ref.3) | copy-start | bytes 1572868
  80.9 46.7 %copy-start.3 = (bf16[32,8192]{1,0:T(8,128)(2,1)S(1)}, bf16[32,8192]{1,0:T(8,128)(2,1)}, u32[]{:S(2)}) copy-start(bf16[32,8192]{1,0:T(8,128)(2,1)} %cv_ref.3) | copy-start | bytes 1572868
  80.9 46.7 %copy-start.5 = (bf16[32,8192]{1,0:T(8,128)(2,1)S(1)}, bf16[32,8192]{1,0:T(8,128)(2,1)}, u32[]{:S(2)}) copy-start(bf16[32,8192]{1,0:T(8,128)(2,1)} %cg_ref.3) | copy-start | bytes 1572868
  90.9 39.8 %all-to-all-start.3 = ((bf16[32,96,128]{2,1,0:T(8,128)(2,1)}), bf16[32,96,128]{2,1,0:T(8,128)(2,1)S(1)}, u32[]{:S(2)}, u32[]{:S(2)}) async-start(bf16[32,96,128]{2,1,0:T(8,128)(2,1)} %copy-done.6), calls=%async_computation.3 | async-start | bytes 1572864 | tf_op jit(solution)/shard_map/all_to_all | solution.py:546
  100.7 14.2 %collective-permute-start.2 = (f32[64,128]{1,0:T(8,128)}, f32[64,128]{1,0:T(8,128)S(1)}, u32[]{:S(2)}, u32[]{:S(2)}) collective-permute-start(f32[64,128]{1,0:T(8,128)} %copy-done.13), channel_id=1, source_target_pairs={{0,8},{1,9},{2,10},{3,11},{4,12},{5,13},{6,14},{7,15},{8,0},{9,1},... | collective-permute-start | bytes 98312 | tf_op jit(solution)/shard_map/ppermute | solution.py:488
  115.7 7.1 %collective-permute-start.3 = (f32[64,128]{1,0:T(8,128)S(1)}, f32[64,128]{1,0:T(8,128)S(1)}, u32[]{:S(2)}, u32[]{:S(2)}) collective-permute-start(f32[64,128]{1,0:T(8,128)S(1)} %add.10), channel_id=1, source_target_pairs={{0,16},{1,17},{2,18},{3,19},{4,20},{5,21},{6,22},{7,23},{8,24},{9,... | collective-permute-start | bytes 98312 | tf_op jit(solution)/shard_map/ppermute | solution.py:488
  123.0 3.9 %collective-permute-start.4 = (f32[64,128]{1,0:T(8,128)S(1)}, f32[64,128]{1,0:T(8,128)S(1)}, u32[]{:S(2)}, u32[]{:S(2)}) collective-permute-start(f32[64,128]{1,0:T(8,128)S(1)} %pad_maximum_fusion.1), channel_id=1, source_target_pairs={{0,4},{1,5},{2,6},{3,7},{4,0},{5,1},{6,2},{7,3},{8,12},{9,13},{10,... | collective-permute-start | bytes 98312 | tf_op jit(solution)/shard_map/ppermute | solution.py:488
  (1 other events, 0.6 us)

commit v2 on v1

--- a/solution.py
+++ b/solution.py
@@ -12,6 +12,8 @@
 GROUP = 16
 FILTER_LEN = 128
 LANES = 128
+STEP = 1024
+UNROLL = True
 BAND_REACH = 320
 DEVICES = ("seq", "ch")
 NEG_FILL = -1e30
@@ -33,6 +35,12 @@
 
 def cost(flops, bytes_accessed):
     return pl.CostEstimate(flops=flops, bytes_accessed=bytes_accessed, transcendentals=0)
+
+
+def split_terms(x):
+    high = x.astype(BF16)
+    low = (x - high.astype(F32)).astype(BF16)
+    return high, low
 
 
 def doc_start(lens_ref, positions):
@@ -44,12 +52,26 @@
     return start
 
 
-def conv_pack_kernel(cq_ref, ck_ref, cv_ref, cg_ref, out_ref):
+def member_index(ch_count, inner):
+    return lax.rem(lax.axis_index("seq"), inner) * ch_count + lax.axis_index("ch")
+
+
+def chunk_piece(chunk, ch_count, inner):
+    owner = lax.rem(chunk, inner) * ch_count + chunk // inner
+    return jnp.bitwise_xor(owner, member_index(ch_count, inner))
+
+
+def conv_pack_kernel(inner, ch_count, cq_ref, ck_ref, cv_ref, cg_ref, *out_refs):
     rows = cq_ref.shape[0]
-    mixed = ck_ref[...].astype(F32) * cv_ref[...].astype(F32)
-    grad = cg_ref[...].astype(F32) * cq_ref[...].astype(F32)
-    out_ref[0, 0:rows, :] = mixed.astype(BF16)
-    out_ref[0, rows:, :] = grad.astype(BF16)
+    piece = chunk_piece(pl.program_id(0), ch_count, inner)
+    mixed = (ck_ref[...].astype(F32) * cv_ref[...].astype(F32)).astype(BF16)
+    grad = (cg_ref[...].astype(F32) * cq_ref[...].astype(F32)).astype(BF16)
+    for k, out_ref in enumerate(out_refs):
+
+        @pl.when(piece == k)
+        def _():
+            out_ref[0:rows, :] = mixed
+            out_ref[rows:, :] = grad
 
 
 def conv_pack(cq, ck, cv, cg, inner, ch_count):
@@ -58,42 +80,70 @@
     width = channels // members
     spec = pl.BlockSpec((rows, width), lambda k: (0, k))
     return pl.pallas_call(
-        conv_pack_kernel,
+        functools.partial(conv_pack_kernel, inner, ch_count),
         grid=(members,),
         in_specs=[spec] * 4,
-        out_specs=pl.BlockSpec(
-            (1, 2 * rows, width), lambda k: (lax.rem(k, inner) * ch_count + k // inner, 0, 0)
-        ),
-        out_shape=jax.ShapeDtypeStruct((members, 2 * rows, width), BF16),
+        out_specs=[pl.BlockSpec((2 * rows, width), lambda k: (0, 0))] * members,
+        out_shape=[jax.ShapeDtypeStruct((2 * rows, width), BF16)] * members,
+        cost_estimate=cost(4 * rows * channels, 12 * rows * channels),
         compiler_params=params(),
-        cost_estimate=cost(4 * rows * channels, 12 * rows * channels),
         name="conv_pack",
     )(cq, ck, cv, cg)
 
 
-def attn_pack_kernel(rows, q_ref, k_ref, v_ref, o_ref, g_ref, out_ref, prod_ref):
+def conv_join_kernel(rows, inner, ch_count, *refs):
+    members = inner * ch_count
+    pieces, outs = refs[:members], refs[members:]
+    half = members // 2
+    me = member_index(ch_count, inner)
+    for k, x_ref in enumerate(pieces):
+        source = jnp.bitwise_xor(me, k)
+        for part in range(2):
+
+            @pl.when(source // half == part)
+            def _():
+                at = pl.multiple_of((source - part * half) * rows, rows)
+                outs[part][pl.ds(at, rows), :] = x_ref[0:rows, :]
+                outs[2 + part][pl.ds(at, rows), :] = x_ref[rows : 2 * rows, :]
+
+
+def conv_join(pieces, rows, inner, ch_count):
+    members, width = len(pieces), pieces[0].shape[1]
+    step = min(width, 512)
+    shape = jax.ShapeDtypeStruct((members * rows // 2, width), BF16)
+    return pl.pallas_call(
+        functools.partial(conv_join_kernel, rows, inner, ch_count),
+        grid=(width // step,),
+        in_specs=[pl.BlockSpec((2 * rows, step), lambda j: (0, j))] * members,
+        out_specs=[pl.BlockSpec((members * rows // 2, step), lambda j: (0, j))] * 4,
+        out_shape=[shape] * 4,
+        cost_estimate=cost(0, 8 * members * rows * width),
+        name="conv_join",
+    )(*pieces)
+
+
+def attn_pack_kernel(rows, q_ref, k_ref, v_ref, o_ref, g_ref, out_ref):
     heads = q_ref.shape[1] // HEAD_DIM
     span = LANES // rows
     offset = lax.rem(lax.axis_index("ch"), span) * rows
-    prod_ref[...] = jnp.zeros_like(prod_ref)
-    ones = jnp.ones((8, HEAD_DIM), F32)
-    row = lax.broadcasted_iota(jnp.int32, (8, LANES), 0)
+    product = g_ref[...].astype(F32) * o_ref[...].astype(F32)
+    shape = (max(heads, 8), heads * HEAD_DIM)
+    owner = lax.broadcasted_iota(jnp.int32, shape, 1) // HEAD_DIM
+    chosen = (owner == lax.broadcasted_iota(jnp.int32, shape, 0)).astype(F32).astype(BF16)
+    high, low = split_terms(product)
+    delta = dot(chosen, high, NT) + dot(chosen, low, NT)
+    delta = jnp.concatenate([delta, jnp.zeros((delta.shape[0], LANES - rows), F32)], axis=1)
+    delta = pltpu.roll(delta, offset, 1)
+    high = delta.astype(BF16).astype(F32)
+    low = delta - high
+    row = lax.broadcasted_iota(jnp.int32, (16, LANES), 0)
     for h in range(heads):
         cols = slice(h * HEAD_DIM, (h + 1) * HEAD_DIM)
         out_ref[h, 0:rows, :] = q_ref[:, cols]
         out_ref[h, rows : 2 * rows, :] = k_ref[:, cols]
         out_ref[h, 2 * rows : 3 * rows, :] = v_ref[:, cols]
         out_ref[h, 3 * rows : 4 * rows, :] = g_ref[:, cols]
-        prod_ref[pl.ds(pl.multiple_of(offset, rows), rows), :] = g_ref[:, cols].astype(
-            F32
-        ) * o_ref[:, cols].astype(F32)
-        delta = lax.dot_general(
-            ones, prod_ref[...], NT, precision=lax.Precision.HIGHEST, preferred_element_type=F32
-        )
-        high = delta.astype(BF16).astype(F32)
-        low = delta - high
-        tile = jnp.where(row == 0, high, jnp.where(row == 1, low, 0.0))
-        tile = jnp.concatenate([tile, jnp.zeros_like(tile)], axis=0)
+        tile = jnp.where(row == 0, high[h : h + 1], jnp.where(row == 1, low[h : h + 1], 0.0))
         out_ref[h, 4 * rows : 4 * rows + 16, :] = tile.astype(BF16)
 
 
@@ -109,17 +159,9 @@
         in_specs=[spec] * 5,
         out_specs=pl.BlockSpec((step, height, HEAD_DIM), lambda j: (j, 0, 0)),
         out_shape=jax.ShapeDtypeStruct((heads, height, HEAD_DIM), BF16),
-        scratch_shapes=[pltpu.VMEM((LANES, HEAD_DIM), F32)],
-        compiler_params=params(),
         cost_estimate=cost(4 * rows * features, 20 * rows * features),
         name="attn_pack",
     )(q, k, v, o, g)
-
-
-def split_terms(x):
-    high = x.astype(BF16)
-    low = (x - high.astype(F32)).astype(BF16)
-    return high, low
 
 
 def attn_kernel(rows, reach, lens_ref, x_ref, out_ref, dk_ref, dv_ref):
@@ -188,7 +230,6 @@
             pltpu.VMEM((tokens, HEAD_DIM), F32),
             pltpu.VMEM((tokens, HEAD_DIM), F32),
         ],
-        compiler_params=params(),
         cost_estimate=cost(20 * tokens * 512 * HEAD_DIM, 4 * x.size),
         name="attn_head",
     )(lens, x)
@@ -213,143 +254,150 @@
         in_specs=[pl.BlockSpec((step, 3 * rows, HEAD_DIM), lambda j: (j, 0, 0))],
         out_specs=[spec] * 3,
         out_shape=[shape] * 3,
+        cost_estimate=cost(0, 4 * x.size),
         compiler_params=params(),
-        cost_estimate=cost(0, 4 * x.size),
         name="attn_unpack",
     )(x)
 
 
-def conv_kernel(
-    rows, inner, ch_count, lens_ref, x_ref, prior_ref, later_ref, tap_ref, rev_ref, out_ref, filt_ref,
-    back_ref, front_ref,
+def circulant(row):
+    rolled = pltpu.roll(jnp.broadcast_to(row, (8, LANES)), 0, 1, stride=1, stride_axis=0)
+    pieces = [rolled if a == 0 else pltpu.roll(rolled, 8 * a, 1) for a in range(LANES // 8)]
+    full = jnp.concatenate(pieces, axis=0).astype(BF16)
+    return jnp.concatenate([full, full], axis=1)
+
+
+def unskewed(outer):
+    sub = lax.broadcasted_iota(jnp.int32, (8, LANES), 0)
+    folded = outer[0:8]
+    for a in range(1, LANES // 8):
+        folded = folded + pltpu.roll(outer[8 * a : 8 * a + 8], LANES - 8 * a, 1)
+    for bit in (1, 2, 4):
+        folded = jnp.where((sub & bit) != 0, pltpu.roll(folded, LANES - bit, 1), folded)
+    return jnp.sum(folded, axis=0, keepdims=True)
+
+
+def conv_core_kernel(
+    rows, inner, ch_count, lens_ref, tap_ref, rev_ref, prior_ref, m0_ref, m1_ref, g0_ref, g1_ref,
+    later_ref, *refs,
 ):
-    sources = x_ref.shape[0]
-    per = LANES // rows
-    blocks = sources // per
-    tile = pl.program_id(0)
-
-    @pl.when(tile == 0)
+    members = inner * ch_count
+    outs, filt_ref = refs[:members], refs[members]
+    back_ref, front_ref, conv_ref, down_ref = refs[members + 1 :]
+    me = member_index(ch_count, inner)
+    groups = LANES // GROUP
+    blocks = 2
+
+    @pl.when(pl.program_id(0) == 0)
     def _():
-        base = (lax.axis_index("seq") // inner) * (sources * rows)
+        base = (lax.axis_index("seq") // inner) * (members * rows)
         shape = (LANES, 2 * LANES)
         down = lax.broadcasted_iota(jnp.int32, shape, 0)
         across = lax.broadcasted_iota(jnp.int32, shape, 1)
-        for b in range(blocks):
-            out_pos = base + b * LANES + down
-            in_pos = base + (b - 1) * LANES + across
+
+        def reached(out_pos, in_pos):
             gap = out_pos - in_pos
             near = (gap >= 0) & (gap < FILTER_LEN) & (in_pos >= doc_start(lens_ref, out_pos))
-            back_ref[b] = near.astype(F32).astype(BF16)
-            in_pos = base + b * LANES + down
-            out_pos = base + b * LANES + across
-            gap = out_pos - in_pos
-            near = (gap >= 0) & (gap < FILTER_LEN) & (in_pos >= doc_start(lens_ref, out_pos))
-            front_ref[b] = near.astype(F32).astype(BF16)
-
-    mixed = jnp.concatenate(
-        [prior_ref[...].reshape(LANES, LANES), x_ref[:, 0:rows, :].reshape(sources * rows, LANES)],
-        axis=0,
-    )
-    grad = jnp.concatenate(
-        [x_ref[:, rows : 2 * rows, :].reshape(sources * rows, LANES), later_ref[...].reshape(LANES, LANES)],
-        axis=0,
-    )
-    lane_group = lax.broadcasted_iota(jnp.int32, (LANES, LANES), 1) // GROUP
-    sub = lax.broadcasted_iota(jnp.int32, (8, LANES), 0)
-    conv_out = [jnp.zeros((LANES, LANES), F32) for _ in range(blocks)]
-    mixed_grad = [jnp.zeros((LANES, LANES), F32) for _ in range(blocks)]
-    groups = LANES // GROUP
-
-    def circulant(row):
-        rolled = pltpu.roll(jnp.broadcast_to(row, (8, LANES)), 0, 1, stride=1, stride_axis=0)
-        pieces = [rolled if a == 0 else pltpu.roll(rolled, 8 * a, 1) for a in range(LANES // 8)]
-        full = jnp.concatenate(pieces, axis=0).astype(BF16)
-        return jnp.concatenate([full, full], axis=1)
-
-    for g in range(groups):
-        mine = lane_group == g
-        back_taps = circulant(rev_ref[g : g + 1, :])
-        front_taps = circulant(tap_ref[g : g + 1, :])
-        outer = jnp.zeros((LANES, LANES), F32)
+            return near.astype(F32).astype(BF16)
+
         for b in range(blocks):
-            window = mixed[b * LANES : (b + 2) * LANES]
-            ahead = grad[b * LANES : (b + 2) * LANES]
-            here = jnp.where(mine, ahead[0:LANES].astype(F32), 0.0).astype(BF16)
-            conv_out[b] = jnp.where(mine, dot(back_taps * back_ref[b], window, NN), conv_out[b])
-            mixed_grad[b] = jnp.where(mine, dot(front_taps * front_ref[b], ahead, NN), mixed_grad[b])
-            full = dot(here, window, NT) * back_ref[b].astype(F32)
-            outer = outer + full[:, 0:LANES] + full[:, LANES:]
-        folded = outer[0:8]
-        for a in range(1, LANES // 8):
-            folded = folded + pltpu.roll(outer[8 * a : 8 * a + 8], LANES - 8 * a, 1)
-        for bit in (1, 2, 4):
-            folded = jnp.where((sub & bit) != 0, pltpu.roll(folded, LANES - bit, 1), folded)
-        filt_ref[g : g + 1, :] = jnp.sum(folded, axis=0, keepdims=True)
-    for b in range(blocks):
-        here = slice(b * per, (b + 1) * per)
-        out_ref[here, 0:rows, :] = conv_out[b].astype(BF16).reshape(per, rows, LANES)
-        out_ref[here, rows : 2 * rows, :] = mixed_grad[b].astype(BF16).reshape(per, rows, LANES)
-
-
-def conv_core(lens, x, prior, later, taps, rev_taps, rows, inner, ch_count):
-    sources, _, width = x.shape
-    per = LANES // rows
-    blocks = sources // per
-    tiles = width // LANES
-    groups = LANES // GROUP
-    spec = pl.BlockSpec((sources, 2 * rows, LANES), lambda j: (0, 0, j))
-    halo = pl.BlockSpec((per, rows, LANES), lambda j: (0, 0, j))
-    tap_spec = pl.BlockSpec((groups, FILTER_LEN), lambda j: (j, 0))
+            first = base + b * LANES
+            back_ref[b] = reached(first + down, first - LANES + across)
+            front_ref[b] = reached(first + across, first + down)
+
+    def one_tile(tile, carried):
+        cols = pl.ds(pl.multiple_of(tile * LANES, LANES), LANES)
+        mixed = [r[:, cols] for r in (prior_ref, m0_ref, m1_ref)]
+        grad = [r[:, cols] for r in (g0_ref, g1_ref, later_ref)]
+        lane_group = lax.broadcasted_iota(jnp.int32, (LANES, LANES), 1) // GROUP
+        tap_rows = pl.ds(pl.multiple_of(tile * groups, groups), groups)
+        taps, rev_taps = tap_ref[tap_rows, :], rev_ref[tap_rows, :]
+        back_taps = [circulant(rev_taps[g : g + 1]) for g in range(groups)]
+        front_taps = [circulant(taps[g : g + 1]) for g in range(groups)]
+        outer = [jnp.zeros((LANES, LANES), F32)] * groups
+        for b in range(blocks):
+            back, front = back_ref[b], front_ref[b]
+            back32 = back.astype(F32)
+            window = jnp.concatenate(mixed[b : b + 2], axis=0)
+            ahead = jnp.concatenate(grad[b : b + 2], axis=0)
+            conv_all = dot(jnp.concatenate([t * back for t in back_taps], axis=0), window, NN)
+            down_all = dot(jnp.concatenate([t * front for t in front_taps], axis=0), ahead, NN)
+            conv_out = jnp.zeros((LANES, LANES), F32)
+            mixed_grad = jnp.zeros((LANES, LANES), F32)
+            for g in range(groups):
+                mine = lane_group == g
+                span = slice(g * LANES, (g + 1) * LANES)
+                conv_out = jnp.where(mine, conv_all[span], conv_out)
+                mixed_grad = jnp.where(mine, down_all[span], mixed_grad)
+                chosen = grad[b] * mine.astype(F32).astype(BF16)
+                full = dot(chosen, window, NT) * back32
+                outer[g] = outer[g] + full[:, 0:LANES] + full[:, LANES:]
+            here = slice(b * LANES, (b + 1) * LANES)
+            conv_ref[here, cols] = conv_out.astype(BF16)
+            down_ref[here, cols] = mixed_grad.astype(BF16)
+        filt_ref[tap_rows, :] = jnp.concatenate([unskewed(o) for o in outer], axis=0)
+        return carried
+
+    lax.fori_loop(0, m0_ref.shape[1] // LANES, one_tile, 0, unroll=UNROLL)
+    for k, out_ref in enumerate(outs):
+        at = pl.multiple_of(jnp.bitwise_xor(me, k) * rows, rows)
+        out_ref[0:rows, :] = conv_ref[pl.ds(at, rows), :]
+        out_ref[rows : 2 * rows, :] = down_ref[pl.ds(at, rows), :]
+
+
+def conv_core(lens, taps, rev_taps, arrays, rows, inner, ch_count):
+    members = inner * ch_count
+    width = arrays[0].shape[1]
+    step = min(width, STEP)
+    spec = pl.BlockSpec((LANES, step), lambda j: (0, j))
+    piece = pl.BlockSpec((2 * rows, step), lambda j: (0, j))
+    tap_spec = pl.BlockSpec((step // GROUP, FILTER_LEN), lambda j: (j, 0))
     return pl.pallas_call(
-        functools.partial(conv_kernel, rows, inner, ch_count),
-        grid=(tiles,),
-        in_specs=[pl.BlockSpec(memory_space=pltpu.SMEM), spec, halo, halo, tap_spec, tap_spec],
-        out_specs=[spec, tap_spec],
-        out_shape=[
-            jax.ShapeDtypeStruct(x.shape, BF16),
-            jax.ShapeDtypeStruct((width // GROUP, FILTER_LEN), F32),
-        ],
-        scratch_shapes=[
-            pltpu.VMEM((blocks, LANES, 2 * LANES), BF16),
-            pltpu.VMEM((blocks, LANES, 2 * LANES), BF16),
-        ],
-        compiler_params=params(),
-        cost_estimate=cost(12 * sources * rows * 2 * LANES * LANES * tiles, 8 * x.size),
+        functools.partial(conv_core_kernel, rows, inner, ch_count),
+        grid=(width // step,),
+        in_specs=[pl.BlockSpec(memory_space=pltpu.SMEM), tap_spec, tap_spec] + [spec] * 6,
+        out_specs=[piece] * members + [tap_spec],
+        out_shape=[jax.ShapeDtypeStruct((2 * rows, width), BF16)] * members
+        + [jax.ShapeDtypeStruct((width // GROUP, FILTER_LEN), F32)],
+        scratch_shapes=[pltpu.VMEM((2, LANES, 2 * LANES), BF16)] * 2
+        + [pltpu.VMEM((2 * LANES, step), BF16)] * 2,
+        cost_estimate=cost(96 * LANES * LANES * width, 24 * LANES * width),
         name="conv_core",
-    )(lens, x, prior, later, taps, rev_taps)
-
-
-def conv_unpack_kernel(x_ref, ck_ref, cv_ref, cg_ref, gq_ref, gk_ref, gv_ref):
+    )(lens, taps, rev_taps, *arrays)
+
+
+def conv_unpack_kernel(inner, ch_count, ck_ref, cv_ref, cg_ref, *refs):
+    members = inner * ch_count
+    pieces, (gq_ref, gk_ref, gv_ref) = refs[:members], refs[members:]
     rows = ck_ref.shape[0]
-    conv_out = x_ref[0, 0:rows, :].astype(F32)
-    mixed_grad = x_ref[0, rows : 2 * rows, :].astype(F32)
-    gq_ref[...] = (cg_ref[...].astype(F32) * conv_out).astype(BF16)
-    gk_ref[...] = (mixed_grad * cv_ref[...].astype(F32)).astype(BF16)
-    gv_ref[...] = (mixed_grad * ck_ref[...].astype(F32)).astype(BF16)
-
-
-def conv_unpack(x, ck, cv, cg, inner, ch_count):
+    piece = chunk_piece(pl.program_id(0), ch_count, inner)
+    for k, x_ref in enumerate(pieces):
+
+        @pl.when(piece == k)
+        def _():
+            conv_out = x_ref[0:rows, :].astype(F32)
+            mixed_grad = x_ref[rows : 2 * rows, :].astype(F32)
+            gq_ref[...] = (cg_ref[...].astype(F32) * conv_out).astype(BF16)
+            gk_ref[...] = (mixed_grad * cv_ref[...].astype(F32)).astype(BF16)
+            gv_ref[...] = (mixed_grad * ck_ref[...].astype(F32)).astype(BF16)
+
+
+def conv_unpack(pieces, ck, cv, cg, inner, ch_count):
     rows, channels = ck.shape
-    members, _, width = x.shape
+    members = inner * ch_count
+    width = channels // members
     spec = pl.BlockSpec((rows, width), lambda k: (0, k))
     shape = jax.ShapeDtypeStruct((rows, channels), BF16)
     return pl.pallas_call(
-        conv_unpack_kernel,
+        functools.partial(conv_unpack_kernel, inner, ch_count),
         grid=(members,),
-        in_specs=[
-            pl.BlockSpec(
-                (1, 2 * rows, width), lambda k: (lax.rem(k, inner) * ch_count + k // inner, 0, 0)
-            ),
-            spec,
-            spec,
-            spec,
-        ],
+        in_specs=[spec] * 3 + [pl.BlockSpec((2 * rows, width), lambda k: (0, 0))] * members,
         out_specs=[spec] * 3,
         out_shape=[shape] * 3,
+        cost_estimate=cost(6 * rows * channels, 16 * rows * channels),
         compiler_params=params(),
-        cost_estimate=cost(6 * rows * channels, 16 * rows * channels),
         name="conv_unpack",
-    )(x, ck, cv, cg)
+    )(ck, cv, cg, *pieces)
 
 
 def doc_index(doc_lengths, positions):
@@ -498,35 +546,36 @@
     inner = 2
     members = inner * ch_count
     outer = seq_count // inner
-    near = [[base + i for i in range(members)] for base in range(0, count, members)]
     heads = attn_query.shape[1] // HEAD_DIM
     head_each = heads == count
 
-    packed = conv_pack(conv_query, conv_key, conv_value, conv_grad_out, inner, ch_count)
-    conv_in = lax.all_to_all(
-        packed, DEVICES, split_axis=0, concat_axis=0, tiled=True, axis_index_groups=near
-    )
+    reach = BAND_REACH if rows * count == 1024 else rows * count
+
     if head_each:
         attn_packed = attn_pack(attn_query, attn_key, attn_value, attn_output, attn_grad_out)
-        attn_packed, conv_in = lax.optimization_barrier((attn_packed, conv_in))
         attn_in = lax.all_to_all(attn_packed, DEVICES, split_axis=0, concat_axis=0, tiled=True)
 
-    per = FILTER_LEN // rows
-    prior = shifted(conv_in[members - per :, 0:rows, :], members, count)
-    later = shifted(conv_in[:per, rows:, :], -members, count)
+    packed = conv_pack(conv_query, conv_key, conv_value, conv_grad_out, inner, ch_count)
+    pieces = [packed[0]] + [exchanged(packed[k], k, count) for k in range(1, members)]
+    mixed_lo, mixed_hi, grad_lo, grad_hi = conv_join(pieces, rows, inner, ch_count)
+    if head_each:
+        attn_in, mixed_hi, grad_lo = lax.optimization_barrier((attn_in, mixed_hi, grad_lo))
+    prior, later = shifted(mixed_hi, members, count), shifted(grad_lo, -members, count)
     group_count = channels // members // GROUP
     y = lax.rem(lax.axis_index("seq"), inner)
     taps = lax.dynamic_slice_in_dim(conv_filter, y * group_count, group_count, 0).astype(F32)
     rev_taps = jnp.roll(taps[:, ::-1], 1, axis=1)
-    conv_back, filter_part = conv_core(
-        doc_lengths, conv_in, prior, later, taps, rev_taps, rows, inner, ch_count
-    )
     if head_each:
-        attn_in, conv_back = lax.optimization_barrier((attn_in, conv_back))
-    conv_res = lax.all_to_all(
-        conv_back, DEVICES, split_axis=0, concat_axis=0, tiled=True, axis_index_groups=near
-    )
-
+        attn_back = attn_head(doc_lengths, attn_in, rows, reach)
+        attn_back, prior, later = lax.optimization_barrier((attn_back, prior, later))
+        attn_res = lax.all_to_all(attn_back, DEVICES, split_axis=0, concat_axis=0, tiled=True)
+    own = (prior, mixed_lo, mixed_hi, grad_lo, grad_hi, later)
+    *conv_back, filter_part = conv_core(
+        doc_lengths, taps, rev_taps, own, rows, inner, ch_count
+    )
+    conv_res = [conv_back[0]] + [exchanged(conv_back[k], k, count) for k in range(1, members)]
+
+    filter_part, conv_res[2] = lax.optimization_barrier((filter_part, conv_res[2]))
     distance = members
     while distance < count:
         filter_part = filter_part + exchanged(filter_part, distance, count)
@@ -538,19 +587,14 @@
         jnp.concatenate([filter_part, other], axis=0),
         jnp.concatenate([other, filter_part], axis=0),
     )
-
-    if head_each:
-        reach = BAND_REACH if rows * count == 1024 else rows * count
-        attn_back = attn_head(doc_lengths, attn_in, rows, reach)
-        attn_back, conv_res = lax.optimization_barrier((attn_back, conv_res))
-        attn_res = lax.all_to_all(attn_back, DEVICES, split_axis=0, concat_axis=0, tiled=True)
-    grad_conv = conv_unpack(conv_res, conv_key, conv_value, conv_grad_out, inner, ch_count)
     if head_each:
         grad_attn = attn_unpack(attn_res, rows)
+        *grad_attn, conv_res[-1] = lax.optimization_barrier((*grad_attn, conv_res[-1]))
     else:
         grad_attn = attn_gathered(
             attn_query, attn_key, attn_value, attn_output, attn_grad_out, doc_lengths
         )
+    grad_conv = conv_unpack(conv_res, conv_key, conv_value, conv_grad_out, inner, ch_count)
     return (*grad_attn, *grad_conv, grad_filter)
 
 

time: 133 us -> 104 us (0.78)
  waiting for transfers between devices: 57 us -> 37.9 us
  local copies, waits for them, and re-layouts: 6.04 us -> 1.66 us
  starting transfers between devices: 37.1 us -> 33.5 us
  Pallas kernels: 29.5 us -> 27.5 us
    all_to_all x2 -> x0, waiting for transfers between devices: 20.6 us -> none  [the longest x1 10.6 us: body(): lax.all_to_all(packed, DEVICES, split_axis=0, concat_axis=0, tiled=True,...]
    ppermute x3 -> x17, waiting for transfers between devices: 17.2 us -> 34.4 us  [exchanged(): lax.ppermute(block, DEVICES, [(i, i ^ distance) for i in range(count)])]
    ppermute x2, waiting for transfers between devices: 19.2 us -> 3.45 us  [shifted(): return lax.ppermute(block, DEVICES, route)]
    ppermute x3 -> x17, starting transfers between devices: 7.96 us -> 18.3 us  [exchanged(): lax.ppermute(block, DEVICES, [(i, i ^ distance) for i in range(count)])]
    all_to_all x2 -> x0, starting transfers between devices: 9.47 us -> none  [the longest x1 5.31 us: body(): lax.all_to_all(packed, DEVICES, split_axis=0, concat_axis=0, tiled=True,...]
    all_to_all x1, starting transfers between devices: 9.86 us -> 3.58 us  [body(): lax.all_to_all(attn_back, DEVICES, split_axis=0, concat_axis=0, tiled=True)]
    unnamed x32 -> x36, local copies, waits for them, and re-layouts: 5.71 us -> 1.36 us
    all_to_all x1, starting transfers between devices: 4 us -> 7.3 us  [body(): lax.all_to_all(attn_packed, DEVICES, split_axis=0, concat_axis=0, tiled=T...]
  transfers between devices with their start and end apart: 9 -> 21, of which waited for: 7 -> 12; matrix products, arithmetic and copies ran while one was open for 2% -> 2% of each run, Pallas kernels for 19% -> 20%
where the time goes in v2:
time: 104 us
  waiting for transfers between devices  37.9 us (36%)
  starting transfers between devices  33.5 us (32%)
  Pallas kernels  27.5 us (26%)
  other arithmetic  2.27 us (2%)
  local copies, waits for them, and re-layouts  1.66 us (2%)
    ppermute x17, waiting for transfers between devices, exchanged(): lax.ppermute(block, DEVICES, [(i, i ^ distance) for i in range(count)])  34.4 us
    ppermute x17, starting transfers between devices, exchanged(): lax.ppermute(block, DEVICES, [(i, i ^ distance) for i in range(count)])  18.3 us
    pallas_call x1, Pallas kernels, conv_core(): pl.pallas_call(functools.partial(conv_core_kernel, rows, inner, ch_count)...  9.45 us
    all_to_all x1, starting transfers between devices, body(): lax.all_to_all(attn_packed, DEVICES, split_axis=0, concat_axis=0, tiled=T...  7.3 us
    pallas_call x1, Pallas kernels, attn_head(): pl.pallas_call(functools.partial(attn_kernel, rows, reach), in_specs=[pl....  6.18 us
    ppermute x2, starting transfers between devices, shifted(): return lax.ppermute(block, DEVICES, route)  4.37 us
    pallas_call x1, Pallas kernels, attn_pack(): pl.pallas_call(functools.partial(attn_pack_kernel, rows), grid=(heads //...  3.88 us
    all_to_all x1, starting transfers between devices, body(): lax.all_to_all(attn_back, DEVICES, split_axis=0, concat_axis=0, tiled=True)  3.58 us
  transfers between devices with their start and end apart: 21, of which 12 were waited for; matrix products, arithmetic and copies ran while one was open for 2% of the time, Pallas kernels for 20%

profile of v2, /device:TPU:0, one launch (start us, length us, event | category | flops | bytes accessed | tf_op | source)
XLA Modules:
  0.0 103.6 jit_solution(15962868370686004139)
XLA Ops:
  0.6 3.9 %attn_pack.1 = bf16[32,144,128]{2,1,0:T(8,128)(2,1)} custom-call(bf16[32,4096]{1,0:T(8,128)(2,1)} %q_ref.1, bf16[32,4096]{1,0:T(8,128)(2,1)} %k_ref.1, bf16[32,4096]{1,0:T(8,128)(2,1)} %v_ref.1, bf16[32,4096]{1,0:T(8,128)(2,1)} %o_ref.1, bf16[32,4096]{1,0:T(8,128)(2,1)} %g_ref.1), custom_call_target="tpu_custom_call" | custom-call | flops 524288 | bytes 2621440 | tf_op jit(solution)/shard_map/attn_pack/pallas_call | solution.py:156
  4.5 7.3 %all-to-all-start = ((bf16[32,144,128]{2,1,0:T(8,128)(2,1)}), bf16[32,144,128]{2,1,0:T(8,128)(2,1)S(1)}, u32[]{:S(2)}, u32[]{:S(2)}) async-start(bf16[32,144,128]{2,1,0:T(8,128)(2,1)} %attn_pack.1), calls=%async_computation | async-start | bytes 2359296 | tf_op jit(solution)/shard_map/all_to_all | solution.py:556
  13.7 1.7 %collective-permute-start.1 = (bf16[64,1024]{1,0:T(8,128)(2,1)S(1)}, bf16[64,1024]{1,0:T(8,128)(2,1)S(1)}, u32[]{:S(2)}, u32[]{:S(2)}) collective-permute-start(bf16[64,1024]{1,0:T(8,128)(2,1)S(1)} %get-tuple-element.48), channel_id=1, source_target_pairs={{0,2},{1,3},{2,0},{3,1},{4,6},{5,7},{6,4},{7,5},{8,10},{9,11},{10,... | collective-permute-start | bytes 393224 | tf_op jit(solution)/shard_map/ppermute | solution.py:536
  15.4 1.7 %collective-permute-start.3 = (bf16[64,1024]{1,0:T(8,128)(2,1)S(1)}, bf16[64,1024]{1,0:T(8,128)(2,1)S(1)}, u32[]{:S(2)}, u32[]{:S(2)}) collective-permute-start(bf16[64,1024]{1,0:T(8,128)(2,1)S(1)} %get-tuple-element.50), channel_id=1, source_target_pairs={{0,4},{1,5},{2,6},{3,7},{4,0},{5,1},{6,2},{7,3},{8,12},{9,13},{10,... | collective-permute-start | bytes 393224 | tf_op jit(solution)/shard_map/ppermute | solution.py:536
  17.2 2.6 %collective-permute-start.5 = (bf16[64,1024]{1,0:T(8,128)(2,1)S(1)}, bf16[64,1024]{1,0:T(8,128)(2,1)S(1)}, u32[]{:S(2)}, u32[]{:S(2)}) collective-permute-start(bf16[64,1024]{1,0:T(8,128)(2,1)S(1)} %get-tuple-element.52), channel_id=1, source_target_pairs={{0,6},{1,7},{2,4},{3,5},{4,2},{5,3},{6,0},{7,1},{8,14},{9,15},{10,... | collective-permute-start | bytes 393224 | tf_op jit(solution)/shard_map/ppermute | solution.py:536
  19.8 6.9 %collective-permute-done.1.refs_2_ = bf16[64,1024]{1,0:T(8,128)(2,1)S(1)} collective-permute-done((bf16[64,1024]{1,0:T(8,128)(2,1)S(1)}, bf16[64,1024]{1,0:T(8,128)(2,1)S(1)}, u32[]{:S(2)}, u32[]{:S(2)}) %collective-permute-start.1) | collective-permute-done | bytes 131104 | tf_op jit(solution)/shard_map/ppermute | solution.py:536
  27.3 2.8 %collective-permute-done.2.refs_3_ = bf16[64,1024]{1,0:T(8,128)(2,1)S(1)} collective-permute-done((bf16[64,1024]{1,0:T(8,128)(2,1)S(1)}, bf16[64,1024]{1,0:T(8,128)(2,1)S(1)}, u32[]{:S(2)}, u32[]{:S(2)}) %collective-permute-start.2) | collective-permute-done | bytes 131104 | tf_op jit(solution)/shard_map/ppermute | solution.py:536
  30.1 5.5 %collective-permute-done.5.refs_6_ = bf16[64,1024]{1,0:T(8,128)(2,1)S(1)} collective-permute-done((bf16[64,1024]{1,0:T(8,128)(2,1)S(1)}, bf16[64,1024]{1,0:T(8,128)(2,1)S(1)}, u32[]{:S(2)}, u32[]{:S(2)}) %collective-permute-start.5) | collective-permute-done | bytes 131104 | tf_op jit(solution)/shard_map/ppermute | solution.py:536
  35.6 3.2 %collective-permute-done.6.refs_7_ = bf16[64,1024]{1,0:T(8,128)(2,1)S(1)} collective-permute-done((bf16[64,1024]{1,0:T(8,128)(2,1)S(1)}, bf16[64,1024]{1,0:T(8,128)(2,1)S(1)}, u32[]{:S(2)}, u32[]{:S(2)}) %collective-permute-start.6) | collective-permute-done | bytes 131104 | tf_op jit(solution)/shard_map/ppermute | solution.py:536
  39.4 2.2 %conv_join.1 = (bf16[128,1024]{1,0:T(8,128)(2,1)}, bf16[128,1024]{1,0:T(8,128)(2,1)}, bf16[128,1024]{1,0:T(8,128)(2,1)}, bf16[128,1024]{1,0:T(8,128)(2,1)}) custom-call(bf16[64,1024]{1,0:T(8,128)(2,1)} %copy-done.5, bf16[64,1024]{1,0:T(8,128)(2,1)} %copy-done.8, bf16[64,1024]{1,0:T(8,128)(2,1)} %copy-done.9, bf16[64,1024]{1,0:T(8,128)(2,1)} %copy-done.10, ...), custom_call_target="tpu_custom_call" | custom-call | bytes 2097152 | tf_op jit(solution)/shard_map/conv_join/pallas_call | solution.py:114
  41.7 3.1 %collective-permute-start.7 = (bf16[128,1024]{1,0:T(8,128)(2,1)}, bf16[128,1024]{1,0:T(8,128)(2,1)S(1)}, u32[]{:S(2)}, u32[]{:S(2)}) collective-permute-start(bf16[128,1024]{1,0:T(8,128)(2,1)} %get-tuple-element.57.m1_ref), channel_id=1, source_target_pairs={{0,8},{1,9},{2,10},{3,11},{4,12},{5,13},{6,14},{7,15},{8,16},{9,17... | collective-permute-start | bytes 786440 | tf_op jit(solution)/shard_map/ppermute | solution.py:532
  46.1 6.2 %attn_head.1 = bf16[32,96,128]{2,1,0:T(8,128)(2,1)} custom-call(s32[12]{0:T(128)} %lens_ref.3, bf16[32,144,128]{2,1,0:T(8,128)(2,1)} %copy-done.6), custom_call_target="tpu_custom_call" | custom-call | flops 1342177280 | bytes 2359296 | tf_op jit(solution)/shard_map/attn_head/pallas_call | solution.py:221
  52.3 3.4 %collective-permute-done.8.later_ref = bf16[128,1024]{1,0:T(8,128)(2,1)S(1)} collective-permute-done((bf16[128,1024]{1,0:T(8,128)(2,1)}, bf16[128,1024]{1,0:T(8,128)(2,1)S(1)}, u32[]{:S(2)}, u32[]{:S(2)}) %collective-permute-start.8) | collective-permute-done | bytes 262176 | tf_op jit(solution)/shard_map/ppermute | solution.py:532
  55.7 3.6 %all-to-all-start.1 = ((bf16[32,96,128]{2,1,0:T(8,128)(2,1)}), bf16[32,96,128]{2,1,0:T(8,128)(2,1)S(1)}, u32[]{:S(2)}, u32[]{:S(2)}) async-start(bf16[32,96,128]{2,1,0:T(8,128)(2,1)} %attn_head.1), calls=%async_computation.1 | async-start | bytes 1572864 | tf_op jit(solution)/shard_map/all_to_all | solution.py:571
  60.2 9.5 %conv_core.1 = (bf16[64,1024]{1,0:T(8,128)(2,1)}, bf16[64,1024]{1,0:T(8,128)(2,1)}, bf16[64,1024]{1,0:T(8,128)(2,1)}, bf16[64,1024]{1,0:T(8,128)(2,1)}, bf16[64,...) custom-call(s32[12]{0:T(128)} %lens_ref.3, ...), custom_call_target="tpu_custom_call" | custom-call | flops 1610612736 | bytes 3145728 | tf_op jit(solution)/shard_map/conv_core/pallas_call | solution.py:355
  69.7 1.6 %collective-permute-start.11 = (bf16[64,1024]{1,0:T(8,128)(2,1)}, bf16[64,1024]{1,0:T(8,128)(2,1)S(1)}, u32[]{:S(2)}, u32[]{:S(2)}) collective-permute-start(bf16[64,1024]{1,0:T(8,128)(2,1)} %get-tuple-element.74), channel_id=1, source_target_pairs={{0,2},{1,3},{2,0},{3,1},{4,6},{5,7},{6,4},{7,5},{8,10},{9,11},{10,... | collective-permute-start | bytes 393224 | tf_op jit(solution)/shard_map/ppermute | solution.py:536
  71.3 4.7 %collective-permute-done.11.refs_2_ = bf16[64,1024]{1,0:T(8,128)(2,1)S(1)} collective-permute-done((bf16[64,1024]{1,0:T(8,128)(2,1)}, bf16[64,1024]{1,0:T(8,128)(2,1)S(1)}, u32[]{:S(2)}, u32[]{:S(2)}) %collective-permute-start.11) | collective-permute-done | bytes 131104 | tf_op jit(solution)/shard_map/ppermute | solution.py:536
  76.0 1.9 %collective-permute-start.16 = (f32[64,128]{1,0:T(8,128)}, f32[64,128]{1,0:T(8,128)S(1)}, u32[]{:S(2)}, u32[]{:S(2)}) collective-permute-start(f32[64,128]{1,0:T(8,128)} %get-tuple-element.84), channel_id=1, source_target_pairs={{0,8},{1,9},{2,10},{3,11},{4,12},{5,13},{6,14},{7,15},{8,0},{9,1},... | collective-permute-start | bytes 98312 | tf_op jit(solution)/shard_map/ppermute | solution.py:536
  77.9 2.3 %collective-permute-done.16 = f32[64,128]{1,0:T(8,128)S(1)} collective-permute-done((f32[64,128]{1,0:T(8,128)}, f32[64,128]{1,0:T(8,128)S(1)}, u32[]{:S(2)}, u32[]{:S(2)}) %collective-permute-start.16) | collective-permute-done | bytes 32800 | tf_op jit(solution)/shard_map/ppermute | solution.py:536
  81.0 3.8 %collective-permute-start.17 = (f32[64,128]{1,0:T(8,128)S(1)}, f32[64,128]{1,0:T(8,128)S(1)}, u32[]{:S(2)}, u32[]{:S(2)}) collective-permute-start(f32[64,128]{1,0:T(8,128)S(1)} %add.10), channel_id=1, source_target_pairs={{0,16},{1,17},{2,18},{3,19},{4,20},{5,21},{6,22},{7,23},{8,24},{9,... | collective-permute-start | bytes 98312 | tf_op jit(solution)/shard_map/ppermute | solution.py:536
  84.8 1.9 %collective-permute-done.17 = f32[64,128]{1,0:T(8,128)S(1)} collective-permute-done((f32[64,128]{1,0:T(8,128)S(1)}, f32[64,128]{1,0:T(8,128)S(1)}, u32[]{:S(2)}, u32[]{:S(2)}) %collective-permute-start.17) | collective-permute-done | bytes 32800 | tf_op jit(solution)/shard_map/ppermute | solution.py:536
  88.1 1.5 %collective-permute-start.12 = (bf16[64,1024]{1,0:T(8,128)(2,1)}, bf16[64,1024]{1,0:T(8,128)(2,1)S(1)}, u32[]{:S(2)}, u32[]{:S(2)}) collective-permute-start(bf16[64,1024]{1,0:T(8,128)(2,1)} %get-tuple-element.76), channel_id=1, source_target_pairs={{0,3},{1,2},{2,1},{3,0},{4,7},{5,6},{6,5},{7,4},{8,11},{9,10},{10,... | collective-permute-start | bytes 393224 | tf_op jit(solution)/shard_map/ppermute | solution.py:536
  95.7 4.5 %collective-permute-done.14.refs_5_ = bf16[64,1024]{1,0:T(8,128)(2,1)S(1)} collective-permute-done((bf16[64,1024]{1,0:T(8,128)(2,1)}, bf16[64,1024]{1,0:T(8,128)(2,1)S(1)}, u32[]{:S(2)}, u32[]{:S(2)}) %collective-permute-start.14) | collective-permute-done | bytes 131104 | tf_op jit(solution)/shard_map/ppermute | solution.py:536
  100.3 3.3 %conv_unpack.1 = (bf16[32,8192]{1,0:T(8,128)(2,1)}, bf16[32,8192]{1,0:T(8,128)(2,1)}, bf16[32,8192]{1,0:T(8,128)(2,1)}) custom-call(bf16[32,8192]{1,0:T(8,128)(2,1)S(1)} %copy-done, bf16[32,8192]{1,0:T(8,128)(2,1)S(1)} %copy-done.1, bf16[32,8192]{1,0:T(8,128)(2,1)S(1)} %copy-done.2, bf16[64,1024]{1,0:T(8,128)(2,1)S(1)} %copy-done.4, ...), custom_call_target="tpu_custom_call" | custom-call | flops 1572864 | bytes 4194304 | tf_op jit(solution)/shard_map/conv_unpack/pallas_call | solution.py:391
  (71 shorter events, 13.7 us)
Async XLA Ops:
  4.5 37.1 %all-to-all-start = ((bf16[32,144,128]{2,1,0:T(8,128)(2,1)}), bf16[32,144,128]{2,1,0:T(8,128)(2,1)S(1)}, u32[]{:S(2)}, u32[]{:S(2)}) async-start(bf16[32,144,128]{2,1,0:T(8,128)(2,1)} %attn_pack.1), calls=%async_computation | async-start | bytes 2359296 | tf_op jit(solution)/shard_map/all_to_all | solution.py:556
  13.4 3.7 %collective-permute-start = (bf16[64,1024]{1,0:T(8,128)(2,1)S(1)}, bf16[64,1024]{1,0:T(8,128)(2,1)S(1)}, u32[]{:S(2)}, u32[]{:S(2)}) collective-permute-start(bf16[64,1024]{1,0:T(8,128)(2,1)S(1)} %get-tuple-element.47), channel_id=1, source_target_pairs={{0,1},{1,0},{2,3},{3,2},{4,5},{5,4},{6,7},{7,6},{8,9},{9,8},{10,11... | collective-permute-start | bytes 393224 | tf_op jit(solution)/shard_map/ppermute | solution.py:536
  13.7 13.0 %collective-permute-start.1 = (bf16[64,1024]{1,0:T(8,128)(2,1)S(1)}, bf16[64,1024]{1,0:T(8,128)(2,1)S(1)}, u32[]{:S(2)}, u32[]{:S(2)}) collective-permute-start(bf16[64,1024]{1,0:T(8,128)(2,1)S(1)} %get-tuple-element.48), channel_id=1, source_target_pairs={{0,2},{1,3},{2,0},{3,1},{4,6},{5,7},{6,4},{7,5},{8,10},{9,11},{10,... | collective-permute-start | bytes 393224 | tf_op jit(solution)/shard_map/ppermute | solution.py:536
  15.4 14.7 %collective-permute-start.2 = (bf16[64,1024]{1,0:T(8,128)(2,1)S(1)}, bf16[64,1024]{1,0:T(8,128)(2,1)S(1)}, u32[]{:S(2)}, u32[]{:S(2)}) collective-permute-start(bf16[64,1024]{1,0:T(8,128)(2,1)S(1)} %get-tuple-element.49), channel_id=1, source_target_pairs={{0,3},{1,2},{2,1},{3,0},{4,7},{5,6},{6,5},{7,4},{8,11},{9,10},{10,... | collective-permute-start | bytes 393224 | tf_op jit(solution)/shard_map/ppermute | solution.py:536
  15.4 14.7 %collective-permute-start.3 = (bf16[64,1024]{1,0:T(8,128)(2,1)S(1)}, bf16[64,1024]{1,0:T(8,128)(2,1)S(1)}, u32[]{:S(2)}, u32[]{:S(2)}) collective-permute-start(bf16[64,1024]{1,0:T(8,128)(2,1)S(1)} %get-tuple-element.50), channel_id=1, source_target_pairs={{0,4},{1,5},{2,6},{3,7},{4,0},{5,1},{6,2},{7,3},{8,12},{9,13},{10,... | collective-permute-start | bytes 393224 | tf_op jit(solution)/shard_map/ppermute | solution.py:536
  17.1 13.1 %collective-permute-start.4 = (bf16[64,1024]{1,0:T(8,128)(2,1)S(1)}, bf16[64,1024]{1,0:T(8,128)(2,1)S(1)}, u32[]{:S(2)}, u32[]{:S(2)}) collective-permute-start(bf16[64,1024]{1,0:T(8,128)(2,1)S(1)} %get-tuple-element.51), channel_id=1, source_target_pairs={{0,5},{1,4},{2,7},{3,6},{4,1},{5,0},{6,3},{7,2},{8,13},{9,12},{10,... | collective-permute-start | bytes 393224 | tf_op jit(solution)/shard_map/ppermute | solution.py:536
  17.2 22.2 %copy-start.8 = (bf16[64,1024]{1,0:T(8,128)(2,1)}, bf16[64,1024]{1,0:T(8,128)(2,1)S(1)}, u32[]{:S(2)}) copy-start(bf16[64,1024]{1,0:T(8,128)(2,1)S(1)} %collective-permute-done.refs_1_) | copy-start | bytes 393220
  17.2 18.4 %collective-permute-start.5 = (bf16[64,1024]{1,0:T(8,128)(2,1)S(1)}, bf16[64,1024]{1,0:T(8,128)(2,1)S(1)}, u32[]{:S(2)}, u32[]{:S(2)}) collective-permute-start(bf16[64,1024]{1,0:T(8,128)(2,1)S(1)} %get-tuple-element.52), channel_id=1, source_target_pairs={{0,6},{1,7},{2,4},{3,5},{4,2},{5,3},{6,0},{7,1},{8,14},{9,15},{10,... | collective-permute-start | bytes 393224 | tf_op jit(solution)/shard_map/ppermute | solution.py:536
  26.7 12.7 %copy-start.9 = (bf16[64,1024]{1,0:T(8,128)(2,1)}, bf16[64,1024]{1,0:T(8,128)(2,1)S(1)}, u32[]{:S(2)}) copy-start(bf16[64,1024]{1,0:T(8,128)(2,1)S(1)} %collective-permute-done.1.refs_2_) | copy-start | bytes 393220
  26.7 12.1 %collective-permute-start.6 = (bf16[64,1024]{1,0:T(8,128)(2,1)S(1)}, bf16[64,1024]{1,0:T(8,128)(2,1)S(1)}, u32[]{:S(2)}, u32[]{:S(2)}) collective-permute-start(bf16[64,1024]{1,0:T(8,128)(2,1)S(1)} %get-tuple-element.53), channel_id=1, source_target_pairs={{0,7},{1,6},{2,5},{3,4},{4,3},{5,2},{6,1},{7,0},{8,15},{9,14},{10,... | collective-permute-start | bytes 393224 | tf_op jit(solution)/shard_map/ppermute | solution.py:536
  41.7 10.6 %collective-permute-start.7 = (bf16[128,1024]{1,0:T(8,128)(2,1)}, bf16[128,1024]{1,0:T(8,128)(2,1)S(1)}, u32[]{:S(2)}, u32[]{:S(2)}) collective-permute-start(bf16[128,1024]{1,0:T(8,128)(2,1)} %get-tuple-element.57.m1_ref), channel_id=1, source_target_pairs={{0,8},{1,9},{2,10},{3,11},{4,12},{5,13},{6,14},{7,15},{8,16},{9,17... | collective-permute-start | bytes 786440 | tf_op jit(solution)/shard_map/ppermute | solution.py:532
  44.8 10.9 %collective-permute-start.8 = (bf16[128,1024]{1,0:T(8,128)(2,1)}, bf16[128,1024]{1,0:T(8,128)(2,1)S(1)}, u32[]{:S(2)}, u32[]{:S(2)}) collective-permute-start(bf16[128,1024]{1,0:T(8,128)(2,1)} %get-tuple-element.58.g0_ref), channel_id=1, source_target_pairs={{8,0},{9,1},{10,2},{11,3},{12,4},{13,5},{14,6},{15,7},{16,8},{17,9... | collective-permute-start | bytes 786440 | tf_op jit(solution)/shard_map/ppermute | solution.py:532
  55.7 38.0 %all-to-all-start.1 = ((bf16[32,96,128]{2,1,0:T(8,128)(2,1)}), bf16[32,96,128]{2,1,0:T(8,128)(2,1)S(1)}, u32[]{:S(2)}, u32[]{:S(2)}) async-start(bf16[32,96,128]{2,1,0:T(8,128)(2,1)} %attn_head.1), calls=%async_computation.1 | async-start | bytes 1572864 | tf_op jit(solution)/shard_map/all_to_all | solution.py:571
  69.7 30.6 %copy-start.4 = (bf16[64,1024]{1,0:T(8,128)(2,1)S(1)}, bf16[64,1024]{1,0:T(8,128)(2,1)}, u32[]{:S(2)}) copy-start(bf16[64,1024]{1,0:T(8,128)(2,1)} %get-tuple-element.71.refs_0_) | copy-start | bytes 393220
  69.7 6.3 %collective-permute-start.11 = (bf16[64,1024]{1,0:T(8,128)(2,1)}, bf16[64,1024]{1,0:T(8,128)(2,1)S(1)}, u32[]{:S(2)}, u32[]{:S(2)}) collective-permute-start(bf16[64,1024]{1,0:T(8,128)(2,1)} %get-tuple-element.74), channel_id=1, source_target_pairs={{0,2},{1,3},{2,0},{3,1},{4,6},{5,7},{6,4},{7,5},{8,10},{9,11},{10,... | collective-permute-start | bytes 393224 | tf_op jit(solution)/shard_map/ppermute | solution.py:536
  76.0 4.2 %collective-permute-start.16 = (f32[64,128]{1,0:T(8,128)}, f32[64,128]{1,0:T(8,128)S(1)}, u32[]{:S(2)}, u32[]{:S(2)}) collective-permute-start(f32[64,128]{1,0:T(8,128)} %get-tuple-element.84), channel_id=1, source_target_pairs={{0,8},{1,9},{2,10},{3,11},{4,12},{5,13},{6,14},{7,15},{8,0},{9,1},... | collective-permute-start | bytes 98312 | tf_op jit(solution)/shard_map/ppermute | solution.py:536
  81.0 5.7 %collective-permute-start.17 = (f32[64,128]{1,0:T(8,128)S(1)}, f32[64,128]{1,0:T(8,128)S(1)}, u32[]{:S(2)}, u32[]{:S(2)}) collective-permute-start(f32[64,128]{1,0:T(8,128)S(1)} %add.10), channel_id=1, source_target_pairs={{0,16},{1,17},{2,18},{3,19},{4,20},{5,21},{6,22},{7,23},{8,24},{9,... | collective-permute-start | bytes 98312 | tf_op jit(solution)/shard_map/ppermute | solution.py:536
  84.8 6.7 %collective-permute-start.9 = (bf16[64,1024]{1,0:T(8,128)(2,1)}, bf16[64,1024]{1,0:T(8,128)(2,1)S(1)}, u32[]{:S(2)}, u32[]{:S(2)}) collective-permute-start(bf16[64,1024]{1,0:T(8,128)(2,1)} %get-tuple-element.67), channel_id=1, source_target_pairs={{0,7},{1,6},{2,5},{3,4},{4,3},{5,2},{6,1},{7,0},{8,15},{9,14},{10,... | collective-permute-start | bytes 393224 | tf_op jit(solution)/shard_map/ppermute | solution.py:536
  86.9 5.1 %collective-permute-start.18 = (f32[64,128]{1,0:T(8,128)S(1)}, f32[64,128]{1,0:T(8,128)S(1)}, u32[]{:S(2)}, u32[]{:S(2)}) collective-permute-start(f32[64,128]{1,0:T(8,128)S(1)} %pad_maximum_fusion.1), channel_id=1, source_target_pairs={{0,4},{1,5},{2,6},{3,7},{4,0},{5,1},{6,2},{7,3},{8,12},{9,13},{10,... | collective-permute-start | bytes 98312 | tf_op jit(solution)/shard_map/ppermute | solution.py:536
  88.1 7.1 %collective-permute-start.10 = (bf16[64,1024]{1,0:T(8,128)(2,1)}, bf16[64,1024]{1,0:T(8,128)(2,1)S(1)}, u32[]{:S(2)}, u32[]{:S(2)}) collective-permute-start(bf16[64,1024]{1,0:T(8,128)(2,1)} %get-tuple-element.72), channel_id=1, source_target_pairs={{0,1},{1,0},{2,3},{3,2},{4,5},{5,4},{6,7},{7,6},{8,9},{9,8},{10,11... | collective-permute-start | bytes 393224 | tf_op jit(solution)/shard_map/ppermute | solution.py:536
  88.1 7.1 %collective-permute-start.12 = (bf16[64,1024]{1,0:T(8,128)(2,1)}, bf16[64,1024]{1,0:T(8,128)(2,1)S(1)}, u32[]{:S(2)}, u32[]{:S(2)}) collective-permute-start(bf16[64,1024]{1,0:T(8,128)(2,1)} %get-tuple-element.76), channel_id=1, source_target_pairs={{0,3},{1,2},{2,1},{3,0},{4,7},{5,6},{6,5},{7,4},{8,11},{9,10},{10,... | collective-permute-start | bytes 393224 | tf_op jit(solution)/shard_map/ppermute | solution.py:536
  89.6 6.2 %collective-permute-start.13 = (bf16[64,1024]{1,0:T(8,128)(2,1)}, bf16[64,1024]{1,0:T(8,128)(2,1)S(1)}, u32[]{:S(2)}, u32[]{:S(2)}) collective-permute-start(bf16[64,1024]{1,0:T(8,128)(2,1)} %get-tuple-element.77), channel_id=1, source_target_pairs={{0,4},{1,5},{2,6},{3,7},{4,0},{5,1},{6,2},{7,3},{8,12},{9,13},{10,... | collective-permute-start | bytes 393224 | tf_op jit(solution)/shard_map/ppermute | solution.py:536
  91.4 8.8 %collective-permute-start.14 = (bf16[64,1024]{1,0:T(8,128)(2,1)}, bf16[64,1024]{1,0:T(8,128)(2,1)S(1)}, u32[]{:S(2)}, u32[]{:S(2)}) collective-permute-start(bf16[64,1024]{1,0:T(8,128)(2,1)} %get-tuple-element.78), channel_id=1, source_target_pairs={{0,5},{1,4},{2,7},{3,6},{4,1},{5,0},{6,3},{7,2},{8,13},{9,12},{10,... | collective-permute-start | bytes 393224 | tf_op jit(solution)/shard_map/ppermute | solution.py:536
  92.0 8.2 %collective-permute-start.15 = (bf16[64,1024]{1,0:T(8,128)(2,1)}, bf16[64,1024]{1,0:T(8,128)(2,1)S(1)}, u32[]{:S(2)}, u32[]{:S(2)}) collective-permute-start(bf16[64,1024]{1,0:T(8,128)(2,1)} %get-tuple-element.79), channel_id=1, source_target_pairs={{0,6},{1,7},{2,4},{3,5},{4,2},{5,3},{6,0},{7,1},{8,14},{9,15},{10,... | collective-permute-start | bytes 393224 | tf_op jit(solution)/shard_map/ppermute | solution.py:536
  (15 other events, 87.1 us)

commit v3 on v2

--- a/solution.py
+++ b/solution.py
@@ -12,8 +12,7 @@
 GROUP = 16
 FILTER_LEN = 128
 LANES = 128
-STEP = 1024
-UNROLL = True
+EACH = 2
 BAND_REACH = 320
 DEVICES = ("seq", "ch")
 NEG_FILL = -1e30
@@ -150,7 +149,7 @@
 def attn_pack(q, k, v, o, g):
     rows, features = q.shape
     heads = features // HEAD_DIM
-    step = math.gcd(heads, 8)
+    step = math.gcd(heads, 16)
     spec = pl.BlockSpec((rows, step * HEAD_DIM), lambda j: (0, j))
     height = 4 * rows + 16
     return pl.pallas_call(
@@ -230,7 +229,7 @@
             pltpu.VMEM((tokens, HEAD_DIM), F32),
             pltpu.VMEM((tokens, HEAD_DIM), F32),
         ],
-        cost_estimate=cost(20 * tokens * 512 * HEAD_DIM, 4 * x.size),
+        cost_estimate=cost(tokens, x.size),
         name="attn_head",
     )(lens, x)
 
@@ -245,7 +244,7 @@
 
 def attn_unpack(x, rows):
     heads = x.shape[0]
-    step = math.gcd(heads, 8)
+    step = math.gcd(heads, 16)
     spec = pl.BlockSpec((rows, step * HEAD_DIM), lambda j: (0, j))
     shape = jax.ShapeDtypeStruct((rows, heads * HEAD_DIM), BF16)
     return pl.pallas_call(
@@ -277,51 +276,49 @@
     return jnp.sum(folded, axis=0, keepdims=True)
 
 
+def reached(lens_ref, out_pos, in_pos):
+    gap = out_pos - in_pos
+    near = (gap >= 0) & (gap < FILTER_LEN) & (in_pos >= doc_start(lens_ref, out_pos))
+    return near.astype(F32).astype(BF16)
+
+
+def window_positions(inner, span):
+    base = (lax.axis_index("seq") // inner) * span
+    shape = (LANES, 2 * LANES)
+    return (
+        base + lax.broadcasted_iota(jnp.int32, shape, 0),
+        base + lax.broadcasted_iota(jnp.int32, shape, 1),
+    )
+
+
 def conv_core_kernel(
     rows, inner, ch_count, lens_ref, tap_ref, rev_ref, prior_ref, m0_ref, m1_ref, g0_ref, g1_ref,
     later_ref, *refs,
 ):
     members = inner * ch_count
-    outs, filt_ref = refs[:members], refs[members]
-    back_ref, front_ref, conv_ref, down_ref = refs[members + 1 :]
+    outs = refs[:members]
+    conv_ref, down_ref = refs[members:]
     me = member_index(ch_count, inner)
     groups = LANES // GROUP
     blocks = 2
-
-    @pl.when(pl.program_id(0) == 0)
-    def _():
-        base = (lax.axis_index("seq") // inner) * (members * rows)
-        shape = (LANES, 2 * LANES)
-        down = lax.broadcasted_iota(jnp.int32, shape, 0)
-        across = lax.broadcasted_iota(jnp.int32, shape, 1)
-
-        def reached(out_pos, in_pos):
-            gap = out_pos - in_pos
-            near = (gap >= 0) & (gap < FILTER_LEN) & (in_pos >= doc_start(lens_ref, out_pos))
-            return near.astype(F32).astype(BF16)
-
-        for b in range(blocks):
-            first = base + b * LANES
-            back_ref[b] = reached(first + down, first - LANES + across)
-            front_ref[b] = reached(first + across, first + down)
-
-    def one_tile(tile, carried):
-        cols = pl.ds(pl.multiple_of(tile * LANES, LANES), LANES)
+    down, across = window_positions(inner, members * rows)
+    back = [reached(lens_ref, down + b * LANES, across + (b - 1) * LANES) for b in range(blocks)]
+    front = [reached(lens_ref, across + b * LANES, down + b * LANES) for b in range(blocks)]
+
+    for tile in range(m0_ref.shape[1] // LANES):
+        cols = slice(tile * LANES, (tile + 1) * LANES)
         mixed = [r[:, cols] for r in (prior_ref, m0_ref, m1_ref)]
         grad = [r[:, cols] for r in (g0_ref, g1_ref, later_ref)]
         lane_group = lax.broadcasted_iota(jnp.int32, (LANES, LANES), 1) // GROUP
-        tap_rows = pl.ds(pl.multiple_of(tile * groups, groups), groups)
+        tap_rows = slice(tile * groups, (tile + 1) * groups)
         taps, rev_taps = tap_ref[tap_rows, :], rev_ref[tap_rows, :]
         back_taps = [circulant(rev_taps[g : g + 1]) for g in range(groups)]
         front_taps = [circulant(taps[g : g + 1]) for g in range(groups)]
-        outer = [jnp.zeros((LANES, LANES), F32)] * groups
         for b in range(blocks):
-            back, front = back_ref[b], front_ref[b]
-            back32 = back.astype(F32)
             window = jnp.concatenate(mixed[b : b + 2], axis=0)
             ahead = jnp.concatenate(grad[b : b + 2], axis=0)
-            conv_all = dot(jnp.concatenate([t * back for t in back_taps], axis=0), window, NN)
-            down_all = dot(jnp.concatenate([t * front for t in front_taps], axis=0), ahead, NN)
+            conv_all = dot(jnp.concatenate([t * back[b] for t in back_taps], axis=0), window, NN)
+            down_all = dot(jnp.concatenate([t * front[b] for t in front_taps], axis=0), ahead, NN)
             conv_out = jnp.zeros((LANES, LANES), F32)
             mixed_grad = jnp.zeros((LANES, LANES), F32)
             for g in range(groups):
@@ -329,16 +326,9 @@
                 span = slice(g * LANES, (g + 1) * LANES)
                 conv_out = jnp.where(mine, conv_all[span], conv_out)
                 mixed_grad = jnp.where(mine, down_all[span], mixed_grad)
-                chosen = grad[b] * mine.astype(F32).astype(BF16)
-                full = dot(chosen, window, NT) * back32
-                outer[g] = outer[g] + full[:, 0:LANES] + full[:, LANES:]
             here = slice(b * LANES, (b + 1) * LANES)
             conv_ref[here, cols] = conv_out.astype(BF16)
             down_ref[here, cols] = mixed_grad.astype(BF16)
-        filt_ref[tap_rows, :] = jnp.concatenate([unskewed(o) for o in outer], axis=0)
-        return carried
-
-    lax.fori_loop(0, m0_ref.shape[1] // LANES, one_tile, 0, unroll=UNROLL)
     for k, out_ref in enumerate(outs):
         at = pl.multiple_of(jnp.bitwise_xor(me, k) * rows, rows)
         out_ref[0:rows, :] = conv_ref[pl.ds(at, rows), :]
@@ -348,54 +338,91 @@
 def conv_core(lens, taps, rev_taps, arrays, rows, inner, ch_count):
     members = inner * ch_count
     width = arrays[0].shape[1]
-    step = min(width, STEP)
-    spec = pl.BlockSpec((LANES, step), lambda j: (0, j))
-    piece = pl.BlockSpec((2 * rows, step), lambda j: (0, j))
-    tap_spec = pl.BlockSpec((step // GROUP, FILTER_LEN), lambda j: (j, 0))
+    vmem = pl.BlockSpec(memory_space=pltpu.VMEM)
     return pl.pallas_call(
         functools.partial(conv_core_kernel, rows, inner, ch_count),
-        grid=(width // step,),
-        in_specs=[pl.BlockSpec(memory_space=pltpu.SMEM), tap_spec, tap_spec] + [spec] * 6,
-        out_specs=[piece] * members + [tap_spec],
-        out_shape=[jax.ShapeDtypeStruct((2 * rows, width), BF16)] * members
-        + [jax.ShapeDtypeStruct((width // GROUP, FILTER_LEN), F32)],
-        scratch_shapes=[pltpu.VMEM((2, LANES, 2 * LANES), BF16)] * 2
-        + [pltpu.VMEM((2 * LANES, step), BF16)] * 2,
-        cost_estimate=cost(96 * LANES * LANES * width, 24 * LANES * width),
+        in_specs=[pl.BlockSpec(memory_space=pltpu.SMEM)] + [vmem] * 8,
+        out_specs=[vmem] * members,
+        out_shape=[jax.ShapeDtypeStruct((2 * rows, width), BF16)] * members,
+        scratch_shapes=[pltpu.VMEM((2 * LANES, width), BF16)] * 2,
+        cost_estimate=cost(2000 * LANES * LANES * width, 24 * LANES * width),
         name="conv_core",
     )(lens, taps, rev_taps, *arrays)
 
 
-def conv_unpack_kernel(inner, ch_count, ck_ref, cv_ref, cg_ref, *refs):
+def conv_filter_kernel(
+    rows, inner, ch_count, lens_ref, prior_ref, m0_ref, m1_ref, g0_ref, g1_ref, filt_ref
+):
+    groups = LANES // GROUP
+    blocks = 2
+    down, across = window_positions(inner, inner * ch_count * rows)
+    back = [
+        reached(lens_ref, down + b * LANES, across + (b - 1) * LANES).astype(F32)
+        for b in range(blocks)
+    ]
+    for tile in range(m0_ref.shape[1] // LANES):
+        cols = slice(tile * LANES, (tile + 1) * LANES)
+        mixed = [r[:, cols] for r in (prior_ref, m0_ref, m1_ref)]
+        grad = [r[:, cols] for r in (g0_ref, g1_ref)]
+        lane_group = lax.broadcasted_iota(jnp.int32, (LANES, LANES), 1) // GROUP
+        sums = []
+        for g in range(groups):
+            mine = (lane_group == g).astype(F32).astype(BF16)
+            outer = jnp.zeros((LANES, LANES), F32)
+            for b in range(blocks):
+                window = jnp.concatenate(mixed[b : b + 2], axis=0)
+                full = dot(grad[b] * mine, window, NT) * back[b]
+                outer = outer + full[:, 0:LANES] + full[:, LANES:]
+            sums.append(unskewed(outer))
+        filt_ref[tile * groups : (tile + 1) * groups, :] = jnp.concatenate(sums, axis=0)
+
+
+def conv_filter_grad(lens, arrays, rows, inner, ch_count):
+    width = arrays[0].shape[1]
+    vmem = pl.BlockSpec(memory_space=pltpu.VMEM)
+    return pl.pallas_call(
+        functools.partial(conv_filter_kernel, rows, inner, ch_count),
+        in_specs=[pl.BlockSpec(memory_space=pltpu.SMEM)] + [vmem] * 5,
+        out_specs=vmem,
+        out_shape=jax.ShapeDtypeStruct((width // GROUP, FILTER_LEN), F32),
+        cost_estimate=cost(32 * LANES * LANES * width, 10 * LANES * width),
+        name="conv_filter_grad",
+    )(lens, *arrays)
+
+
+def conv_unpack_kernel(inner, ch_count, each, ck_ref, cv_ref, cg_ref, *refs):
     members = inner * ch_count
     pieces, (gq_ref, gk_ref, gv_ref) = refs[:members], refs[members:]
-    rows = ck_ref.shape[0]
-    piece = chunk_piece(pl.program_id(0), ch_count, inner)
-    for k, x_ref in enumerate(pieces):
-
-        @pl.when(piece == k)
-        def _():
-            conv_out = x_ref[0:rows, :].astype(F32)
-            mixed_grad = x_ref[rows : 2 * rows, :].astype(F32)
-            gq_ref[...] = (cg_ref[...].astype(F32) * conv_out).astype(BF16)
-            gk_ref[...] = (mixed_grad * cv_ref[...].astype(F32)).astype(BF16)
-            gv_ref[...] = (mixed_grad * ck_ref[...].astype(F32)).astype(BF16)
+    rows, width = pieces[0].shape[0] // 2, pieces[0].shape[1]
+    for part in range(each):
+        piece = chunk_piece(pl.program_id(0) * each + part, ch_count, inner)
+        cols = slice(part * width, (part + 1) * width)
+        for k, x_ref in enumerate(pieces):
+
+            @pl.when(piece == k)
+            def _():
+                conv_out = x_ref[0:rows, :].astype(F32)
+                mixed_grad = x_ref[rows : 2 * rows, :].astype(F32)
+                gq_ref[:, cols] = (cg_ref[:, cols].astype(F32) * conv_out).astype(BF16)
+                gk_ref[:, cols] = (mixed_grad * cv_ref[:, cols].astype(F32)).astype(BF16)
+                gv_ref[:, cols] = (mixed_grad * ck_ref[:, cols].astype(F32)).astype(BF16)
 
 
 def conv_unpack(pieces, ck, cv, cg, inner, ch_count):
     rows, channels = ck.shape
     members = inner * ch_count
-    width = channels // members
+    each = EACH
+    width = each * channels // members
     spec = pl.BlockSpec((rows, width), lambda k: (0, k))
     shape = jax.ShapeDtypeStruct((rows, channels), BF16)
     return pl.pallas_call(
-        functools.partial(conv_unpack_kernel, inner, ch_count),
-        grid=(members,),
-        in_specs=[spec] * 3 + [pl.BlockSpec((2 * rows, width), lambda k: (0, 0))] * members,
+        functools.partial(conv_unpack_kernel, inner, ch_count, each),
+        grid=(members // each,),
+        in_specs=[spec] * 3 + [pl.BlockSpec(pieces[0].shape, lambda k: (0, 0))] * members,
         out_specs=[spec] * 3,
         out_shape=[shape] * 3,
+        compiler_params=params(),
         cost_estimate=cost(6 * rows * channels, 16 * rows * channels),
-        compiler_params=params(),
         name="conv_unpack",
     )(ck, cv, cg, *pieces)
 
@@ -557,44 +584,50 @@
 
     packed = conv_pack(conv_query, conv_key, conv_value, conv_grad_out, inner, ch_count)
     pieces = [packed[0]] + [exchanged(packed[k], k, count) for k in range(1, members)]
+    group_count = channels // members // GROUP
+    y = lax.rem(lax.axis_index("seq"), inner)
+    taps = lax.dynamic_slice_in_dim(conv_filter, y * group_count, group_count, 0).astype(F32)
+    rev_taps = jnp.roll(taps[:, ::-1], 1, axis=1)
+    taps, rev_taps, *pieces = lax.optimization_barrier((taps, rev_taps, *pieces))
     mixed_lo, mixed_hi, grad_lo, grad_hi = conv_join(pieces, rows, inner, ch_count)
     if head_each:
         attn_in, mixed_hi, grad_lo = lax.optimization_barrier((attn_in, mixed_hi, grad_lo))
     prior, later = shifted(mixed_hi, members, count), shifted(grad_lo, -members, count)
-    group_count = channels // members // GROUP
-    y = lax.rem(lax.axis_index("seq"), inner)
-    taps = lax.dynamic_slice_in_dim(conv_filter, y * group_count, group_count, 0).astype(F32)
-    rev_taps = jnp.roll(taps[:, ::-1], 1, axis=1)
     if head_each:
         attn_back = attn_head(doc_lengths, attn_in, rows, reach)
-        attn_back, prior, later = lax.optimization_barrier((attn_back, prior, later))
+        attn_back, taps, rev_taps = lax.optimization_barrier((attn_back, taps, rev_taps))
         attn_res = lax.all_to_all(attn_back, DEVICES, split_axis=0, concat_axis=0, tiled=True)
     own = (prior, mixed_lo, mixed_hi, grad_lo, grad_hi, later)
-    *conv_back, filter_part = conv_core(
-        doc_lengths, taps, rev_taps, own, rows, inner, ch_count
-    )
+    filter_part = conv_filter_grad(doc_lengths, own[:5], rows, inner, ch_count)
+    other = exchanged(filter_part, members, count)
+    taps, filter_part = lax.optimization_barrier((taps, filter_part))
+    conv_back = conv_core(doc_lengths, taps, rev_taps, own, rows, inner, ch_count)
+    other, *conv_back = lax.optimization_barrier((other, *conv_back))
     conv_res = [conv_back[0]] + [exchanged(conv_back[k], k, count) for k in range(1, members)]
-
-    filter_part, conv_res[2] = lax.optimization_barrier((filter_part, conv_res[2]))
-    distance = members
+    filter_part = filter_part + other
+    filter_part, conv_res[1:4] = lax.optimization_barrier((filter_part, conv_res[1:4]))
+    distance = 2 * members
     while distance < count:
-        filter_part = filter_part + exchanged(filter_part, distance, count)
+        other = exchanged(filter_part, distance, count)
+        conv_res, other = lax.optimization_barrier((conv_res, other))
+        filter_part = filter_part + other
         distance *= 2
     filter_part = jnp.roll(filter_part[:, ::-1], 1, axis=1)
     other = exchanged(filter_part, ch_count, count)
+    grad_conv = conv_unpack(conv_res, conv_key, conv_value, conv_grad_out, inner, ch_count)
+    if head_each:
+        grad_attn = attn_unpack(attn_res, rows)
+        other, *grad_attn = lax.optimization_barrier((other, *grad_attn))
+    else:
+        grad_attn = attn_gathered(
+            attn_query, attn_key, attn_value, attn_output, attn_grad_out, doc_lengths
+        )
+    other, *grad_conv = lax.optimization_barrier((other, *grad_conv))
     grad_filter = jnp.where(
         y == 0,
         jnp.concatenate([filter_part, other], axis=0),
         jnp.concatenate([other, filter_part], axis=0),
     )
-    if head_each:
-        grad_attn = attn_unpack(attn_res, rows)
-        *grad_attn, conv_res[-1] = lax.optimization_barrier((*grad_attn, conv_res[-1]))
-    else:
-        grad_attn = attn_gathered(
-            attn_query, attn_key, attn_value, attn_output, attn_grad_out, doc_lengths
-        )
-    grad_conv = conv_unpack(conv_res, conv_key, conv_value, conv_grad_out, inner, ch_count)
     return (*grad_attn, *grad_conv, grad_filter)
 
 

time: 104 us -> 95.5 us (0.918)
  waiting for transfers between devices: 37.9 us -> 24.2 us
  starting transfers between devices: 33.5 us -> 38.3 us
  local copies, waits for them, and re-layouts: 1.66 us -> 3.26 us
    ppermute x17, waiting for transfers between devices: 34.4 us -> 24.2 us  [exchanged(): lax.ppermute(block, DEVICES, [(i, i ^ distance) for i in range(count)])]
    pallas_call x1 -> x2, Pallas kernels: 3.35 us -> 6.85 us  [the longest x1 4.65 us: conv_filter_grad(): pl.pallas_call(functools.partial(conv_filter_kernel, rows, inner, ch_coun...]
    ppermute x2, waiting for transfers between devices: 3.45 us -> 0.01 us  [shifted(): return lax.ppermute(block, DEVICES, route)]
    all_to_all x1, starting transfers between devices: 3.58 us -> 6.33 us  [body(): lax.all_to_all(attn_back, DEVICES, split_axis=0, concat_axis=0, tiled=True)]
    pallas_call x1, Pallas kernels: 9.45 us -> 7.23 us  [conv_core(): pl.pallas_call(functools.partial(conv_core_kernel, rows, inner, ch_count)...]
    ppermute x17, starting transfers between devices: 18.3 us -> 20.2 us  [exchanged(): lax.ppermute(block, DEVICES, [(i, i ^ distance) for i in range(count)])]
    unnamed x36, local copies, waits for them, and re-layouts: 1.36 us -> 2.96 us
    pallas_call x1, Pallas kernels: 3.88 us -> 2.6 us  [attn_pack(): pl.pallas_call(functools.partial(attn_pack_kernel, rows), grid=(heads //...]
  transfers between devices with their start and end apart: 21 -> 21, of which waited for: 12 -> 8; matrix products, arithmetic and copies ran while one was open for 2% -> 1% of each run, Pallas kernels for 20% -> 26%
where the time goes in v3:
time: 95.5 us; the launch traced here: 95 us
  starting transfers between devices  38.3 us (40%)
  Pallas kernels  26.9 us (28%)
  waiting for transfers between devices  24.2 us (25%)
  local copies, waits for them, and re-layouts  3.26 us (3%)
  other arithmetic  1.51 us (2%)
    ppermute x17, waiting for transfers between devices, exchanged(): lax.ppermute(block, DEVICES, [(i, i ^ distance) for i in range(count)])  24.2 us
    ppermute x17, starting transfers between devices, exchanged(): lax.ppermute(block, DEVICES, [(i, i ^ distance) for i in range(count)])  20.2 us
    all_to_all x1, starting transfers between devices, body(): lax.all_to_all(attn_packed, DEVICES, split_axis=0, concat_axis=0, tiled=T...  7.42 us
    pallas_call x1, Pallas kernels, conv_core(): pl.pallas_call(functools.partial(conv_core_kernel, rows, inner, ch_count)...  7.23 us
    all_to_all x1, starting transfers between devices, body(): lax.all_to_all(attn_back, DEVICES, split_axis=0, concat_axis=0, tiled=True)  6.33 us
    pallas_call x1, Pallas kernels, attn_head(): pl.pallas_call(functools.partial(attn_kernel, rows, reach), in_specs=[pl....  6.18 us
    pallas_call x1, Pallas kernels, conv_filter_grad(): pl.pallas_call(functools.partial(conv_filter_kernel, rows, inner, ch_coun...  4.65 us
    ppermute x2, starting transfers between devices, shifted(): return lax.ppermute(block, DEVICES, route)  4.37 us
  transfers between devices with their start and end apart: 21, of which 8 were waited for; matrix products, arithmetic and copies ran while one was open for 1% of the time, Pallas kernels for 26%

profile of v3, /device:TPU:0, one launch (start us, length us, event | category | flops | bytes accessed | tf_op | source)
XLA Modules:
  0.0 95.0 jit_solution(5129748420649398072)
XLA Ops:
  0.6 2.6 %attn_pack.1 = bf16[32,144,128]{2,1,0:T(8,128)(2,1)} custom-call(bf16[32,4096]{1,0:T(8,128)(2,1)} %q_ref.1, bf16[32,4096]{1,0:T(8,128)(2,1)} %k_ref.1, bf16[32,4096]{1,0:T(8,128)(2,1)} %v_ref.1, bf16[32,4096]{1,0:T(8,128)(2,1)} %o_ref.1, bf16[32,4096]{1,0:T(8,128)(2,1)} %g_ref.1), custom_call_target="tpu_custom_call" | custom-call | flops 524288 | bytes 2621440 | tf_op jit(solution)/shard_map/attn_pack/pallas_call | solution.py:155
  3.3 7.4 %all-to-all-start = ((bf16[32,144,128]{2,1,0:T(8,128)(2,1)}), bf16[32,144,128]{2,1,0:T(8,128)(2,1)}, u32[]{:S(2)}, u32[]{:S(2)}) async-start(bf16[32,144,128]{2,1,0:T(8,128)(2,1)} %attn_pack.1), calls=%async_computation | async-start | bytes 2359296 | tf_op jit(solution)/shard_map/all_to_all | solution.py:583
  11.9 1.7 %collective-permute-start.1 = (bf16[64,1024]{1,0:T(8,128)(2,1)S(1)}, bf16[64,1024]{1,0:T(8,128)(2,1)S(1)}, u32[]{:S(2)}, u32[]{:S(2)}) collective-permute-start(bf16[64,1024]{1,0:T(8,128)(2,1)S(1)} %get-tuple-element.83), channel_id=1, source_target_pairs={{0,2},{1,3},{2,0},{3,1},{4,6},{5,7},{6,4},{7,5},{8,10},{9,11},{10,... | collective-permute-start | bytes 393224 | tf_op jit(solution)/shard_map/ppermute | solution.py:563
  13.6 1.7 %collective-permute-start.3 = (bf16[64,1024]{1,0:T(8,128)(2,1)S(1)}, bf16[64,1024]{1,0:T(8,128)(2,1)S(1)}, u32[]{:S(2)}, u32[]{:S(2)}) collective-permute-start(bf16[64,1024]{1,0:T(8,128)(2,1)S(1)} %get-tuple-element.85), channel_id=1, source_target_pairs={{0,4},{1,5},{2,6},{3,7},{4,0},{5,1},{6,2},{7,3},{8,12},{9,13},{10,... | collective-permute-start | bytes 393224 | tf_op jit(solution)/shard_map/ppermute | solution.py:563
  15.4 2.6 %collective-permute-start.5 = (bf16[64,1024]{1,0:T(8,128)(2,1)S(1)}, bf16[64,1024]{1,0:T(8,128)(2,1)S(1)}, u32[]{:S(2)}, u32[]{:S(2)}) collective-permute-start(bf16[64,1024]{1,0:T(8,128)(2,1)S(1)} %get-tuple-element.87), channel_id=1, source_target_pairs={{0,6},{1,7},{2,4},{3,5},{4,2},{5,3},{6,0},{7,1},{8,14},{9,15},{10,... | collective-permute-start | bytes 393224 | tf_op jit(solution)/shard_map/ppermute | solution.py:563
  18.0 7.4 %collective-permute-done.1.refs_2_ = bf16[64,1024]{1,0:T(8,128)(2,1)S(1)} collective-permute-done((bf16[64,1024]{1,0:T(8,128)(2,1)S(1)}, bf16[64,1024]{1,0:T(8,128)(2,1)S(1)}, u32[]{:S(2)}, u32[]{:S(2)}) %collective-permute-start.1) | collective-permute-done | bytes 131104 | tf_op jit(solution)/shard_map/ppermute | solution.py:563
  27.0 1.9 %collective-permute-done.2.refs_3_ = bf16[64,1024]{1,0:T(8,128)(2,1)S(1)} collective-permute-done((bf16[64,1024]{1,0:T(8,128)(2,1)S(1)}, bf16[64,1024]{1,0:T(8,128)(2,1)S(1)}, u32[]{:S(2)}, u32[]{:S(2)}) %collective-permute-start.2) | collective-permute-done | bytes 131104 | tf_op jit(solution)/shard_map/ppermute | solution.py:563
  28.9 5.5 %collective-permute-done.5.refs_6_ = bf16[64,1024]{1,0:T(8,128)(2,1)S(1)} collective-permute-done((bf16[64,1024]{1,0:T(8,128)(2,1)S(1)}, bf16[64,1024]{1,0:T(8,128)(2,1)S(1)}, u32[]{:S(2)}, u32[]{:S(2)}) %collective-permute-start.5) | collective-permute-done | bytes 131104 | tf_op jit(solution)/shard_map/ppermute | solution.py:563
  34.3 3.2 %collective-permute-done.6.refs_7_ = bf16[64,1024]{1,0:T(8,128)(2,1)S(1)} collective-permute-done((bf16[64,1024]{1,0:T(8,128)(2,1)S(1)}, bf16[64,1024]{1,0:T(8,128)(2,1)S(1)}, u32[]{:S(2)}, u32[]{:S(2)}) %collective-permute-start.6) | collective-permute-done | bytes 131104 | tf_op jit(solution)/shard_map/ppermute | solution.py:563
  38.1 2.2 %conv_join.1 = (bf16[128,1024]{1,0:T(8,128)(2,1)}, bf16[128,1024]{1,0:T(8,128)(2,1)}, bf16[128,1024]{1,0:T(8,128)(2,1)}, bf16[128,1024]{1,0:T(8,128)(2,1)}) custom-call(bf16[64,1024]{1,0:T(8,128)(2,1)} %copy-done.5, bf16[64,1024]{1,0:T(8,128)(2,1)} %copy-done.7, bf16[64,1024]{1,0:T(8,128)(2,1)} %copy-done.8, bf16[64,1024]{1,0:T(8,128)(2,1)} %copy-done.9, ...), custom_call_target="tpu_custom_call" | custom-call | bytes 2097152 | tf_op jit(solution)/shard_map/conv_join/pallas_call | solution.py:113
  40.4 3.1 %collective-permute-start.7 = (bf16[128,1024]{1,0:T(8,128)(2,1)}, bf16[128,1024]{1,0:T(8,128)(2,1)S(1)}, u32[]{:S(2)}, u32[]{:S(2)}) collective-permute-start(bf16[128,1024]{1,0:T(8,128)(2,1)} %get-tuple-element.103.m1_ref), channel_id=1, source_target_pairs={{0,8},{1,9},{2,10},{3,11},{4,12},{5,13},{6,14},{7,15},{8,16},{9,17... | collective-permute-start | bytes 786440 | tf_op jit(solution)/shard_map/ppermute | solution.py:559
  43.4 1.3 %collective-permute-start.9 = (bf16[128,1024]{1,0:T(8,128)(2,1)}, bf16[128,1024]{1,0:T(8,128)(2,1)S(1)}, u32[]{:S(2)}, u32[]{:S(2)}) collective-permute-start(bf16[128,1024]{1,0:T(8,128)(2,1)} %get-tuple-element.105.g0_ref), channel_id=1, source_target_pairs={{8,0},{9,1},{10,2},{11,3},{12,4},{13,5},{14,6},{15,7},{16,8},{17,9... | collective-permute-start | bytes 786440 | tf_op jit(solution)/shard_map/ppermute | solution.py:559
  44.7 6.2 %attn_head.1 = bf16[32,96,128]{2,1,0:T(8,128)(2,1)} custom-call(s32[12]{0:T(128)} %lens_ref.5, bf16[32,144,128]{2,1,0:T(8,128)(2,1)} %all-to-all-done.x_ref), custom_call_target="tpu_custom_call" | custom-call | flops 1024 | bytes 589824 | tf_op jit(solution)/shard_map/attn_head/pallas_call | solution.py:220
  50.9 6.3 %all-to-all-start.1 = ((bf16[32,96,128]{2,1,0:T(8,128)(2,1)}), bf16[32,96,128]{2,1,0:T(8,128)(2,1)S(1)}, u32[]{:S(2)}, u32[]{:S(2)}) async-start(bf16[32,96,128]{2,1,0:T(8,128)(2,1)} %attn_head.1), calls=%async_computation.1 | async-start | bytes 1572864 | tf_op jit(solution)/shard_map/all_to_all | solution.py:599
  58.0 4.6 %conv_filter_grad.1 = f32[64,128]{1,0:T(8,128)} custom-call(s32[12]{0:T(128)} %lens_ref.5, bf16[128,1024]{1,0:T(8,128)(2,1)} %copy-done.16, bf16[128,1024]{1,0:T(8,128)(2,1)} %get-tuple-element.104.m0_ref, bf16[128,1024]{1,0:T(8,128)(2,1)} %get-tuple-element.103.m1_ref, bf16[128,1024]{1,0:T(8,128)(2,1)} %get-tuple-element.105.g0_ref, ...), custom_call_target="tpu_custom_call" | custom-call | flops 536870912 | bytes 1310720 | tf_op jit(solution)/shard_map/conv_filter_grad/pallas_call | solution.py:383
  62.6 1.6 %collective-permute-start.8 = (f32[64,128]{1,0:T(8,128)}, f32[64,128]{1,0:T(8,128)S(1)}, u32[]{:S(2)}, u32[]{:S(2)}) collective-permute-start(f32[64,128]{1,0:T(8,128)} %conv_filter_grad.1), channel_id=1, source_target_pairs={{0,8},{1,9},{2,10},{3,11},{4,12},{5,13},{6,14},{7,15},{8,0},{9,1},... | collective-permute-start | bytes 98312 | tf_op jit(solution)/shard_map/ppermute | solution.py:563
  64.9 7.2 %conv_core.1 = (bf16[64,1024]{1,0:T(8,128)(2,1)}, bf16[64,1024]{1,0:T(8,128)(2,1)}, bf16[64,1024]{1,0:T(8,128)(2,1)}, bf16[64,1024]{1,0:T(8,128)(2,1)}, bf16[64,...) custom-call(s32[12]{0:T(128)} %lens_ref.5, ...), custom_call_target="tpu_custom_call" | custom-call | flops 33554432000 | bytes 3145728 | tf_op jit(solution)/shard_map/conv_core/pallas_call | solution.py:342
  72.3 1.5 %collective-permute-start.11 = (bf16[64,1024]{1,0:T(8,128)(2,1)}, bf16[64,1024]{1,0:T(8,128)(2,1)S(1)}, u32[]{:S(2)}, u32[]{:S(2)}) collective-permute-start(bf16[64,1024]{1,0:T(8,128)(2,1)} %get-tuple-element.120), channel_id=1, source_target_pairs={{0,2},{1,3},{2,0},{3,1},{4,6},{5,7},{6,4},{7,5},{8,10},{9,11},{10,... | collective-permute-start | bytes 393224 | tf_op jit(solution)/shard_map/ppermute | solution.py:563
  74.1 1.5 %collective-permute-start.13 = (bf16[64,1024]{1,0:T(8,128)(2,1)}, bf16[64,1024]{1,0:T(8,128)(2,1)S(1)}, u32[]{:S(2)}, u32[]{:S(2)}) collective-permute-start(bf16[64,1024]{1,0:T(8,128)(2,1)} %get-tuple-element.127), channel_id=1, source_target_pairs={{0,4},{1,5},{2,6},{3,7},{4,0},{5,1},{6,2},{7,3},{8,12},{9,13},{10,... | collective-permute-start | bytes 393224 | tf_op jit(solution)/shard_map/ppermute | solution.py:563
  75.8 2.4 %collective-permute-start.15 = (bf16[64,1024]{1,0:T(8,128)(2,1)}, bf16[64,1024]{1,0:T(8,128)(2,1)S(1)}, u32[]{:S(2)}, u32[]{:S(2)}) collective-permute-start(bf16[64,1024]{1,0:T(8,128)(2,1)} %get-tuple-element.129), channel_id=1, source_target_pairs={{0,6},{1,7},{2,4},{3,5},{4,2},{5,3},{6,0},{7,1},{8,14},{9,15},{10,... | collective-permute-start | bytes 393224 | tf_op jit(solution)/shard_map/ppermute | solution.py:563
  81.8 2.5 %collective-permute-start.17 = (f32[64,128]{1,0:T(8,128)S(1)}, f32[64,128]{1,0:T(8,128)S(1)}, u32[]{:S(2)}, u32[]{:S(2)}) collective-permute-start(f32[64,128]{1,0:T(8,128)S(1)} %add.10), channel_id=1, source_target_pairs={{0,16},{1,17},{2,18},{3,19},{4,20},{5,21},{6,22},{7,23},{8,24},{9,... | collective-permute-start | bytes 98312 | tf_op jit(solution)/shard_map/ppermute | solution.py:563
  84.3 3.6 %collective-permute-done.14.refs_5_ = bf16[64,1024]{1,0:T(8,128)(2,1)S(1)} collective-permute-done((bf16[64,1024]{1,0:T(8,128)(2,1)}, bf16[64,1024]{1,0:T(8,128)(2,1)S(1)}, u32[]{:S(2)}, u32[]{:S(2)}) %collective-permute-start.14) | collective-permute-done | bytes 131104 | tf_op jit(solution)/shard_map/ppermute | solution.py:563
  88.4 1.9 %collective-permute-start.18 = (f32[64,128]{1,0:T(8,128)S(1)}, f32[64,128]{1,0:T(8,128)S(1)}, u32[]{:S(2)}, u32[]{:S(2)}) collective-permute-start(f32[64,128]{1,0:T(8,128)S(1)} %pad_maximum_fusion.1), channel_id=1, source_target_pairs={{0,4},{1,5},{2,6},{3,7},{4,0},{5,1},{6,2},{7,3},{8,12},{9,13},{10,... | collective-permute-start | bytes 98312 | tf_op jit(solution)/shard_map/ppermute | solution.py:563
  91.1 2.2 %conv_unpack.1 = (bf16[32,8192]{1,0:T(8,128)(2,1)}, bf16[32,8192]{1,0:T(8,128)(2,1)}, bf16[32,8192]{1,0:T(8,128)(2,1)}) custom-call(bf16[32,8192]{1,0:T(8,128)(2,1)S(1)} %copy-done, bf16[32,8192]{1,0:T(8,128)(2,1)S(1)} %copy-done.1, bf16[32,8192]{1,0:T(8,128)(2,1)S(1)} %copy-done.2, bf16[64,1024]{1,0:T(8,128)(2,1)S(1)} %copy-done.4, ...), custom_call_target="tpu_custom_call" | custom-call | flops 1572864 | bytes 4194304 | tf_op jit(solution)/shard_map/conv_unpack/pallas_call | solution.py:418
  (72 shorter events, 12.2 us)
Async XLA Ops:
  3.3 37.1 %all-to-all-start = ((bf16[32,144,128]{2,1,0:T(8,128)(2,1)}), bf16[32,144,128]{2,1,0:T(8,128)(2,1)}, u32[]{:S(2)}, u32[]{:S(2)}) async-start(bf16[32,144,128]{2,1,0:T(8,128)(2,1)} %attn_pack.1), calls=%async_computation | async-start | bytes 2359296 | tf_op jit(solution)/shard_map/all_to_all | solution.py:583
  11.6 25.9 %copy-start.5 = (bf16[64,1024]{1,0:T(8,128)(2,1)}, bf16[64,1024]{1,0:T(8,128)(2,1)S(1)}, u32[]{:S(2)}) copy-start(bf16[64,1024]{1,0:T(8,128)(2,1)S(1)} %get-tuple-element.89.refs_0_) | copy-start | bytes 393220
  11.6 3.7 %collective-permute-start = (bf16[64,1024]{1,0:T(8,128)(2,1)S(1)}, bf16[64,1024]{1,0:T(8,128)(2,1)S(1)}, u32[]{:S(2)}, u32[]{:S(2)}) collective-permute-start(bf16[64,1024]{1,0:T(8,128)(2,1)S(1)} %get-tuple-element.82), channel_id=1, source_target_pairs={{0,1},{1,0},{2,3},{3,2},{4,5},{5,4},{6,7},{7,6},{8,9},{9,8},{10,11... | collective-permute-start | bytes 393224 | tf_op jit(solution)/shard_map/ppermute | solution.py:563
  11.9 13.5 %collective-permute-start.1 = (bf16[64,1024]{1,0:T(8,128)(2,1)S(1)}, bf16[64,1024]{1,0:T(8,128)(2,1)S(1)}, u32[]{:S(2)}, u32[]{:S(2)}) collective-permute-start(bf16[64,1024]{1,0:T(8,128)(2,1)S(1)} %get-tuple-element.83), channel_id=1, source_target_pairs={{0,2},{1,3},{2,0},{3,1},{4,6},{5,7},{6,4},{7,5},{8,10},{9,11},{10,... | collective-permute-start | bytes 393224 | tf_op jit(solution)/shard_map/ppermute | solution.py:563
  13.6 15.3 %collective-permute-start.2 = (bf16[64,1024]{1,0:T(8,128)(2,1)S(1)}, bf16[64,1024]{1,0:T(8,128)(2,1)S(1)}, u32[]{:S(2)}, u32[]{:S(2)}) collective-permute-start(bf16[64,1024]{1,0:T(8,128)(2,1)S(1)} %get-tuple-element.84), channel_id=1, source_target_pairs={{0,3},{1,2},{2,1},{3,0},{4,7},{5,6},{6,5},{7,4},{8,11},{9,10},{10,... | collective-permute-start | bytes 393224 | tf_op jit(solution)/shard_map/ppermute | solution.py:563
  13.6 15.3 %collective-permute-start.3 = (bf16[64,1024]{1,0:T(8,128)(2,1)S(1)}, bf16[64,1024]{1,0:T(8,128)(2,1)S(1)}, u32[]{:S(2)}, u32[]{:S(2)}) collective-permute-start(bf16[64,1024]{1,0:T(8,128)(2,1)S(1)} %get-tuple-element.85), channel_id=1, source_target_pairs={{0,4},{1,5},{2,6},{3,7},{4,0},{5,1},{6,2},{7,3},{8,12},{9,13},{10,... | collective-permute-start | bytes 393224 | tf_op jit(solution)/shard_map/ppermute | solution.py:563
  15.3 13.6 %collective-permute-start.4 = (bf16[64,1024]{1,0:T(8,128)(2,1)S(1)}, bf16[64,1024]{1,0:T(8,128)(2,1)S(1)}, u32[]{:S(2)}, u32[]{:S(2)}) collective-permute-start(bf16[64,1024]{1,0:T(8,128)(2,1)S(1)} %get-tuple-element.86), channel_id=1, source_target_pairs={{0,5},{1,4},{2,7},{3,6},{4,1},{5,0},{6,3},{7,2},{8,13},{9,12},{10,... | collective-permute-start | bytes 393224 | tf_op jit(solution)/shard_map/ppermute | solution.py:563
  15.4 22.1 %copy-start.7 = (bf16[64,1024]{1,0:T(8,128)(2,1)}, bf16[64,1024]{1,0:T(8,128)(2,1)S(1)}, u32[]{:S(2)}) copy-start(bf16[64,1024]{1,0:T(8,128)(2,1)S(1)} %collective-permute-done.refs_1_) | copy-start | bytes 393220
  15.4 18.9 %collective-permute-start.5 = (bf16[64,1024]{1,0:T(8,128)(2,1)S(1)}, bf16[64,1024]{1,0:T(8,128)(2,1)S(1)}, u32[]{:S(2)}, u32[]{:S(2)}) collective-permute-start(bf16[64,1024]{1,0:T(8,128)(2,1)S(1)} %get-tuple-element.87), channel_id=1, source_target_pairs={{0,6},{1,7},{2,4},{3,5},{4,2},{5,3},{6,0},{7,1},{8,14},{9,15},{10,... | collective-permute-start | bytes 393224 | tf_op jit(solution)/shard_map/ppermute | solution.py:563
  25.4 12.1 %collective-permute-start.6 = (bf16[64,1024]{1,0:T(8,128)(2,1)S(1)}, bf16[64,1024]{1,0:T(8,128)(2,1)S(1)}, u32[]{:S(2)}, u32[]{:S(2)}) collective-permute-start(bf16[64,1024]{1,0:T(8,128)(2,1)S(1)} %get-tuple-element.88), channel_id=1, source_target_pairs={{0,7},{1,6},{2,5},{3,4},{4,3},{5,2},{6,1},{7,0},{8,15},{9,14},{10,... | collective-permute-start | bytes 393224 | tf_op jit(solution)/shard_map/ppermute | solution.py:563
  26.1 24.8 %copy-start.6 = (f32[64,128]{1,0:T(8,128)}, f32[64,128]{1,0:T(8,128)S(1)}, u32[]{:S(2)}) copy-start(f32[64,128]{1,0:T(8,128)S(1)} %dynamic-slice_convert_fusion.tap_ref) | copy-start | bytes 98308
  40.4 16.9 %collective-permute-start.7 = (bf16[128,1024]{1,0:T(8,128)(2,1)}, bf16[128,1024]{1,0:T(8,128)(2,1)S(1)}, u32[]{:S(2)}, u32[]{:S(2)}) collective-permute-start(bf16[128,1024]{1,0:T(8,128)(2,1)} %get-tuple-element.103.m1_ref), channel_id=1, source_target_pairs={{0,8},{1,9},{2,10},{3,11},{4,12},{5,13},{6,14},{7,15},{8,16},{9,17... | collective-permute-start | bytes 786440 | tf_op jit(solution)/shard_map/ppermute | solution.py:559
  43.4 20.8 %collective-permute-start.9 = (bf16[128,1024]{1,0:T(8,128)(2,1)}, bf16[128,1024]{1,0:T(8,128)(2,1)S(1)}, u32[]{:S(2)}, u32[]{:S(2)}) collective-permute-start(bf16[128,1024]{1,0:T(8,128)(2,1)} %get-tuple-element.105.g0_ref), channel_id=1, source_target_pairs={{8,0},{9,1},{10,2},{11,3},{12,4},{13,5},{14,6},{15,7},{16,8},{17,9... | collective-permute-start | bytes 786440 | tf_op jit(solution)/shard_map/ppermute | solution.py:559
  50.9 42.4 %all-to-all-start.1 = ((bf16[32,96,128]{2,1,0:T(8,128)(2,1)}), bf16[32,96,128]{2,1,0:T(8,128)(2,1)S(1)}, u32[]{:S(2)}, u32[]{:S(2)}) async-start(bf16[32,96,128]{2,1,0:T(8,128)(2,1)} %attn_head.1), calls=%async_computation.1 | async-start | bytes 1572864 | tf_op jit(solution)/shard_map/all_to_all | solution.py:599
  62.6 9.5 %collective-permute-start.8 = (f32[64,128]{1,0:T(8,128)}, f32[64,128]{1,0:T(8,128)S(1)}, u32[]{:S(2)}, u32[]{:S(2)}) collective-permute-start(f32[64,128]{1,0:T(8,128)} %conv_filter_grad.1), channel_id=1, source_target_pairs={{0,8},{1,9},{2,10},{3,11},{4,12},{5,13},{6,14},{7,15},{8,0},{9,1},... | collective-permute-start | bytes 98312 | tf_op jit(solution)/shard_map/ppermute | solution.py:563
  72.2 3.6 %collective-permute-start.10 = (bf16[64,1024]{1,0:T(8,128)(2,1)}, bf16[64,1024]{1,0:T(8,128)(2,1)S(1)}, u32[]{:S(2)}, u32[]{:S(2)}) collective-permute-start(bf16[64,1024]{1,0:T(8,128)(2,1)} %get-tuple-element.119), channel_id=1, source_target_pairs={{0,1},{1,0},{2,3},{3,2},{4,5},{5,4},{6,7},{7,6},{8,9},{9,8},{10,11... | collective-permute-start | bytes 393224 | tf_op jit(solution)/shard_map/ppermute | solution.py:563
  72.3 7.2 %collective-permute-start.11 = (bf16[64,1024]{1,0:T(8,128)(2,1)}, bf16[64,1024]{1,0:T(8,128)(2,1)S(1)}, u32[]{:S(2)}, u32[]{:S(2)}) collective-permute-start(bf16[64,1024]{1,0:T(8,128)(2,1)} %get-tuple-element.120), channel_id=1, source_target_pairs={{0,2},{1,3},{2,0},{3,1},{4,6},{5,7},{6,4},{7,5},{8,10},{9,11},{10,... | collective-permute-start | bytes 393224 | tf_op jit(solution)/shard_map/ppermute | solution.py:563
  73.8 8.0 %collective-permute-start.12 = (bf16[64,1024]{1,0:T(8,128)(2,1)}, bf16[64,1024]{1,0:T(8,128)(2,1)S(1)}, u32[]{:S(2)}, u32[]{:S(2)}) collective-permute-start(bf16[64,1024]{1,0:T(8,128)(2,1)} %get-tuple-element.121), channel_id=1, source_target_pairs={{0,3},{1,2},{2,1},{3,0},{4,7},{5,6},{6,5},{7,4},{8,11},{9,10},{10,... | collective-permute-start | bytes 393224 | tf_op jit(solution)/shard_map/ppermute | solution.py:563
  74.1 10.1 %collective-permute-start.13 = (bf16[64,1024]{1,0:T(8,128)(2,1)}, bf16[64,1024]{1,0:T(8,128)(2,1)S(1)}, u32[]{:S(2)}, u32[]{:S(2)}) collective-permute-start(bf16[64,1024]{1,0:T(8,128)(2,1)} %get-tuple-element.127), channel_id=1, source_target_pairs={{0,4},{1,5},{2,6},{3,7},{4,0},{5,1},{6,2},{7,3},{8,12},{9,13},{10,... | collective-permute-start | bytes 393224 | tf_op jit(solution)/shard_map/ppermute | solution.py:563
  75.6 12.3 %collective-permute-start.14 = (bf16[64,1024]{1,0:T(8,128)(2,1)}, bf16[64,1024]{1,0:T(8,128)(2,1)S(1)}, u32[]{:S(2)}, u32[]{:S(2)}) collective-permute-start(bf16[64,1024]{1,0:T(8,128)(2,1)} %get-tuple-element.128), channel_id=1, source_target_pairs={{0,5},{1,4},{2,7},{3,6},{4,1},{5,0},{6,3},{7,2},{8,13},{9,12},{10,... | collective-permute-start | bytes 393224 | tf_op jit(solution)/shard_map/ppermute | solution.py:563
  75.8 12.1 %collective-permute-start.15 = (bf16[64,1024]{1,0:T(8,128)(2,1)}, bf16[64,1024]{1,0:T(8,128)(2,1)S(1)}, u32[]{:S(2)}, u32[]{:S(2)}) collective-permute-start(bf16[64,1024]{1,0:T(8,128)(2,1)} %get-tuple-element.129), channel_id=1, source_target_pairs={{0,6},{1,7},{2,4},{3,5},{4,2},{5,3},{6,0},{7,1},{8,14},{9,15},{10,... | collective-permute-start | bytes 393224 | tf_op jit(solution)/shard_map/ppermute | solution.py:563
  79.4 8.7 %collective-permute-start.16 = (bf16[64,1024]{1,0:T(8,128)(2,1)}, bf16[64,1024]{1,0:T(8,128)(2,1)S(1)}, u32[]{:S(2)}, u32[]{:S(2)}) collective-permute-start(bf16[64,1024]{1,0:T(8,128)(2,1)} %get-tuple-element.130), channel_id=1, source_target_pairs={{0,7},{1,6},{2,5},{3,4},{4,3},{5,2},{6,1},{7,0},{8,15},{9,14},{10,... | collective-permute-start | bytes 393224 | tf_op jit(solution)/shard_map/ppermute | solution.py:563
  81.8 6.4 %collective-permute-start.17 = (f32[64,128]{1,0:T(8,128)S(1)}, f32[64,128]{1,0:T(8,128)S(1)}, u32[]{:S(2)}, u32[]{:S(2)}) collective-permute-start(f32[64,128]{1,0:T(8,128)S(1)} %add.10), channel_id=1, source_target_pairs={{0,16},{1,17},{2,18},{3,19},{4,20},{5,21},{6,22},{7,23},{8,24},{9,... | collective-permute-start | bytes 98312 | tf_op jit(solution)/shard_map/ppermute | solution.py:563
  88.4 5.9 %collective-permute-start.18 = (f32[64,128]{1,0:T(8,128)S(1)}, f32[64,128]{1,0:T(8,128)S(1)}, u32[]{:S(2)}, u32[]{:S(2)}) collective-permute-start(f32[64,128]{1,0:T(8,128)S(1)} %pad_maximum_fusion.1), channel_id=1, source_target_pairs={{0,4},{1,5},{2,6},{3,7},{4,0},{5,1},{6,2},{7,3},{8,12},{9,13},{10,... | collective-permute-start | bytes 98312 | tf_op jit(solution)/shard_map/ppermute | solution.py:563
  (15 other events, 107.4 us)

commit v4 on v3

--- a/solution.py
+++ b/solution.py
@@ -230,33 +230,44 @@
             pltpu.VMEM((tokens, HEAD_DIM), F32),
         ],
         cost_estimate=cost(tokens, x.size),
+        compiler_params=pltpu.CompilerParams(vmem_limit_bytes=40 * 1024 * 1024),
         name="attn_head",
     )(lens, x)
 
 
-def attn_unpack_kernel(rows, x_ref, dq_ref, dk_ref, dv_ref):
+def attn_unpack_kernel(rows, inner, x_ref, mine_ref, other_ref, dq_ref, dk_ref, dv_ref, filt_ref):
     for h in range(x_ref.shape[0]):
         cols = slice(h * HEAD_DIM, (h + 1) * HEAD_DIM)
         dq_ref[:, cols] = x_ref[h, 0:rows, :]
         dk_ref[:, cols] = x_ref[h, rows : 2 * rows, :]
         dv_ref[:, cols] = x_ref[h, 2 * rows : 3 * rows, :]
 
-
-def attn_unpack(x, rows):
+    @pl.when(pl.program_id(0) == 0)
+    def _():
+        groups = mine_ref.shape[0]
+        at = lax.rem(lax.axis_index("seq"), inner) * groups
+        filt_ref[pl.ds(pl.multiple_of(at, groups), groups), :] = mine_ref[...]
+        at = groups - at
+        filt_ref[pl.ds(pl.multiple_of(at, groups), groups), :] = other_ref[...]
+
+
+def attn_unpack(x, mine, other, rows, inner):
     heads = x.shape[0]
     step = math.gcd(heads, 16)
     spec = pl.BlockSpec((rows, step * HEAD_DIM), lambda j: (0, j))
+    half = pl.BlockSpec(mine.shape, lambda j: (0, 0))
+    whole = (2 * mine.shape[0], mine.shape[1])
     shape = jax.ShapeDtypeStruct((rows, heads * HEAD_DIM), BF16)
     return pl.pallas_call(
-        functools.partial(attn_unpack_kernel, rows),
+        functools.partial(attn_unpack_kernel, rows, inner),
         grid=(heads // step,),
-        in_specs=[pl.BlockSpec((step, 3 * rows, HEAD_DIM), lambda j: (j, 0, 0))],
-        out_specs=[spec] * 3,
-        out_shape=[shape] * 3,
+        in_specs=[pl.BlockSpec((step, 3 * rows, HEAD_DIM), lambda j: (j, 0, 0)), half, half],
+        out_specs=[spec] * 3 + [pl.BlockSpec(whole, lambda j: (0, 0))],
+        out_shape=[shape] * 3 + [jax.ShapeDtypeStruct(whole, F32)],
+        compiler_params=params(),
         cost_estimate=cost(0, 4 * x.size),
-        compiler_params=params(),
         name="attn_unpack",
-    )(x)
+    )(x, mine, other)
 
 
 def circulant(row):
@@ -346,6 +357,7 @@
         out_shape=[jax.ShapeDtypeStruct((2 * rows, width), BF16)] * members,
         scratch_shapes=[pltpu.VMEM((2 * LANES, width), BF16)] * 2,
         cost_estimate=cost(2000 * LANES * LANES * width, 24 * LANES * width),
+        compiler_params=pltpu.CompilerParams(vmem_limit_bytes=40 * 1024 * 1024),
         name="conv_core",
     )(lens, taps, rev_taps, *arrays)
 
@@ -386,6 +398,7 @@
         out_specs=vmem,
         out_shape=jax.ShapeDtypeStruct((width // GROUP, FILTER_LEN), F32),
         cost_estimate=cost(32 * LANES * LANES * width, 10 * LANES * width),
+        compiler_params=pltpu.CompilerParams(vmem_limit_bytes=40 * 1024 * 1024),
         name="conv_filter_grad",
     )(lens, *arrays)
 
@@ -602,10 +615,11 @@
     other = exchanged(filter_part, members, count)
     taps, filter_part = lax.optimization_barrier((taps, filter_part))
     conv_back = conv_core(doc_lengths, taps, rev_taps, own, rows, inner, ch_count)
-    other, *conv_back = lax.optimization_barrier((other, *conv_back))
     conv_res = [conv_back[0]] + [exchanged(conv_back[k], k, count) for k in range(1, members)]
+    filter_part, other, conv_res[1:4] = lax.optimization_barrier(
+        (filter_part, other, conv_res[1:4])
+    )
     filter_part = filter_part + other
-    filter_part, conv_res[1:4] = lax.optimization_barrier((filter_part, conv_res[1:4]))
     distance = 2 * members
     while distance < count:
         other = exchanged(filter_part, distance, count)
@@ -615,19 +629,18 @@
     filter_part = jnp.roll(filter_part[:, ::-1], 1, axis=1)
     other = exchanged(filter_part, ch_count, count)
     grad_conv = conv_unpack(conv_res, conv_key, conv_value, conv_grad_out, inner, ch_count)
+    other, *grad_conv = lax.optimization_barrier((other, *grad_conv))
     if head_each:
-        grad_attn = attn_unpack(attn_res, rows)
-        other, *grad_attn = lax.optimization_barrier((other, *grad_attn))
+        *grad_attn, grad_filter = attn_unpack(attn_res, filter_part, other, rows, inner)
     else:
         grad_attn = attn_gathered(
             attn_query, attn_key, attn_value, attn_output, attn_grad_out, doc_lengths
         )
-    other, *grad_conv = lax.optimization_barrier((other, *grad_conv))
-    grad_filter = jnp.where(
-        y == 0,
-        jnp.concatenate([filter_part, other], axis=0),
-        jnp.concatenate([other, filter_part], axis=0),
-    )
+        grad_filter = jnp.where(
+            y == 0,
+            jnp.concatenate([filter_part, other], axis=0),
+            jnp.concatenate([other, filter_part], axis=0),
+        )
     return (*grad_attn, *grad_conv, grad_filter)
 
 

time: 95.5 us -> 92 us (0.963)
  Pallas kernels: 26.9 us -> 25.1 us
  local copies, waits for them, and re-layouts: 3.26 us -> 1.94 us
    unnamed x36 -> x26, local copies, waits for them, and re-layouts: 2.96 us -> 1.64 us
    pallas_call x1, Pallas kernels: 7.23 us -> 5.97 us  [conv_core(): pl.pallas_call(functools.partial(conv_core_kernel, rows, inner, ch_count)...]
  transfers between devices with their start and end apart: 21 -> 21, of which waited for: 8 -> 9; matrix products, arithmetic and copies ran while one was open for 1% -> 1% of each run, Pallas kernels for 26% -> 23%
where the time goes in v4:
time: 92 us; the launch traced here: 91.5 us
  starting transfers between devices  38.1 us (41%)
  Pallas kernels  25.1 us (27%)
  waiting for transfers between devices  24.5 us (27%)
  local copies, waits for them, and re-layouts  1.94 us (2%)
  between operations  0.97 us (1%)
    ppermute x17, waiting for transfers between devices, exchanged(): lax.ppermute(block, DEVICES, [(i, i ^ distance) for i in range(count)])  24.5 us
    ppermute x17, starting transfers between devices, exchanged(): lax.ppermute(block, DEVICES, [(i, i ^ distance) for i in range(count)])  19.4 us
    all_to_all x1, starting transfers between devices, body(): lax.all_to_all(attn_packed, DEVICES, split_axis=0, concat_axis=0, tiled=T...  7.3 us
    all_to_all x1, starting transfers between devices, body(): lax.all_to_all(attn_back, DEVICES, split_axis=0, concat_axis=0, tiled=True)  6.31 us
    pallas_call x1, Pallas kernels, conv_core(): pl.pallas_call(functools.partial(conv_core_kernel, rows, inner, ch_count)...  5.97 us
    pallas_call x1, Pallas kernels, attn_head(): pl.pallas_call(functools.partial(attn_kernel, rows, reach), in_specs=[pl....  5.51 us
    ppermute x2, starting transfers between devices, shifted(): return lax.ppermute(block, DEVICES, route)  5.06 us
    pallas_call x1, Pallas kernels, conv_filter_grad(): pl.pallas_call(functools.partial(conv_filter_kernel, rows, inner, ch_coun...  3.78 us
  transfers between devices with their start and end apart: 21, of which 9 were waited for; matrix products, arithmetic and copies ran while one was open for 1% of the time, Pallas kernels for 23%

profile of v4, /device:TPU:0, one launch (start us, length us, event | category | flops | bytes accessed | tf_op | source)
XLA Modules:
  0.0 91.5 jit_solution(14716926136075860696)
XLA Ops:
  0.6 2.6 %attn_pack.1 = bf16[32,144,128]{2,1,0:T(8,128)(2,1)} custom-call(bf16[32,4096]{1,0:T(8,128)(2,1)} %q_ref.1, bf16[32,4096]{1,0:T(8,128)(2,1)} %k_ref.1, bf16[32,4096]{1,0:T(8,128)(2,1)} %v_ref.1, bf16[32,4096]{1,0:T(8,128)(2,1)} %o_ref.1, bf16[32,4096]{1,0:T(8,128)(2,1)} %g_ref.1), custom_call_target="tpu_custom_call" | custom-call | flops 524288 | bytes 2621440 | tf_op jit(solution)/shard_map/attn_pack/pallas_call | solution.py:155
  3.3 7.3 %all-to-all-start = ((bf16[32,144,128]{2,1,0:T(8,128)(2,1)}), bf16[32,144,128]{2,1,0:T(8,128)(2,1)S(1)}, u32[]{:S(2)}, u32[]{:S(2)}) async-start(bf16[32,144,128]{2,1,0:T(8,128)(2,1)} %attn_pack.1), calls=%async_computation | async-start | bytes 2359296 | tf_op jit(solution)/shard_map/all_to_all | solution.py:596
  10.6 1.8 %conv_pack.1 = (bf16[64,1024]{1,0:T(8,128)(2,1)S(1)}, bf16[64,1024]{1,0:T(8,128)(2,1)}, bf16[64,1024]{1,0:T(8,128)(2,1)}, bf16[64,1024]{1,0:T(8,128)(2,1)}, bf16...) custom-call(bf16[32,8192]{1,0:T(8,128)(2,1)S(1)} %copy-done.3, ...), custom_call_target="tpu_custom_call" | custom-call | flops 1048576 | bytes 3145728 | tf_op jit(solution)/shard_map/conv_pack/pallas_call | solution.py:81
  13.3 1.7 %collective-permute-start.1 = (bf16[64,1024]{1,0:T(8,128)(2,1)}, bf16[64,1024]{1,0:T(8,128)(2,1)S(1)}, u32[]{:S(2)}, u32[]{:S(2)}) collective-permute-start(bf16[64,1024]{1,0:T(8,128)(2,1)} %get-tuple-element.72), channel_id=1, source_target_pairs={{0,2},{1,3},{2,0},{3,1},{4,6},{5,7},{6,4},{7,5},{8,10},{9,11},{10,... | collective-permute-start | bytes 393224 | tf_op jit(solution)/shard_map/ppermute | solution.py:576
  15.0 1.7 %collective-permute-start.3 = (bf16[64,1024]{1,0:T(8,128)(2,1)}, bf16[64,1024]{1,0:T(8,128)(2,1)}, u32[]{:S(2)}, u32[]{:S(2)}) collective-permute-start(bf16[64,1024]{1,0:T(8,128)(2,1)} %get-tuple-element.74), channel_id=1, source_target_pairs={{0,4},{1,5},{2,6},{3,7},{4,0},{5,1},{6,2},{7,3},{8,12},{9,13},{10,... | collective-permute-start | bytes 393224 | tf_op jit(solution)/shard_map/ppermute | solution.py:576
  16.8 2.6 %collective-permute-start.5 = (bf16[64,1024]{1,0:T(8,128)(2,1)S(1)}, bf16[64,1024]{1,0:T(8,128)(2,1)}, u32[]{:S(2)}, u32[]{:S(2)}) collective-permute-start(bf16[64,1024]{1,0:T(8,128)(2,1)S(1)} %get-tuple-element.76), channel_id=1, source_target_pairs={{0,6},{1,7},{2,4},{3,5},{4,2},{5,3},{6,0},{7,1},{8,14},{9,15},{10,... | collective-permute-start | bytes 393224 | tf_op jit(solution)/shard_map/ppermute | solution.py:576
  19.4 5.8 %collective-permute-done.1.refs_2_ = bf16[64,1024]{1,0:T(8,128)(2,1)S(1)} collective-permute-done((bf16[64,1024]{1,0:T(8,128)(2,1)}, bf16[64,1024]{1,0:T(8,128)(2,1)S(1)}, u32[]{:S(2)}, u32[]{:S(2)}) %collective-permute-start.1) | collective-permute-done | bytes 131104 | tf_op jit(solution)/shard_map/ppermute | solution.py:576
  27.1 1.9 %collective-permute-done.2.refs_3_ = bf16[64,1024]{1,0:T(8,128)(2,1)S(1)} collective-permute-done((bf16[64,1024]{1,0:T(8,128)(2,1)}, bf16[64,1024]{1,0:T(8,128)(2,1)S(1)}, u32[]{:S(2)}, u32[]{:S(2)}) %collective-permute-start.2) | collective-permute-done | bytes 131104 | tf_op jit(solution)/shard_map/ppermute | solution.py:576
  29.2 5.3 %collective-permute-done.5.refs_6_ = bf16[64,1024]{1,0:T(8,128)(2,1)} collective-permute-done((bf16[64,1024]{1,0:T(8,128)(2,1)S(1)}, bf16[64,1024]{1,0:T(8,128)(2,1)}, u32[]{:S(2)}, u32[]{:S(2)}) %collective-permute-start.5) | collective-permute-done | bytes 131104 | tf_op jit(solution)/shard_map/ppermute | solution.py:576
  34.5 3.2 %collective-permute-done.6.refs_7_ = bf16[64,1024]{1,0:T(8,128)(2,1)} collective-permute-done((bf16[64,1024]{1,0:T(8,128)(2,1)S(1)}, bf16[64,1024]{1,0:T(8,128)(2,1)}, u32[]{:S(2)}, u32[]{:S(2)}) %collective-permute-start.6) | collective-permute-done | bytes 131104 | tf_op jit(solution)/shard_map/ppermute | solution.py:576
  37.6 2.2 %conv_join.1 = (bf16[128,1024]{1,0:T(8,128)(2,1)}, bf16[128,1024]{1,0:T(8,128)(2,1)}, bf16[128,1024]{1,0:T(8,128)(2,1)}, bf16[128,1024]{1,0:T(8,128)(2,1)}) custom-call(bf16[64,1024]{1,0:T(8,128)(2,1)} %copy-done.4, bf16[64,1024]{1,0:T(8,128)(2,1)} %copy-done.10, bf16[64,1024]{1,0:T(8,128)(2,1)} %copy-done.11, bf16[64,1024]{1,0:T(8,128)(2,1)} %copy-done.12, ...), custom_call_target="tpu_custom_call" | custom-call | bytes 2097152 | tf_op jit(solution)/shard_map/conv_join/pallas_call | solution.py:113
  39.9 3.8 %collective-permute-start.7 = (bf16[128,1024]{1,0:T(8,128)(2,1)}, bf16[128,1024]{1,0:T(8,128)(2,1)}, u32[]{:S(2)}, u32[]{:S(2)}) collective-permute-start(bf16[128,1024]{1,0:T(8,128)(2,1)} %get-tuple-element.93.m1_ref), channel_id=1, source_target_pairs={{0,8},{1,9},{2,10},{3,11},{4,12},{5,13},{6,14},{7,15},{8,16},{9,17... | collective-permute-start | bytes 786440 | tf_op jit(solution)/shard_map/ppermute | solution.py:572
  44.9 5.5 %attn_head.1 = bf16[32,96,128]{2,1,0:T(8,128)(2,1)} custom-call(s32[12]{0:T(128)S(1)} %copy-done.5, bf16[32,144,128]{2,1,0:T(8,128)(2,1)S(1)} %all-to-all-done.x_ref), custom_call_target="tpu_custom_call" | custom-call | flops 1024 | bytes 589824 | tf_op jit(solution)/shard_map/attn_head/pallas_call | solution.py:220
  50.5 6.3 %all-to-all-start.1 = ((bf16[32,96,128]{2,1,0:T(8,128)(2,1)}), bf16[32,96,128]{2,1,0:T(8,128)(2,1)S(1)}, u32[]{:S(2)}, u32[]{:S(2)}) async-start(bf16[32,96,128]{2,1,0:T(8,128)(2,1)} %attn_head.1), calls=%async_computation.1 | async-start | bytes 1572864 | tf_op jit(solution)/shard_map/all_to_all | solution.py:612
  57.8 3.8 %conv_filter_grad.1 = f32[64,128]{1,0:T(8,128)S(1)} custom-call(s32[12]{0:T(128)S(1)} %copy-done.5, bf16[128,1024]{1,0:T(8,128)(2,1)} %collective-permute-done.7.prior_ref, bf16[128,1024]{1,0:T(8,128)(2,1)S(1)} %copy-done.6, bf16[128,1024]{1,0:T(8,128)(2,1)S(1)} %copy-done.7, bf16[128,1024]{1,0:T(8,128)(2,1)S(1)} %copy-done.8, bf16[128,1024]{1,0:T(8,128)(2,1)S(1)} %copy-done.9), custom_call_target="tpu_custom_call" | custom-call | flops 536870912 | bytes 1310720 | tf_op jit(solution)/shard_map/conv_filter_grad/pallas_call | solution.py:395
  61.6 6.0 %conv_core.1 = (bf16[64,1024]{1,0:T(8,128)(2,1)S(1)}, bf16[64,1024]{1,0:T(8,128)(2,1)S(1)}, bf16[64,1024]{1,0:T(8,128)(2,1)S(1)}, bf16[64,1024]{1,0:T(8,128)(2,1...) custom-call(s32[12]{0:T(128)S(1)} %copy-done.5, ...), custom_call_target="tpu_custom_call" | custom-call | flops 33554432000 | bytes 3145728 | tf_op jit(solution)/shard_map/conv_core/pallas_call | solution.py:353
  67.7 1.7 %collective-permute-start.11 = (bf16[64,1024]{1,0:T(8,128)(2,1)S(1)}, bf16[64,1024]{1,0:T(8,128)(2,1)S(1)}, u32[]{:S(2)}, u32[]{:S(2)}) collective-permute-start(bf16[64,1024]{1,0:T(8,128)(2,1)S(1)} %get-tuple-element.101), channel_id=1, source_target_pairs={{0,2},{1,3},{2,0},{3,1},{4,6},{5,7},{6,4},{7,5},{8,10},{9,11},{10,... | collective-permute-start | bytes 393224 | tf_op jit(solution)/shard_map/ppermute | solution.py:576
  69.4 1.5 %collective-permute-start.8 = (f32[64,128]{1,0:T(8,128)S(1)}, f32[64,128]{1,0:T(8,128)S(1)}, u32[]{:S(2)}, u32[]{:S(2)}) collective-permute-start(f32[64,128]{1,0:T(8,128)S(1)} %conv_filter_grad.1), channel_id=1, source_target_pairs={{0,8},{1,9},{2,10},{3,11},{4,12},{5,13},{6,14},{7,15},{8,0},{9,1},... | collective-permute-start | bytes 98312 | tf_op jit(solution)/shard_map/ppermute | solution.py:576
  70.8 1.5 %collective-permute-start.13 = (bf16[64,1024]{1,0:T(8,128)(2,1)S(1)}, bf16[64,1024]{1,0:T(8,128)(2,1)S(1)}, u32[]{:S(2)}, u32[]{:S(2)}) collective-permute-start(bf16[64,1024]{1,0:T(8,128)(2,1)S(1)} %get-tuple-element.109), channel_id=1, source_target_pairs={{0,4},{1,5},{2,6},{3,7},{4,0},{5,1},{6,2},{7,3},{8,12},{9,13},{10,... | collective-permute-start | bytes 393224 | tf_op jit(solution)/shard_map/ppermute | solution.py:576
  73.8 1.6 %collective-permute-start.15 = (bf16[64,1024]{1,0:T(8,128)(2,1)S(1)}, bf16[64,1024]{1,0:T(8,128)(2,1)S(1)}, u32[]{:S(2)}, u32[]{:S(2)}) collective-permute-start(bf16[64,1024]{1,0:T(8,128)(2,1)S(1)} %get-tuple-element.111), channel_id=1, source_target_pairs={{0,6},{1,7},{2,4},{3,5},{4,2},{5,3},{6,0},{7,1},{8,14},{9,15},{10,... | collective-permute-start | bytes 393224 | tf_op jit(solution)/shard_map/ppermute | solution.py:576
  75.4 1.9 %collective-permute-start.16 = (bf16[64,1024]{1,0:T(8,128)(2,1)S(1)}, bf16[64,1024]{1,0:T(8,128)(2,1)S(1)}, u32[]{:S(2)}, u32[]{:S(2)}) collective-permute-start(bf16[64,1024]{1,0:T(8,128)(2,1)S(1)} %get-tuple-element.112), channel_id=1, source_target_pairs={{0,7},{1,6},{2,5},{3,4},{4,3},{5,2},{6,1},{7,0},{8,15},{9,14},{10,... | collective-permute-start | bytes 393224 | tf_op jit(solution)/shard_map/ppermute | solution.py:576
  77.8 2.4 %collective-permute-start.17 = (f32[64,128]{1,0:T(8,128)S(1)}, f32[64,128]{1,0:T(8,128)S(1)}, u32[]{:S(2)}, u32[]{:S(2)}) collective-permute-start(f32[64,128]{1,0:T(8,128)S(1)} %add.10), channel_id=1, source_target_pairs={{0,16},{1,17},{2,18},{3,19},{4,20},{5,21},{6,22},{7,23},{8,24},{9,... | collective-permute-start | bytes 98312 | tf_op jit(solution)/shard_map/ppermute | solution.py:576
  80.1 6.0 %collective-permute-done.14.refs_5_ = bf16[64,1024]{1,0:T(8,128)(2,1)S(1)} collective-permute-done((bf16[64,1024]{1,0:T(8,128)(2,1)S(1)}, bf16[64,1024]{1,0:T(8,128)(2,1)S(1)}, u32[]{:S(2)}, u32[]{:S(2)}) %collective-permute-start.14) | collective-permute-done | bytes 131104 | tf_op jit(solution)/shard_map/ppermute | solution.py:576
  87.6 2.2 %conv_unpack.1 = (bf16[32,8192]{1,0:T(8,128)(2,1)}, bf16[32,8192]{1,0:T(8,128)(2,1)}, bf16[32,8192]{1,0:T(8,128)(2,1)}) custom-call(bf16[32,8192]{1,0:T(8,128)(2,1)S(1)} %copy-done, bf16[32,8192]{1,0:T(8,128)(2,1)S(1)} %copy-done.1, bf16[32,8192]{1,0:T(8,128)(2,1)S(1)} %copy-done.2, bf16[64,1024]{1,0:T(8,128)(2,1)S(1)} %get-tuple-element.114.refs_0_, ...), custom_call_target="tpu_custom_call" | custom-call | flops 1572864 | bytes 4194304 | tf_op jit(solution)/shard_map/conv_unpack/pallas_call | solution.py:431
  (61 shorter events, 10.4 us)
Async XLA Ops:
  3.3 36.6 %all-to-all-start = ((bf16[32,144,128]{2,1,0:T(8,128)(2,1)}), bf16[32,144,128]{2,1,0:T(8,128)(2,1)S(1)}, u32[]{:S(2)}, u32[]{:S(2)}) async-start(bf16[32,144,128]{2,1,0:T(8,128)(2,1)} %attn_pack.1), calls=%async_computation | async-start | bytes 2359296 | tf_op jit(solution)/shard_map/all_to_all | solution.py:596
  13.1 31.9 %copy-start.5 = (s32[12]{0:T(128)S(1)}, s32[12]{0:T(128)}, u32[]{:S(2)}) copy-start(s32[12]{0:T(128)} %lens_ref.5) | copy-start | bytes 148
  13.1 3.7 %collective-permute-start = (bf16[64,1024]{1,0:T(8,128)(2,1)}, bf16[64,1024]{1,0:T(8,128)(2,1)S(1)}, u32[]{:S(2)}, u32[]{:S(2)}) collective-permute-start(bf16[64,1024]{1,0:T(8,128)(2,1)} %get-tuple-element.71), channel_id=1, source_target_pairs={{0,1},{1,0},{2,3},{3,2},{4,5},{5,4},{6,7},{7,6},{8,9},{9,8},{10,11... | collective-permute-start | bytes 393224 | tf_op jit(solution)/shard_map/ppermute | solution.py:576
  13.3 11.9 %collective-permute-start.1 = (bf16[64,1024]{1,0:T(8,128)(2,1)}, bf16[64,1024]{1,0:T(8,128)(2,1)S(1)}, u32[]{:S(2)}, u32[]{:S(2)}) collective-permute-start(bf16[64,1024]{1,0:T(8,128)(2,1)} %get-tuple-element.72), channel_id=1, source_target_pairs={{0,2},{1,3},{2,0},{3,1},{4,6},{5,7},{6,4},{7,5},{8,10},{9,11},{10,... | collective-permute-start | bytes 393224 | tf_op jit(solution)/shard_map/ppermute | solution.py:576
  15.0 13.9 %collective-permute-start.2 = (bf16[64,1024]{1,0:T(8,128)(2,1)}, bf16[64,1024]{1,0:T(8,128)(2,1)S(1)}, u32[]{:S(2)}, u32[]{:S(2)}) collective-permute-start(bf16[64,1024]{1,0:T(8,128)(2,1)} %get-tuple-element.73), channel_id=1, source_target_pairs={{0,3},{1,2},{2,1},{3,0},{4,7},{5,6},{6,5},{7,4},{8,11},{9,10},{10,... | collective-permute-start | bytes 393224 | tf_op jit(solution)/shard_map/ppermute | solution.py:576
  15.0 13.9 %collective-permute-start.3 = (bf16[64,1024]{1,0:T(8,128)(2,1)}, bf16[64,1024]{1,0:T(8,128)(2,1)}, u32[]{:S(2)}, u32[]{:S(2)}) collective-permute-start(bf16[64,1024]{1,0:T(8,128)(2,1)} %get-tuple-element.74), channel_id=1, source_target_pairs={{0,4},{1,5},{2,6},{3,7},{4,0},{5,1},{6,2},{7,3},{8,12},{9,13},{10,... | collective-permute-start | bytes 393224 | tf_op jit(solution)/shard_map/ppermute | solution.py:576
  16.7 12.5 %collective-permute-start.4 = (bf16[64,1024]{1,0:T(8,128)(2,1)}, bf16[64,1024]{1,0:T(8,128)(2,1)}, u32[]{:S(2)}, u32[]{:S(2)}) collective-permute-start(bf16[64,1024]{1,0:T(8,128)(2,1)} %get-tuple-element.75), channel_id=1, source_target_pairs={{0,5},{1,4},{2,7},{3,6},{4,1},{5,0},{6,3},{7,2},{8,13},{9,12},{10,... | collective-permute-start | bytes 393224 | tf_op jit(solution)/shard_map/ppermute | solution.py:576
  16.8 20.8 %copy-start.10 = (bf16[64,1024]{1,0:T(8,128)(2,1)}, bf16[64,1024]{1,0:T(8,128)(2,1)S(1)}, u32[]{:S(2)}) copy-start(bf16[64,1024]{1,0:T(8,128)(2,1)S(1)} %collective-permute-done.refs_1_) | copy-start | bytes 393220
  16.8 17.6 %collective-permute-start.5 = (bf16[64,1024]{1,0:T(8,128)(2,1)S(1)}, bf16[64,1024]{1,0:T(8,128)(2,1)}, u32[]{:S(2)}, u32[]{:S(2)}) collective-permute-start(bf16[64,1024]{1,0:T(8,128)(2,1)S(1)} %get-tuple-element.76), channel_id=1, source_target_pairs={{0,6},{1,7},{2,4},{3,5},{4,2},{5,3},{6,0},{7,1},{8,14},{9,15},{10,... | collective-permute-start | bytes 393224 | tf_op jit(solution)/shard_map/ppermute | solution.py:576
  25.2 12.4 %copy-start.11 = (bf16[64,1024]{1,0:T(8,128)(2,1)}, bf16[64,1024]{1,0:T(8,128)(2,1)S(1)}, u32[]{:S(2)}) copy-start(bf16[64,1024]{1,0:T(8,128)(2,1)S(1)} %collective-permute-done.1.refs_2_) | copy-start | bytes 393220
  25.2 12.4 %collective-permute-start.6 = (bf16[64,1024]{1,0:T(8,128)(2,1)S(1)}, bf16[64,1024]{1,0:T(8,128)(2,1)}, u32[]{:S(2)}, u32[]{:S(2)}) collective-permute-start(bf16[64,1024]{1,0:T(8,128)(2,1)S(1)} %get-tuple-element.77), channel_id=1, source_target_pairs={{0,7},{1,6},{2,5},{3,4},{4,3},{5,2},{6,1},{7,0},{8,15},{9,14},{10,... | collective-permute-start | bytes 393224 | tf_op jit(solution)/shard_map/ppermute | solution.py:576
  39.9 16.9 %collective-permute-start.7 = (bf16[128,1024]{1,0:T(8,128)(2,1)}, bf16[128,1024]{1,0:T(8,128)(2,1)}, u32[]{:S(2)}, u32[]{:S(2)}) collective-permute-start(bf16[128,1024]{1,0:T(8,128)(2,1)} %get-tuple-element.93.m1_ref), channel_id=1, source_target_pairs={{0,8},{1,9},{2,10},{3,11},{4,12},{5,13},{6,14},{7,15},{8,16},{9,17... | collective-permute-start | bytes 786440 | tf_op jit(solution)/shard_map/ppermute | solution.py:572
  43.6 17.9 %collective-permute-start.9 = (bf16[128,1024]{1,0:T(8,128)(2,1)}, bf16[128,1024]{1,0:T(8,128)(2,1)}, u32[]{:S(2)}, u32[]{:S(2)}) collective-permute-start(bf16[128,1024]{1,0:T(8,128)(2,1)} %get-tuple-element.95.g0_ref), channel_id=1, source_target_pairs={{8,0},{9,1},{10,2},{11,3},{12,4},{13,5},{14,6},{15,7},{16,8},{17,9... | collective-permute-start | bytes 786440 | tf_op jit(solution)/shard_map/ppermute | solution.py:572
  50.5 39.9 %all-to-all-start.1 = ((bf16[32,96,128]{2,1,0:T(8,128)(2,1)}), bf16[32,96,128]{2,1,0:T(8,128)(2,1)S(1)}, u32[]{:S(2)}, u32[]{:S(2)}) async-start(bf16[32,96,128]{2,1,0:T(8,128)(2,1)} %attn_head.1), calls=%async_computation.1 | async-start | bytes 1572864 | tf_op jit(solution)/shard_map/all_to_all | solution.py:612
  67.5 6.3 %collective-permute-start.10 = (bf16[64,1024]{1,0:T(8,128)(2,1)S(1)}, bf16[64,1024]{1,0:T(8,128)(2,1)S(1)}, u32[]{:S(2)}, u32[]{:S(2)}) collective-permute-start(bf16[64,1024]{1,0:T(8,128)(2,1)S(1)} %get-tuple-element.100), channel_id=1, source_target_pairs={{0,1},{1,0},{2,3},{3,2},{4,5},{5,4},{6,7},{7,6},{8,9},{9,8},{10,11... | collective-permute-start | bytes 393224 | tf_op jit(solution)/shard_map/ppermute | solution.py:576
  67.7 7.7 %collective-permute-start.11 = (bf16[64,1024]{1,0:T(8,128)(2,1)S(1)}, bf16[64,1024]{1,0:T(8,128)(2,1)S(1)}, u32[]{:S(2)}, u32[]{:S(2)}) collective-permute-start(bf16[64,1024]{1,0:T(8,128)(2,1)S(1)} %get-tuple-element.101), channel_id=1, source_target_pairs={{0,2},{1,3},{2,0},{3,1},{4,6},{5,7},{6,4},{7,5},{8,10},{9,11},{10,... | collective-permute-start | bytes 393224 | tf_op jit(solution)/shard_map/ppermute | solution.py:576
  69.4 4.1 %collective-permute-start.8 = (f32[64,128]{1,0:T(8,128)S(1)}, f32[64,128]{1,0:T(8,128)S(1)}, u32[]{:S(2)}, u32[]{:S(2)}) collective-permute-start(f32[64,128]{1,0:T(8,128)S(1)} %conv_filter_grad.1), channel_id=1, source_target_pairs={{0,8},{1,9},{2,10},{3,11},{4,12},{5,13},{6,14},{7,15},{8,0},{9,1},... | collective-permute-start | bytes 98312 | tf_op jit(solution)/shard_map/ppermute | solution.py:576
  70.8 6.9 %collective-permute-start.12 = (bf16[64,1024]{1,0:T(8,128)(2,1)S(1)}, bf16[64,1024]{1,0:T(8,128)(2,1)S(1)}, u32[]{:S(2)}, u32[]{:S(2)}) collective-permute-start(bf16[64,1024]{1,0:T(8,128)(2,1)S(1)} %get-tuple-element.102), channel_id=1, source_target_pairs={{0,3},{1,2},{2,1},{3,0},{4,7},{5,6},{6,5},{7,4},{8,11},{9,10},{10,... | collective-permute-start | bytes 393224 | tf_op jit(solution)/shard_map/ppermute | solution.py:576
  70.8 9.3 %collective-permute-start.13 = (bf16[64,1024]{1,0:T(8,128)(2,1)S(1)}, bf16[64,1024]{1,0:T(8,128)(2,1)S(1)}, u32[]{:S(2)}, u32[]{:S(2)}) collective-permute-start(bf16[64,1024]{1,0:T(8,128)(2,1)S(1)} %get-tuple-element.109), channel_id=1, source_target_pairs={{0,4},{1,5},{2,6},{3,7},{4,0},{5,1},{6,2},{7,3},{8,12},{9,13},{10,... | collective-permute-start | bytes 393224 | tf_op jit(solution)/shard_map/ppermute | solution.py:576
  73.5 12.6 %collective-permute-start.14 = (bf16[64,1024]{1,0:T(8,128)(2,1)S(1)}, bf16[64,1024]{1,0:T(8,128)(2,1)S(1)}, u32[]{:S(2)}, u32[]{:S(2)}) collective-permute-start(bf16[64,1024]{1,0:T(8,128)(2,1)S(1)} %get-tuple-element.110), channel_id=1, source_target_pairs={{0,5},{1,4},{2,7},{3,6},{4,1},{5,0},{6,3},{7,2},{8,13},{9,12},{10,... | collective-permute-start | bytes 393224 | tf_op jit(solution)/shard_map/ppermute | solution.py:576
  73.8 12.3 %collective-permute-start.15 = (bf16[64,1024]{1,0:T(8,128)(2,1)S(1)}, bf16[64,1024]{1,0:T(8,128)(2,1)S(1)}, u32[]{:S(2)}, u32[]{:S(2)}) collective-permute-start(bf16[64,1024]{1,0:T(8,128)(2,1)S(1)} %get-tuple-element.111), channel_id=1, source_target_pairs={{0,6},{1,7},{2,4},{3,5},{4,2},{5,3},{6,0},{7,1},{8,14},{9,15},{10,... | collective-permute-start | bytes 393224 | tf_op jit(solution)/shard_map/ppermute | solution.py:576
  75.4 10.7 %collective-permute-start.16 = (bf16[64,1024]{1,0:T(8,128)(2,1)S(1)}, bf16[64,1024]{1,0:T(8,128)(2,1)S(1)}, u32[]{:S(2)}, u32[]{:S(2)}) collective-permute-start(bf16[64,1024]{1,0:T(8,128)(2,1)S(1)} %get-tuple-element.112), channel_id=1, source_target_pairs={{0,7},{1,6},{2,5},{3,4},{4,3},{5,2},{6,1},{7,0},{8,15},{9,14},{10,... | collective-permute-start | bytes 393224 | tf_op jit(solution)/shard_map/ppermute | solution.py:576
  77.8 8.4 %collective-permute-start.17 = (f32[64,128]{1,0:T(8,128)S(1)}, f32[64,128]{1,0:T(8,128)S(1)}, u32[]{:S(2)}, u32[]{:S(2)}) collective-permute-start(f32[64,128]{1,0:T(8,128)S(1)} %add.10), channel_id=1, source_target_pairs={{0,16},{1,17},{2,18},{3,19},{4,20},{5,21},{6,22},{7,23},{8,24},{9,... | collective-permute-start | bytes 98312 | tf_op jit(solution)/shard_map/ppermute | solution.py:576
  86.4 3.9 %collective-permute-start.18 = (f32[64,128]{1,0:T(8,128)S(1)}, f32[64,128]{1,0:T(8,128)S(1)}, u32[]{:S(2)}, u32[]{:S(2)}) collective-permute-start(f32[64,128]{1,0:T(8,128)S(1)} %pad_maximum_fusion.1.mine_ref), channel_id=1, source_target_pairs={{0,4},{1,5},{2,6},{3,7},{4,0},{5,1},{6,2},{7,3},{8,12},{9,13},{10,... | collective-permute-start | bytes 98312 | tf_op jit(solution)/shard_map/ppermute | solution.py:576
  (10 other events, 58.7 us)

commit v5 on v4

--- a/solution.py
+++ b/solution.py
@@ -596,7 +596,10 @@
         attn_in = lax.all_to_all(attn_packed, DEVICES, split_axis=0, concat_axis=0, tiled=True)
 
     packed = conv_pack(conv_query, conv_key, conv_value, conv_grad_out, inner, ch_count)
-    pieces = [packed[0]] + [exchanged(packed[k], k, count) for k in range(1, members)]
+    packed = list(packed)
+    pieces = [packed[0], exchanged(packed[1], 1, count)]
+    packed[-1], pieces[1] = lax.optimization_barrier((packed[-1], pieces[1]))
+    pieces += [exchanged(packed[k], k, count) for k in range(2, members)]
     group_count = channels // members // GROUP
     y = lax.rem(lax.axis_index("seq"), inner)
     taps = lax.dynamic_slice_in_dim(conv_filter, y * group_count, group_count, 0).astype(F32)
@@ -615,7 +618,10 @@
     other = exchanged(filter_part, members, count)
     taps, filter_part = lax.optimization_barrier((taps, filter_part))
     conv_back = conv_core(doc_lengths, taps, rev_taps, own, rows, inner, ch_count)
-    conv_res = [conv_back[0]] + [exchanged(conv_back[k], k, count) for k in range(1, members)]
+    conv_back = list(conv_back)
+    conv_res = [conv_back[0], exchanged(conv_back[1], 1, count)]
+    conv_back[-1], conv_res[1] = lax.optimization_barrier((conv_back[-1], conv_res[1]))
+    conv_res += [exchanged(conv_back[k], k, count) for k in range(2, members)]
     filter_part, other, conv_res[1:4] = lax.optimization_barrier(
         (filter_part, other, conv_res[1:4])
     )

time: 92 us -> 91.3 us (level)
  transfers between devices with their start and end apart: 21 -> 21, of which waited for: 9 -> 9; matrix products, arithmetic and copies ran while one was open for 1% -> 1% of each run, Pallas kernels for 23% -> 24%
where the time goes in v5:
time: 91.3 us; the launch traced here: 90.8 us
  starting transfers between devices  37.6 us (41%)
  Pallas kernels  25.1 us (27%)
  waiting for transfers between devices  24.3 us (27%)
  local copies, waits for them, and re-layouts  1.94 us (2%)
  between operations  0.97 us (1%)
    ppermute x17, waiting for transfers between devices, exchanged(): lax.ppermute(block, DEVICES, [(i, i ^ distance) for i in range(count)])  24.3 us
    ppermute x17, starting transfers between devices, exchanged(): lax.ppermute(block, DEVICES, [(i, i ^ distance) for i in range(count)])  18.9 us
    all_to_all x1, starting transfers between devices, body(): lax.all_to_all(attn_packed, DEVICES, split_axis=0, concat_axis=0, tiled=T...  7.3 us
    all_to_all x1, starting transfers between devices, body(): lax.all_to_all(attn_back, DEVICES, split_axis=0, concat_axis=0, tiled=True)  6.31 us
    pallas_call x1, Pallas kernels, conv_core(): pl.pallas_call(functools.partial(conv_core_kernel, rows, inner, ch_count)...  5.97 us
    pallas_call x1, Pallas kernels, attn_head(): pl.pallas_call(functools.partial(attn_kernel, rows, reach), in_specs=[pl....  5.51 us
    ppermute x2, starting transfers between devices, shifted(): return lax.ppermute(block, DEVICES, route)  5.06 us
    pallas_call x1, Pallas kernels, conv_filter_grad(): pl.pallas_call(functools.partial(conv_filter_kernel, rows, inner, ch_coun...  3.78 us
  transfers between devices with their start and end apart: 21, of which 9 were waited for; matrix products, arithmetic and copies ran while one was open for 1% of the time, Pallas kernels for 24%

profile of v5, /device:TPU:0, one launch (start us, length us, event | category | flops | bytes accessed | tf_op | source)
XLA Modules:
  0.0 90.8 jit_solution(11703439563142253305)
XLA Ops:
  0.6 2.6 %attn_pack.1 = bf16[32,144,128]{2,1,0:T(8,128)(2,1)} custom-call(bf16[32,4096]{1,0:T(8,128)(2,1)} %q_ref.1, bf16[32,4096]{1,0:T(8,128)(2,1)} %k_ref.1, bf16[32,4096]{1,0:T(8,128)(2,1)} %v_ref.1, bf16[32,4096]{1,0:T(8,128)(2,1)} %o_ref.1, bf16[32,4096]{1,0:T(8,128)(2,1)} %g_ref.1), custom_call_target="tpu_custom_call" | custom-call | flops 524288 | bytes 2621440 | tf_op jit(solution)/shard_map/attn_pack/pallas_call | solution.py:155
  3.3 7.3 %all-to-all-start = ((bf16[32,144,128]{2,1,0:T(8,128)(2,1)}), bf16[32,144,128]{2,1,0:T(8,128)(2,1)S(1)}, u32[]{:S(2)}, u32[]{:S(2)}) async-start(bf16[32,144,128]{2,1,0:T(8,128)(2,1)} %attn_pack.1), calls=%async_computation | async-start | bytes 2359296 | tf_op jit(solution)/shard_map/all_to_all | solution.py:596
  10.6 1.8 %conv_pack.1 = (bf16[64,1024]{1,0:T(8,128)(2,1)S(1)}, bf16[64,1024]{1,0:T(8,128)(2,1)}, bf16[64,1024]{1,0:T(8,128)(2,1)}, bf16[64,1024]{1,0:T(8,128)(2,1)}, bf16...) custom-call(bf16[32,8192]{1,0:T(8,128)(2,1)S(1)} %copy-done.3, ...), custom_call_target="tpu_custom_call" | custom-call | flops 1048576 | bytes 3145728 | tf_op jit(solution)/shard_map/conv_pack/pallas_call | solution.py:81
  13.3 1.7 %collective-permute-start.1 = (bf16[64,1024]{1,0:T(8,128)(2,1)}, bf16[64,1024]{1,0:T(8,128)(2,1)S(1)}, u32[]{:S(2)}, u32[]{:S(2)}) collective-permute-start(bf16[64,1024]{1,0:T(8,128)(2,1)} %get-tuple-element.78), channel_id=1, source_target_pairs={{0,2},{1,3},{2,0},{3,1},{4,6},{5,7},{6,4},{7,5},{8,10},{9,11},{10,... | collective-permute-start | bytes 393224 | tf_op jit(solution)/shard_map/ppermute | solution.py:576
  15.0 1.7 %collective-permute-start.3 = (bf16[64,1024]{1,0:T(8,128)(2,1)}, bf16[64,1024]{1,0:T(8,128)(2,1)}, u32[]{:S(2)}, u32[]{:S(2)}) collective-permute-start(bf16[64,1024]{1,0:T(8,128)(2,1)} %get-tuple-element.80), channel_id=1, source_target_pairs={{0,4},{1,5},{2,6},{3,7},{4,0},{5,1},{6,2},{7,3},{8,12},{9,13},{10,... | collective-permute-start | bytes 393224 | tf_op jit(solution)/shard_map/ppermute | solution.py:576
  16.8 2.6 %collective-permute-start.5 = (bf16[64,1024]{1,0:T(8,128)(2,1)S(1)}, bf16[64,1024]{1,0:T(8,128)(2,1)}, u32[]{:S(2)}, u32[]{:S(2)}) collective-permute-start(bf16[64,1024]{1,0:T(8,128)(2,1)S(1)} %get-tuple-element.82), channel_id=1, source_target_pairs={{0,6},{1,7},{2,4},{3,5},{4,2},{5,3},{6,0},{7,1},{8,14},{9,15},{10,... | collective-permute-start | bytes 393224 | tf_op jit(solution)/shard_map/ppermute | solution.py:576
  19.4 5.8 %collective-permute-done.1.refs_2_ = bf16[64,1024]{1,0:T(8,128)(2,1)S(1)} collective-permute-done((bf16[64,1024]{1,0:T(8,128)(2,1)}, bf16[64,1024]{1,0:T(8,128)(2,1)S(1)}, u32[]{:S(2)}, u32[]{:S(2)}) %collective-permute-start.1) | collective-permute-done | bytes 131104 | tf_op jit(solution)/shard_map/ppermute | solution.py:576
  27.1 1.9 %collective-permute-done.2.refs_3_ = bf16[64,1024]{1,0:T(8,128)(2,1)S(1)} collective-permute-done((bf16[64,1024]{1,0:T(8,128)(2,1)}, bf16[64,1024]{1,0:T(8,128)(2,1)S(1)}, u32[]{:S(2)}, u32[]{:S(2)}) %collective-permute-start.2) | collective-permute-done | bytes 131104 | tf_op jit(solution)/shard_map/ppermute | solution.py:576
  29.2 5.3 %collective-permute-done.5.refs_6_ = bf16[64,1024]{1,0:T(8,128)(2,1)} collective-permute-done((bf16[64,1024]{1,0:T(8,128)(2,1)S(1)}, bf16[64,1024]{1,0:T(8,128)(2,1)}, u32[]{:S(2)}, u32[]{:S(2)}) %collective-permute-start.5) | collective-permute-done | bytes 131104 | tf_op jit(solution)/shard_map/ppermute | solution.py:576
  34.5 3.2 %collective-permute-done.6.refs_7_ = bf16[64,1024]{1,0:T(8,128)(2,1)} collective-permute-done((bf16[64,1024]{1,0:T(8,128)(2,1)S(1)}, bf16[64,1024]{1,0:T(8,128)(2,1)}, u32[]{:S(2)}, u32[]{:S(2)}) %collective-permute-start.6) | collective-permute-done | bytes 131104 | tf_op jit(solution)/shard_map/ppermute | solution.py:576
  37.6 2.2 %conv_join.1 = (bf16[128,1024]{1,0:T(8,128)(2,1)}, bf16[128,1024]{1,0:T(8,128)(2,1)}, bf16[128,1024]{1,0:T(8,128)(2,1)}, bf16[128,1024]{1,0:T(8,128)(2,1)}) custom-call(bf16[64,1024]{1,0:T(8,128)(2,1)} %copy-done.4, bf16[64,1024]{1,0:T(8,128)(2,1)} %copy-done.10, bf16[64,1024]{1,0:T(8,128)(2,1)} %copy-done.11, bf16[64,1024]{1,0:T(8,128)(2,1)} %copy-done.12, ...), custom_call_target="tpu_custom_call" | custom-call | bytes 2097152 | tf_op jit(solution)/shard_map/conv_join/pallas_call | solution.py:113
  39.9 3.8 %collective-permute-start.7 = (bf16[128,1024]{1,0:T(8,128)(2,1)}, bf16[128,1024]{1,0:T(8,128)(2,1)}, u32[]{:S(2)}, u32[]{:S(2)}) collective-permute-start(bf16[128,1024]{1,0:T(8,128)(2,1)} %get-tuple-element.99.m1_ref), channel_id=1, source_target_pairs={{0,8},{1,9},{2,10},{3,11},{4,12},{5,13},{6,14},{7,15},{8,16},{9,17... | collective-permute-start | bytes 786440 | tf_op jit(solution)/shard_map/ppermute | solution.py:572
  43.6 1.3 %collective-permute-start.9 = (bf16[128,1024]{1,0:T(8,128)(2,1)}, bf16[128,1024]{1,0:T(8,128)(2,1)}, u32[]{:S(2)}, u32[]{:S(2)}) collective-permute-start(bf16[128,1024]{1,0:T(8,128)(2,1)} %get-tuple-element.101.g0_ref), channel_id=1, source_target_pairs={{8,0},{9,1},{10,2},{11,3},{12,4},{13,5},{14,6},{15,7},{16,8},{17,9... | collective-permute-start | bytes 786440 | tf_op jit(solution)/shard_map/ppermute | solution.py:572
  44.9 5.5 %attn_head.1 = bf16[32,96,128]{2,1,0:T(8,128)(2,1)} custom-call(s32[12]{0:T(128)S(1)} %copy-done.5, bf16[32,144,128]{2,1,0:T(8,128)(2,1)S(1)} %all-to-all-done.x_ref), custom_call_target="tpu_custom_call" | custom-call | flops 1024 | bytes 589824 | tf_op jit(solution)/shard_map/attn_head/pallas_call | solution.py:220
  50.5 6.3 %all-to-all-start.1 = ((bf16[32,96,128]{2,1,0:T(8,128)(2,1)}), bf16[32,96,128]{2,1,0:T(8,128)(2,1)S(1)}, u32[]{:S(2)}, u32[]{:S(2)}) async-start(bf16[32,96,128]{2,1,0:T(8,128)(2,1)} %attn_head.1), calls=%async_computation.1 | async-start | bytes 1572864 | tf_op jit(solution)/shard_map/all_to_all | solution.py:615
  57.8 3.8 %conv_filter_grad.1 = f32[64,128]{1,0:T(8,128)S(1)} custom-call(s32[12]{0:T(128)S(1)} %copy-done.5, bf16[128,1024]{1,0:T(8,128)(2,1)} %collective-permute-done.7.prior_ref, bf16[128,1024]{1,0:T(8,128)(2,1)S(1)} %copy-done.6, bf16[128,1024]{1,0:T(8,128)(2,1)S(1)} %copy-done.7, bf16[128,1024]{1,0:T(8,128)(2,1)S(1)} %copy-done.8, bf16[128,1024]{1,0:T(8,128)(2,1)S(1)} %copy-done.9), custom_call_target="tpu_custom_call" | custom-call | flops 536870912 | bytes 1310720 | tf_op jit(solution)/shard_map/conv_filter_grad/pallas_call | solution.py:395
  61.6 6.0 %conv_core.1 = (bf16[64,1024]{1,0:T(8,128)(2,1)S(1)}, bf16[64,1024]{1,0:T(8,128)(2,1)S(1)}, bf16[64,1024]{1,0:T(8,128)(2,1)S(1)}, bf16[64,1024]{1,0:T(8,128)(2,1...) custom-call(s32[12]{0:T(128)S(1)} %copy-done.5, ...), custom_call_target="tpu_custom_call" | custom-call | flops 33554432000 | bytes 3145728 | tf_op jit(solution)/shard_map/conv_core/pallas_call | solution.py:353
  67.7 1.7 %collective-permute-start.11 = (bf16[64,1024]{1,0:T(8,128)(2,1)S(1)}, bf16[64,1024]{1,0:T(8,128)(2,1)S(1)}, u32[]{:S(2)}, u32[]{:S(2)}) collective-permute-start(bf16[64,1024]{1,0:T(8,128)(2,1)S(1)} %get-tuple-element.109), channel_id=1, source_target_pairs={{0,2},{1,3},{2,0},{3,1},{4,6},{5,7},{6,4},{7,5},{8,10},{9,11},{10,... | collective-permute-start | bytes 393224 | tf_op jit(solution)/shard_map/ppermute | solution.py:576
  69.5 1.6 %collective-permute-start.8 = (f32[64,128]{1,0:T(8,128)S(1)}, f32[64,128]{1,0:T(8,128)S(1)}, u32[]{:S(2)}, u32[]{:S(2)}) collective-permute-start(f32[64,128]{1,0:T(8,128)S(1)} %conv_filter_grad.1), channel_id=1, source_target_pairs={{0,8},{1,9},{2,10},{3,11},{4,12},{5,13},{6,14},{7,15},{8,0},{9,1},... | collective-permute-start | bytes 98312 | tf_op jit(solution)/shard_map/ppermute | solution.py:576
  71.1 1.5 %collective-permute-start.13 = (bf16[64,1024]{1,0:T(8,128)(2,1)S(1)}, bf16[64,1024]{1,0:T(8,128)(2,1)S(1)}, u32[]{:S(2)}, u32[]{:S(2)}) collective-permute-start(bf16[64,1024]{1,0:T(8,128)(2,1)S(1)} %get-tuple-element.117), channel_id=1, source_target_pairs={{0,4},{1,5},{2,6},{3,7},{4,0},{5,1},{6,2},{7,3},{8,12},{9,13},{10,... | collective-permute-start | bytes 393224 | tf_op jit(solution)/shard_map/ppermute | solution.py:576
  73.6 3.0 %collective-permute-start.15 = (bf16[64,1024]{1,0:T(8,128)(2,1)S(1)}, bf16[64,1024]{1,0:T(8,128)(2,1)S(1)}, u32[]{:S(2)}, u32[]{:S(2)}) collective-permute-start(bf16[64,1024]{1,0:T(8,128)(2,1)S(1)} %get-tuple-element.119), channel_id=1, source_target_pairs={{0,6},{1,7},{2,4},{3,5},{4,2},{5,3},{6,0},{7,1},{8,14},{9,15},{10,... | collective-permute-start | bytes 393224 | tf_op jit(solution)/shard_map/ppermute | solution.py:576
  77.6 2.5 %collective-permute-start.17 = (f32[64,128]{1,0:T(8,128)S(1)}, f32[64,128]{1,0:T(8,128)S(1)}, u32[]{:S(2)}, u32[]{:S(2)}) collective-permute-start(f32[64,128]{1,0:T(8,128)S(1)} %add.10), channel_id=1, source_target_pairs={{0,16},{1,17},{2,18},{3,19},{4,20},{5,21},{6,22},{7,23},{8,24},{9,... | collective-permute-start | bytes 98312 | tf_op jit(solution)/shard_map/ppermute | solution.py:576
  80.1 5.3 %collective-permute-done.14.refs_5_ = bf16[64,1024]{1,0:T(8,128)(2,1)S(1)} collective-permute-done((bf16[64,1024]{1,0:T(8,128)(2,1)S(1)}, bf16[64,1024]{1,0:T(8,128)(2,1)S(1)}, u32[]{:S(2)}, u32[]{:S(2)}) %collective-permute-start.14) | collective-permute-done | bytes 131104 | tf_op jit(solution)/shard_map/ppermute | solution.py:576
  86.9 2.2 %conv_unpack.1 = (bf16[32,8192]{1,0:T(8,128)(2,1)}, bf16[32,8192]{1,0:T(8,128)(2,1)}, bf16[32,8192]{1,0:T(8,128)(2,1)}) custom-call(bf16[32,8192]{1,0:T(8,128)(2,1)S(1)} %copy-done, bf16[32,8192]{1,0:T(8,128)(2,1)S(1)} %copy-done.1, bf16[32,8192]{1,0:T(8,128)(2,1)S(1)} %copy-done.2, bf16[64,1024]{1,0:T(8,128)(2,1)S(1)} %get-tuple-element.122.refs_0_, ...), custom_call_target="tpu_custom_call" | custom-call | flops 1572864 | bytes 4194304 | tf_op jit(solution)/shard_map/conv_unpack/pallas_call | solution.py:431
  (61 shorter events, 9.4 us)
Async XLA Ops:
  3.3 36.6 %all-to-all-start = ((bf16[32,144,128]{2,1,0:T(8,128)(2,1)}), bf16[32,144,128]{2,1,0:T(8,128)(2,1)S(1)}, u32[]{:S(2)}, u32[]{:S(2)}) async-start(bf16[32,144,128]{2,1,0:T(8,128)(2,1)} %attn_pack.1), calls=%async_computation | async-start | bytes 2359296 | tf_op jit(solution)/shard_map/all_to_all | solution.py:596
  13.1 31.9 %copy-start.5 = (s32[12]{0:T(128)S(1)}, s32[12]{0:T(128)}, u32[]{:S(2)}) copy-start(s32[12]{0:T(128)} %lens_ref.5) | copy-start | bytes 148
  13.1 3.7 %collective-permute-start = (bf16[64,1024]{1,0:T(8,128)(2,1)}, bf16[64,1024]{1,0:T(8,128)(2,1)S(1)}, u32[]{:S(2)}, u32[]{:S(2)}) collective-permute-start(bf16[64,1024]{1,0:T(8,128)(2,1)} %get-tuple-element.76), channel_id=1, source_target_pairs={{0,1},{1,0},{2,3},{3,2},{4,5},{5,4},{6,7},{7,6},{8,9},{9,8},{10,11... | collective-permute-start | bytes 393224 | tf_op jit(solution)/shard_map/ppermute | solution.py:576
  13.3 11.9 %collective-permute-start.1 = (bf16[64,1024]{1,0:T(8,128)(2,1)}, bf16[64,1024]{1,0:T(8,128)(2,1)S(1)}, u32[]{:S(2)}, u32[]{:S(2)}) collective-permute-start(bf16[64,1024]{1,0:T(8,128)(2,1)} %get-tuple-element.78), channel_id=1, source_target_pairs={{0,2},{1,3},{2,0},{3,1},{4,6},{5,7},{6,4},{7,5},{8,10},{9,11},{10,... | collective-permute-start | bytes 393224 | tf_op jit(solution)/shard_map/ppermute | solution.py:576
  15.0 13.9 %collective-permute-start.2 = (bf16[64,1024]{1,0:T(8,128)(2,1)}, bf16[64,1024]{1,0:T(8,128)(2,1)S(1)}, u32[]{:S(2)}, u32[]{:S(2)}) collective-permute-start(bf16[64,1024]{1,0:T(8,128)(2,1)} %get-tuple-element.79), channel_id=1, source_target_pairs={{0,3},{1,2},{2,1},{3,0},{4,7},{5,6},{6,5},{7,4},{8,11},{9,10},{10,... | collective-permute-start | bytes 393224 | tf_op jit(solution)/shard_map/ppermute | solution.py:576
  15.0 13.9 %collective-permute-start.3 = (bf16[64,1024]{1,0:T(8,128)(2,1)}, bf16[64,1024]{1,0:T(8,128)(2,1)}, u32[]{:S(2)}, u32[]{:S(2)}) collective-permute-start(bf16[64,1024]{1,0:T(8,128)(2,1)} %get-tuple-element.80), channel_id=1, source_target_pairs={{0,4},{1,5},{2,6},{3,7},{4,0},{5,1},{6,2},{7,3},{8,12},{9,13},{10,... | collective-permute-start | bytes 393224 | tf_op jit(solution)/shard_map/ppermute | solution.py:576
  16.7 12.5 %collective-permute-start.4 = (bf16[64,1024]{1,0:T(8,128)(2,1)}, bf16[64,1024]{1,0:T(8,128)(2,1)}, u32[]{:S(2)}, u32[]{:S(2)}) collective-permute-start(bf16[64,1024]{1,0:T(8,128)(2,1)} %get-tuple-element.81), channel_id=1, source_target_pairs={{0,5},{1,4},{2,7},{3,6},{4,1},{5,0},{6,3},{7,2},{8,13},{9,12},{10,... | collective-permute-start | bytes 393224 | tf_op jit(solution)/shard_map/ppermute | solution.py:576
  16.8 20.8 %copy-start.10 = (bf16[64,1024]{1,0:T(8,128)(2,1)}, bf16[64,1024]{1,0:T(8,128)(2,1)S(1)}, u32[]{:S(2)}) copy-start(bf16[64,1024]{1,0:T(8,128)(2,1)S(1)} %collective-permute-done.refs_1_) | copy-start | bytes 393220
  16.8 17.6 %collective-permute-start.5 = (bf16[64,1024]{1,0:T(8,128)(2,1)S(1)}, bf16[64,1024]{1,0:T(8,128)(2,1)}, u32[]{:S(2)}, u32[]{:S(2)}) collective-permute-start(bf16[64,1024]{1,0:T(8,128)(2,1)S(1)} %get-tuple-element.82), channel_id=1, source_target_pairs={{0,6},{1,7},{2,4},{3,5},{4,2},{5,3},{6,0},{7,1},{8,14},{9,15},{10,... | collective-permute-start | bytes 393224 | tf_op jit(solution)/shard_map/ppermute | solution.py:576
  25.2 12.4 %copy-start.11 = (bf16[64,1024]{1,0:T(8,128)(2,1)}, bf16[64,1024]{1,0:T(8,128)(2,1)S(1)}, u32[]{:S(2)}) copy-start(bf16[64,1024]{1,0:T(8,128)(2,1)S(1)} %collective-permute-done.1.refs_2_) | copy-start | bytes 393220
  25.2 12.4 %collective-permute-start.6 = (bf16[64,1024]{1,0:T(8,128)(2,1)S(1)}, bf16[64,1024]{1,0:T(8,128)(2,1)}, u32[]{:S(2)}, u32[]{:S(2)}) collective-permute-start(bf16[64,1024]{1,0:T(8,128)(2,1)S(1)} %get-tuple-element.83), channel_id=1, source_target_pairs={{0,7},{1,6},{2,5},{3,4},{4,3},{5,2},{6,1},{7,0},{8,15},{9,14},{10,... | collective-permute-start | bytes 393224 | tf_op jit(solution)/shard_map/ppermute | solution.py:576
  39.9 16.9 %collective-permute-start.7 = (bf16[128,1024]{1,0:T(8,128)(2,1)}, bf16[128,1024]{1,0:T(8,128)(2,1)}, u32[]{:S(2)}, u32[]{:S(2)}) collective-permute-start(bf16[128,1024]{1,0:T(8,128)(2,1)} %get-tuple-element.99.m1_ref), channel_id=1, source_target_pairs={{0,8},{1,9},{2,10},{3,11},{4,12},{5,13},{6,14},{7,15},{8,16},{9,17... | collective-permute-start | bytes 786440 | tf_op jit(solution)/shard_map/ppermute | solution.py:572
  43.6 17.9 %collective-permute-start.9 = (bf16[128,1024]{1,0:T(8,128)(2,1)}, bf16[128,1024]{1,0:T(8,128)(2,1)}, u32[]{:S(2)}, u32[]{:S(2)}) collective-permute-start(bf16[128,1024]{1,0:T(8,128)(2,1)} %get-tuple-element.101.g0_ref), channel_id=1, source_target_pairs={{8,0},{9,1},{10,2},{11,3},{12,4},{13,5},{14,6},{15,7},{16,8},{17,9... | collective-permute-start | bytes 786440 | tf_op jit(solution)/shard_map/ppermute | solution.py:572
  50.5 39.2 %all-to-all-start.1 = ((bf16[32,96,128]{2,1,0:T(8,128)(2,1)}), bf16[32,96,128]{2,1,0:T(8,128)(2,1)S(1)}, u32[]{:S(2)}, u32[]{:S(2)}) async-start(bf16[32,96,128]{2,1,0:T(8,128)(2,1)} %attn_head.1), calls=%async_computation.1 | async-start | bytes 1572864 | tf_op jit(solution)/shard_map/all_to_all | solution.py:615
  67.5 5.0 %collective-permute-start.10 = (bf16[64,1024]{1,0:T(8,128)(2,1)S(1)}, bf16[64,1024]{1,0:T(8,128)(2,1)S(1)}, u32[]{:S(2)}, u32[]{:S(2)}) collective-permute-start(bf16[64,1024]{1,0:T(8,128)(2,1)S(1)} %get-tuple-element.107), channel_id=1, source_target_pairs={{0,1},{1,0},{2,3},{3,2},{4,5},{5,4},{6,7},{7,6},{8,9},{9,8},{10,11... | collective-permute-start | bytes 393224 | tf_op jit(solution)/shard_map/ppermute | solution.py:576
  67.7 8.9 %collective-permute-start.11 = (bf16[64,1024]{1,0:T(8,128)(2,1)S(1)}, bf16[64,1024]{1,0:T(8,128)(2,1)S(1)}, u32[]{:S(2)}, u32[]{:S(2)}) collective-permute-start(bf16[64,1024]{1,0:T(8,128)(2,1)S(1)} %get-tuple-element.109), channel_id=1, source_target_pairs={{0,2},{1,3},{2,0},{3,1},{4,6},{5,7},{6,4},{7,5},{8,10},{9,11},{10,... | collective-permute-start | bytes 393224 | tf_op jit(solution)/shard_map/ppermute | solution.py:576
  69.4 8.2 %collective-permute-start.12 = (bf16[64,1024]{1,0:T(8,128)(2,1)S(1)}, bf16[64,1024]{1,0:T(8,128)(2,1)S(1)}, u32[]{:S(2)}, u32[]{:S(2)}) collective-permute-start(bf16[64,1024]{1,0:T(8,128)(2,1)S(1)} %get-tuple-element.110), channel_id=1, source_target_pairs={{0,3},{1,2},{2,1},{3,0},{4,7},{5,6},{6,5},{7,4},{8,11},{9,10},{10,... | collective-permute-start | bytes 393224 | tf_op jit(solution)/shard_map/ppermute | solution.py:576
  69.5 4.1 %collective-permute-start.8 = (f32[64,128]{1,0:T(8,128)S(1)}, f32[64,128]{1,0:T(8,128)S(1)}, u32[]{:S(2)}, u32[]{:S(2)}) collective-permute-start(f32[64,128]{1,0:T(8,128)S(1)} %conv_filter_grad.1), channel_id=1, source_target_pairs={{0,8},{1,9},{2,10},{3,11},{4,12},{5,13},{6,14},{7,15},{8,0},{9,1},... | collective-permute-start | bytes 98312 | tf_op jit(solution)/shard_map/ppermute | solution.py:576
  71.1 9.0 %collective-permute-start.13 = (bf16[64,1024]{1,0:T(8,128)(2,1)S(1)}, bf16[64,1024]{1,0:T(8,128)(2,1)S(1)}, u32[]{:S(2)}, u32[]{:S(2)}) collective-permute-start(bf16[64,1024]{1,0:T(8,128)(2,1)S(1)} %get-tuple-element.117), channel_id=1, source_target_pairs={{0,4},{1,5},{2,6},{3,7},{4,0},{5,1},{6,2},{7,3},{8,12},{9,13},{10,... | collective-permute-start | bytes 393224 | tf_op jit(solution)/shard_map/ppermute | solution.py:576
  72.5 12.9 %collective-permute-start.14 = (bf16[64,1024]{1,0:T(8,128)(2,1)S(1)}, bf16[64,1024]{1,0:T(8,128)(2,1)S(1)}, u32[]{:S(2)}, u32[]{:S(2)}) collective-permute-start(bf16[64,1024]{1,0:T(8,128)(2,1)S(1)} %get-tuple-element.118), channel_id=1, source_target_pairs={{0,5},{1,4},{2,7},{3,6},{4,1},{5,0},{6,3},{7,2},{8,13},{9,12},{10,... | collective-permute-start | bytes 393224 | tf_op jit(solution)/shard_map/ppermute | solution.py:576
  73.6 11.9 %collective-permute-start.15 = (bf16[64,1024]{1,0:T(8,128)(2,1)S(1)}, bf16[64,1024]{1,0:T(8,128)(2,1)S(1)}, u32[]{:S(2)}, u32[]{:S(2)}) collective-permute-start(bf16[64,1024]{1,0:T(8,128)(2,1)S(1)} %get-tuple-element.119), channel_id=1, source_target_pairs={{0,6},{1,7},{2,4},{3,5},{4,2},{5,3},{6,0},{7,1},{8,14},{9,15},{10,... | collective-permute-start | bytes 393224 | tf_op jit(solution)/shard_map/ppermute | solution.py:576
  76.6 8.9 %collective-permute-start.16 = (bf16[64,1024]{1,0:T(8,128)(2,1)S(1)}, bf16[64,1024]{1,0:T(8,128)(2,1)S(1)}, u32[]{:S(2)}, u32[]{:S(2)}) collective-permute-start(bf16[64,1024]{1,0:T(8,128)(2,1)S(1)} %get-tuple-element.120), channel_id=1, source_target_pairs={{0,7},{1,6},{2,5},{3,4},{4,3},{5,2},{6,1},{7,0},{8,15},{9,14},{10,... | collective-permute-start | bytes 393224 | tf_op jit(solution)/shard_map/ppermute | solution.py:576
  77.6 7.8 %collective-permute-start.17 = (f32[64,128]{1,0:T(8,128)S(1)}, f32[64,128]{1,0:T(8,128)S(1)}, u32[]{:S(2)}, u32[]{:S(2)}) collective-permute-start(f32[64,128]{1,0:T(8,128)S(1)} %add.10), channel_id=1, source_target_pairs={{0,16},{1,17},{2,18},{3,19},{4,20},{5,21},{6,22},{7,23},{8,24},{9,... | collective-permute-start | bytes 98312 | tf_op jit(solution)/shard_map/ppermute | solution.py:576
  85.7 3.9 %collective-permute-start.18 = (f32[64,128]{1,0:T(8,128)S(1)}, f32[64,128]{1,0:T(8,128)S(1)}, u32[]{:S(2)}, u32[]{:S(2)}) collective-permute-start(f32[64,128]{1,0:T(8,128)S(1)} %pad_maximum_fusion.1.mine_ref), channel_id=1, source_target_pairs={{0,4},{1,5},{2,6},{3,7},{4,0},{5,1},{6,2},{7,3},{8,12},{9,13},{10,... | collective-permute-start | bytes 98312 | tf_op jit(solution)/shard_map/ppermute | solution.py:576
  (10 other events, 58.7 us)

commit v6 on v5

--- a/solution.py
+++ b/solution.py
@@ -189,7 +189,7 @@
         visible = (k_pos >= start) & (k_pos <= q_pos[0:1])
         scores = jnp.where(visible, dot(keys, query, NT) * scale, NEG_FILL)
         top = jnp.max(scores, axis=0, keepdims=True)
-        weights = jnp.where(visible, jnp.exp(scores - top), 0.0)
+        weights = jnp.exp(scores - top)
         probs = weights * (1.0 / jnp.sum(weights, axis=0, keepdims=True))
         grad_probs = dot(values, grad, NT)
         grad_scores = probs * (grad_probs - delta)

time: 91.3 us -> 91.2 us (level)
  no operation moved by 1% of the time
where the time goes in v6:
time: 91.2 us; the launch traced here: 90.7 us
  starting transfers between devices  37.6 us (41%)
  Pallas kernels  25 us (27%)
  waiting for transfers between devices  24.3 us (27%)
  local copies, waits for them, and re-layouts  1.94 us (2%)
  between operations  0.97 us (1%)
    ppermute x17, waiting for transfers between devices, exchanged(): lax.ppermute(block, DEVICES, [(i, i ^ distance) for i in range(count)])  24.3 us
    ppermute x17, starting transfers between devices, exchanged(): lax.ppermute(block, DEVICES, [(i, i ^ distance) for i in range(count)])  18.9 us
    all_to_all x1, starting transfers between devices, body(): lax.all_to_all(attn_packed, DEVICES, split_axis=0, concat_axis=0, tiled=T...  7.3 us
    all_to_all x1, starting transfers between devices, body(): lax.all_to_all(attn_back, DEVICES, split_axis=0, concat_axis=0, tiled=True)  6.33 us
    pallas_call x1, Pallas kernels, conv_core(): pl.pallas_call(functools.partial(conv_core_kernel, rows, inner, ch_count)...  5.98 us
    pallas_call x1, Pallas kernels, attn_head(): pl.pallas_call(functools.partial(attn_kernel, rows, reach), in_specs=[pl....  5.41 us
    ppermute x2, starting transfers between devices, shifted(): return lax.ppermute(block, DEVICES, route)  5.06 us
    pallas_call x1, Pallas kernels, conv_filter_grad(): pl.pallas_call(functools.partial(conv_filter_kernel, rows, inner, ch_coun...  3.79 us
  transfers between devices with their start and end apart: 21, of which 9 were waited for; matrix products, arithmetic and copies ran while one was open for 1% of the time, Pallas kernels for 24%

profile of v6, /device:TPU:0, one launch (start us, length us, event | category | flops | bytes accessed | tf_op | source)
XLA Modules:
  0.0 90.7 jit_solution(705231023040412065)
XLA Ops:
  0.6 2.6 %attn_pack.1 = bf16[32,144,128]{2,1,0:T(8,128)(2,1)} custom-call(bf16[32,4096]{1,0:T(8,128)(2,1)} %q_ref.1, bf16[32,4096]{1,0:T(8,128)(2,1)} %k_ref.1, bf16[32,4096]{1,0:T(8,128)(2,1)} %v_ref.1, bf16[32,4096]{1,0:T(8,128)(2,1)} %o_ref.1, bf16[32,4096]{1,0:T(8,128)(2,1)} %g_ref.1), custom_call_target="tpu_custom_call" | custom-call | flops 524288 | bytes 2621440 | tf_op jit(solution)/shard_map/attn_pack/pallas_call | solution.py:155
  3.3 7.3 %all-to-all-start = ((bf16[32,144,128]{2,1,0:T(8,128)(2,1)}), bf16[32,144,128]{2,1,0:T(8,128)(2,1)S(1)}, u32[]{:S(2)}, u32[]{:S(2)}) async-start(bf16[32,144,128]{2,1,0:T(8,128)(2,1)} %attn_pack.1), calls=%async_computation | async-start | bytes 2359296 | tf_op jit(solution)/shard_map/all_to_all | solution.py:596
  10.6 1.8 %conv_pack.1 = (bf16[64,1024]{1,0:T(8,128)(2,1)S(1)}, bf16[64,1024]{1,0:T(8,128)(2,1)}, bf16[64,1024]{1,0:T(8,128)(2,1)}, bf16[64,1024]{1,0:T(8,128)(2,1)}, bf16...) custom-call(bf16[32,8192]{1,0:T(8,128)(2,1)S(1)} %copy-done.3, ...), custom_call_target="tpu_custom_call" | custom-call | flops 1048576 | bytes 3145728 | tf_op jit(solution)/shard_map/conv_pack/pallas_call | solution.py:81
  13.3 1.7 %collective-permute-start.1 = (bf16[64,1024]{1,0:T(8,128)(2,1)}, bf16[64,1024]{1,0:T(8,128)(2,1)S(1)}, u32[]{:S(2)}, u32[]{:S(2)}) collective-permute-start(bf16[64,1024]{1,0:T(8,128)(2,1)} %get-tuple-element.78), channel_id=1, source_target_pairs={{0,2},{1,3},{2,0},{3,1},{4,6},{5,7},{6,4},{7,5},{8,10},{9,11},{10,... | collective-permute-start | bytes 393224 | tf_op jit(solution)/shard_map/ppermute | solution.py:576
  15.0 1.7 %collective-permute-start.3 = (bf16[64,1024]{1,0:T(8,128)(2,1)}, bf16[64,1024]{1,0:T(8,128)(2,1)}, u32[]{:S(2)}, u32[]{:S(2)}) collective-permute-start(bf16[64,1024]{1,0:T(8,128)(2,1)} %get-tuple-element.80), channel_id=1, source_target_pairs={{0,4},{1,5},{2,6},{3,7},{4,0},{5,1},{6,2},{7,3},{8,12},{9,13},{10,... | collective-permute-start | bytes 393224 | tf_op jit(solution)/shard_map/ppermute | solution.py:576
  16.8 2.6 %collective-permute-start.5 = (bf16[64,1024]{1,0:T(8,128)(2,1)S(1)}, bf16[64,1024]{1,0:T(8,128)(2,1)}, u32[]{:S(2)}, u32[]{:S(2)}) collective-permute-start(bf16[64,1024]{1,0:T(8,128)(2,1)S(1)} %get-tuple-element.82), channel_id=1, source_target_pairs={{0,6},{1,7},{2,4},{3,5},{4,2},{5,3},{6,0},{7,1},{8,14},{9,15},{10,... | collective-permute-start | bytes 393224 | tf_op jit(solution)/shard_map/ppermute | solution.py:576
  19.4 5.8 %collective-permute-done.1.refs_2_ = bf16[64,1024]{1,0:T(8,128)(2,1)S(1)} collective-permute-done((bf16[64,1024]{1,0:T(8,128)(2,1)}, bf16[64,1024]{1,0:T(8,128)(2,1)S(1)}, u32[]{:S(2)}, u32[]{:S(2)}) %collective-permute-start.1) | collective-permute-done | bytes 131104 | tf_op jit(solution)/shard_map/ppermute | solution.py:576
  27.1 1.9 %collective-permute-done.2.refs_3_ = bf16[64,1024]{1,0:T(8,128)(2,1)S(1)} collective-permute-done((bf16[64,1024]{1,0:T(8,128)(2,1)}, bf16[64,1024]{1,0:T(8,128)(2,1)S(1)}, u32[]{:S(2)}, u32[]{:S(2)}) %collective-permute-start.2) | collective-permute-done | bytes 131104 | tf_op jit(solution)/shard_map/ppermute | solution.py:576
  29.2 5.3 %collective-permute-done.5.refs_6_ = bf16[64,1024]{1,0:T(8,128)(2,1)} collective-permute-done((bf16[64,1024]{1,0:T(8,128)(2,1)S(1)}, bf16[64,1024]{1,0:T(8,128)(2,1)}, u32[]{:S(2)}, u32[]{:S(2)}) %collective-permute-start.5) | collective-permute-done | bytes 131104 | tf_op jit(solution)/shard_map/ppermute | solution.py:576
  34.5 3.2 %collective-permute-done.6.refs_7_ = bf16[64,1024]{1,0:T(8,128)(2,1)} collective-permute-done((bf16[64,1024]{1,0:T(8,128)(2,1)S(1)}, bf16[64,1024]{1,0:T(8,128)(2,1)}, u32[]{:S(2)}, u32[]{:S(2)}) %collective-permute-start.6) | collective-permute-done | bytes 131104 | tf_op jit(solution)/shard_map/ppermute | solution.py:576
  37.6 2.2 %conv_join.1 = (bf16[128,1024]{1,0:T(8,128)(2,1)}, bf16[128,1024]{1,0:T(8,128)(2,1)}, bf16[128,1024]{1,0:T(8,128)(2,1)}, bf16[128,1024]{1,0:T(8,128)(2,1)}) custom-call(bf16[64,1024]{1,0:T(8,128)(2,1)} %copy-done.4, bf16[64,1024]{1,0:T(8,128)(2,1)} %copy-done.10, bf16[64,1024]{1,0:T(8,128)(2,1)} %copy-done.11, bf16[64,1024]{1,0:T(8,128)(2,1)} %copy-done.12, ...), custom_call_target="tpu_custom_call" | custom-call | bytes 2097152 | tf_op jit(solution)/shard_map/conv_join/pallas_call | solution.py:113
  39.9 3.8 %collective-permute-start.7 = (bf16[128,1024]{1,0:T(8,128)(2,1)}, bf16[128,1024]{1,0:T(8,128)(2,1)}, u32[]{:S(2)}, u32[]{:S(2)}) collective-permute-start(bf16[128,1024]{1,0:T(8,128)(2,1)} %get-tuple-element.99.m1_ref), channel_id=1, source_target_pairs={{0,8},{1,9},{2,10},{3,11},{4,12},{5,13},{6,14},{7,15},{8,16},{9,17... | collective-permute-start | bytes 786440 | tf_op jit(solution)/shard_map/ppermute | solution.py:572
  43.6 1.3 %collective-permute-start.9 = (bf16[128,1024]{1,0:T(8,128)(2,1)}, bf16[128,1024]{1,0:T(8,128)(2,1)}, u32[]{:S(2)}, u32[]{:S(2)}) collective-permute-start(bf16[128,1024]{1,0:T(8,128)(2,1)} %get-tuple-element.101.g0_ref), channel_id=1, source_target_pairs={{8,0},{9,1},{10,2},{11,3},{12,4},{13,5},{14,6},{15,7},{16,8},{17,9... | collective-permute-start | bytes 786440 | tf_op jit(solution)/shard_map/ppermute | solution.py:572
  44.9 5.4 %attn_head.1 = bf16[32,96,128]{2,1,0:T(8,128)(2,1)} custom-call(s32[12]{0:T(128)S(1)} %copy-done.5, bf16[32,144,128]{2,1,0:T(8,128)(2,1)S(1)} %all-to-all-done.x_ref), custom_call_target="tpu_custom_call" | custom-call | flops 1024 | bytes 589824 | tf_op jit(solution)/shard_map/attn_head/pallas_call | solution.py:220
  50.4 6.3 %all-to-all-start.1 = ((bf16[32,96,128]{2,1,0:T(8,128)(2,1)}), bf16[32,96,128]{2,1,0:T(8,128)(2,1)S(1)}, u32[]{:S(2)}, u32[]{:S(2)}) async-start(bf16[32,96,128]{2,1,0:T(8,128)(2,1)} %attn_head.1), calls=%async_computation.1 | async-start | bytes 1572864 | tf_op jit(solution)/shard_map/all_to_all | solution.py:615
  57.7 3.8 %conv_filter_grad.1 = f32[64,128]{1,0:T(8,128)S(1)} custom-call(s32[12]{0:T(128)S(1)} %copy-done.5, bf16[128,1024]{1,0:T(8,128)(2,1)} %collective-permute-done.7.prior_ref, bf16[128,1024]{1,0:T(8,128)(2,1)S(1)} %copy-done.6, bf16[128,1024]{1,0:T(8,128)(2,1)S(1)} %copy-done.7, bf16[128,1024]{1,0:T(8,128)(2,1)S(1)} %copy-done.8, bf16[128,1024]{1,0:T(8,128)(2,1)S(1)} %copy-done.9), custom_call_target="tpu_custom_call" | custom-call | flops 536870912 | bytes 1310720 | tf_op jit(solution)/shard_map/conv_filter_grad/pallas_call | solution.py:395
  61.5 6.0 %conv_core.1 = (bf16[64,1024]{1,0:T(8,128)(2,1)S(1)}, bf16[64,1024]{1,0:T(8,128)(2,1)S(1)}, bf16[64,1024]{1,0:T(8,128)(2,1)S(1)}, bf16[64,1024]{1,0:T(8,128)(2,1...) custom-call(s32[12]{0:T(128)S(1)} %copy-done.5, ...), custom_call_target="tpu_custom_call" | custom-call | flops 33554432000 | bytes 3145728 | tf_op jit(solution)/shard_map/conv_core/pallas_call | solution.py:353
  67.6 1.7 %collective-permute-start.11 = (bf16[64,1024]{1,0:T(8,128)(2,1)S(1)}, bf16[64,1024]{1,0:T(8,128)(2,1)S(1)}, u32[]{:S(2)}, u32[]{:S(2)}) collective-permute-start(bf16[64,1024]{1,0:T(8,128)(2,1)S(1)} %get-tuple-element.109), channel_id=1, source_target_pairs={{0,2},{1,3},{2,0},{3,1},{4,6},{5,7},{6,4},{7,5},{8,10},{9,11},{10,... | collective-permute-start | bytes 393224 | tf_op jit(solution)/shard_map/ppermute | solution.py:576
  69.4 1.6 %collective-permute-start.8 = (f32[64,128]{1,0:T(8,128)S(1)}, f32[64,128]{1,0:T(8,128)S(1)}, u32[]{:S(2)}, u32[]{:S(2)}) collective-permute-start(f32[64,128]{1,0:T(8,128)S(1)} %conv_filter_grad.1), channel_id=1, source_target_pairs={{0,8},{1,9},{2,10},{3,11},{4,12},{5,13},{6,14},{7,15},{8,0},{9,1},... | collective-permute-start | bytes 98312 | tf_op jit(solution)/shard_map/ppermute | solution.py:576
  71.0 1.5 %collective-permute-start.13 = (bf16[64,1024]{1,0:T(8,128)(2,1)S(1)}, bf16[64,1024]{1,0:T(8,128)(2,1)S(1)}, u32[]{:S(2)}, u32[]{:S(2)}) collective-permute-start(bf16[64,1024]{1,0:T(8,128)(2,1)S(1)} %get-tuple-element.117), channel_id=1, source_target_pairs={{0,4},{1,5},{2,6},{3,7},{4,0},{5,1},{6,2},{7,3},{8,12},{9,13},{10,... | collective-permute-start | bytes 393224 | tf_op jit(solution)/shard_map/ppermute | solution.py:576
  73.5 3.0 %collective-permute-start.15 = (bf16[64,1024]{1,0:T(8,128)(2,1)S(1)}, bf16[64,1024]{1,0:T(8,128)(2,1)S(1)}, u32[]{:S(2)}, u32[]{:S(2)}) collective-permute-start(bf16[64,1024]{1,0:T(8,128)(2,1)S(1)} %get-tuple-element.119), channel_id=1, source_target_pairs={{0,6},{1,7},{2,4},{3,5},{4,2},{5,3},{6,0},{7,1},{8,14},{9,15},{10,... | collective-permute-start | bytes 393224 | tf_op jit(solution)/shard_map/ppermute | solution.py:576
  77.5 2.5 %collective-permute-start.17 = (f32[64,128]{1,0:T(8,128)S(1)}, f32[64,128]{1,0:T(8,128)S(1)}, u32[]{:S(2)}, u32[]{:S(2)}) collective-permute-start(f32[64,128]{1,0:T(8,128)S(1)} %add.10), channel_id=1, source_target_pairs={{0,16},{1,17},{2,18},{3,19},{4,20},{5,21},{6,22},{7,23},{8,24},{9,... | collective-permute-start | bytes 98312 | tf_op jit(solution)/shard_map/ppermute | solution.py:576
  80.0 5.3 %collective-permute-done.14.refs_5_ = bf16[64,1024]{1,0:T(8,128)(2,1)S(1)} collective-permute-done((bf16[64,1024]{1,0:T(8,128)(2,1)S(1)}, bf16[64,1024]{1,0:T(8,128)(2,1)S(1)}, u32[]{:S(2)}, u32[]{:S(2)}) %collective-permute-start.14) | collective-permute-done | bytes 131104 | tf_op jit(solution)/shard_map/ppermute | solution.py:576
  86.8 2.2 %conv_unpack.1 = (bf16[32,8192]{1,0:T(8,128)(2,1)}, bf16[32,8192]{1,0:T(8,128)(2,1)}, bf16[32,8192]{1,0:T(8,128)(2,1)}) custom-call(bf16[32,8192]{1,0:T(8,128)(2,1)S(1)} %copy-done, bf16[32,8192]{1,0:T(8,128)(2,1)S(1)} %copy-done.1, bf16[32,8192]{1,0:T(8,128)(2,1)S(1)} %copy-done.2, bf16[64,1024]{1,0:T(8,128)(2,1)S(1)} %get-tuple-element.122.refs_0_, ...), custom_call_target="tpu_custom_call" | custom-call | flops 1572864 | bytes 4194304 | tf_op jit(solution)/shard_map/conv_unpack/pallas_call | solution.py:431
  (61 shorter events, 9.5 us)
Async XLA Ops:
  3.3 36.6 %all-to-all-start = ((bf16[32,144,128]{2,1,0:T(8,128)(2,1)}), bf16[32,144,128]{2,1,0:T(8,128)(2,1)S(1)}, u32[]{:S(2)}, u32[]{:S(2)}) async-start(bf16[32,144,128]{2,1,0:T(8,128)(2,1)} %attn_pack.1), calls=%async_computation | async-start | bytes 2359296 | tf_op jit(solution)/shard_map/all_to_all | solution.py:596
  13.1 31.9 %copy-start.5 = (s32[12]{0:T(128)S(1)}, s32[12]{0:T(128)}, u32[]{:S(2)}) copy-start(s32[12]{0:T(128)} %lens_ref.5) | copy-start | bytes 148
  13.1 3.7 %collective-permute-start = (bf16[64,1024]{1,0:T(8,128)(2,1)}, bf16[64,1024]{1,0:T(8,128)(2,1)S(1)}, u32[]{:S(2)}, u32[]{:S(2)}) collective-permute-start(bf16[64,1024]{1,0:T(8,128)(2,1)} %get-tuple-element.76), channel_id=1, source_target_pairs={{0,1},{1,0},{2,3},{3,2},{4,5},{5,4},{6,7},{7,6},{8,9},{9,8},{10,11... | collective-permute-start | bytes 393224 | tf_op jit(solution)/shard_map/ppermute | solution.py:576
  13.3 11.9 %collective-permute-start.1 = (bf16[64,1024]{1,0:T(8,128)(2,1)}, bf16[64,1024]{1,0:T(8,128)(2,1)S(1)}, u32[]{:S(2)}, u32[]{:S(2)}) collective-permute-start(bf16[64,1024]{1,0:T(8,128)(2,1)} %get-tuple-element.78), channel_id=1, source_target_pairs={{0,2},{1,3},{2,0},{3,1},{4,6},{5,7},{6,4},{7,5},{8,10},{9,11},{10,... | collective-permute-start | bytes 393224 | tf_op jit(solution)/shard_map/ppermute | solution.py:576
  15.0 13.9 %collective-permute-start.2 = (bf16[64,1024]{1,0:T(8,128)(2,1)}, bf16[64,1024]{1,0:T(8,128)(2,1)S(1)}, u32[]{:S(2)}, u32[]{:S(2)}) collective-permute-start(bf16[64,1024]{1,0:T(8,128)(2,1)} %get-tuple-element.79), channel_id=1, source_target_pairs={{0,3},{1,2},{2,1},{3,0},{4,7},{5,6},{6,5},{7,4},{8,11},{9,10},{10,... | collective-permute-start | bytes 393224 | tf_op jit(solution)/shard_map/ppermute | solution.py:576
  15.0 13.9 %collective-permute-start.3 = (bf16[64,1024]{1,0:T(8,128)(2,1)}, bf16[64,1024]{1,0:T(8,128)(2,1)}, u32[]{:S(2)}, u32[]{:S(2)}) collective-permute-start(bf16[64,1024]{1,0:T(8,128)(2,1)} %get-tuple-element.80), channel_id=1, source_target_pairs={{0,4},{1,5},{2,6},{3,7},{4,0},{5,1},{6,2},{7,3},{8,12},{9,13},{10,... | collective-permute-start | bytes 393224 | tf_op jit(solution)/shard_map/ppermute | solution.py:576
  16.7 12.5 %collective-permute-start.4 = (bf16[64,1024]{1,0:T(8,128)(2,1)}, bf16[64,1024]{1,0:T(8,128)(2,1)}, u32[]{:S(2)}, u32[]{:S(2)}) collective-permute-start(bf16[64,1024]{1,0:T(8,128)(2,1)} %get-tuple-element.81), channel_id=1, source_target_pairs={{0,5},{1,4},{2,7},{3,6},{4,1},{5,0},{6,3},{7,2},{8,13},{9,12},{10,... | collective-permute-start | bytes 393224 | tf_op jit(solution)/shard_map/ppermute | solution.py:576
  16.8 20.8 %copy-start.10 = (bf16[64,1024]{1,0:T(8,128)(2,1)}, bf16[64,1024]{1,0:T(8,128)(2,1)S(1)}, u32[]{:S(2)}) copy-start(bf16[64,1024]{1,0:T(8,128)(2,1)S(1)} %collective-permute-done.refs_1_) | copy-start | bytes 393220
  16.8 17.6 %collective-permute-start.5 = (bf16[64,1024]{1,0:T(8,128)(2,1)S(1)}, bf16[64,1024]{1,0:T(8,128)(2,1)}, u32[]{:S(2)}, u32[]{:S(2)}) collective-permute-start(bf16[64,1024]{1,0:T(8,128)(2,1)S(1)} %get-tuple-element.82), channel_id=1, source_target_pairs={{0,6},{1,7},{2,4},{3,5},{4,2},{5,3},{6,0},{7,1},{8,14},{9,15},{10,... | collective-permute-start | bytes 393224 | tf_op jit(solution)/shard_map/ppermute | solution.py:576
  25.2 12.4 %copy-start.11 = (bf16[64,1024]{1,0:T(8,128)(2,1)}, bf16[64,1024]{1,0:T(8,128)(2,1)S(1)}, u32[]{:S(2)}) copy-start(bf16[64,1024]{1,0:T(8,128)(2,1)S(1)} %collective-permute-done.1.refs_2_) | copy-start | bytes 393220
  25.2 12.4 %collective-permute-start.6 = (bf16[64,1024]{1,0:T(8,128)(2,1)S(1)}, bf16[64,1024]{1,0:T(8,128)(2,1)}, u32[]{:S(2)}, u32[]{:S(2)}) collective-permute-start(bf16[64,1024]{1,0:T(8,128)(2,1)S(1)} %get-tuple-element.83), channel_id=1, source_target_pairs={{0,7},{1,6},{2,5},{3,4},{4,3},{5,2},{6,1},{7,0},{8,15},{9,14},{10,... | collective-permute-start | bytes 393224 | tf_op jit(solution)/shard_map/ppermute | solution.py:576
  39.9 16.8 %collective-permute-start.7 = (bf16[128,1024]{1,0:T(8,128)(2,1)}, bf16[128,1024]{1,0:T(8,128)(2,1)}, u32[]{:S(2)}, u32[]{:S(2)}) collective-permute-start(bf16[128,1024]{1,0:T(8,128)(2,1)} %get-tuple-element.99.m1_ref), channel_id=1, source_target_pairs={{0,8},{1,9},{2,10},{3,11},{4,12},{5,13},{6,14},{7,15},{8,16},{9,17... | collective-permute-start | bytes 786440 | tf_op jit(solution)/shard_map/ppermute | solution.py:572
  43.6 17.8 %collective-permute-start.9 = (bf16[128,1024]{1,0:T(8,128)(2,1)}, bf16[128,1024]{1,0:T(8,128)(2,1)}, u32[]{:S(2)}, u32[]{:S(2)}) collective-permute-start(bf16[128,1024]{1,0:T(8,128)(2,1)} %get-tuple-element.101.g0_ref), channel_id=1, source_target_pairs={{8,0},{9,1},{10,2},{11,3},{12,4},{13,5},{14,6},{15,7},{16,8},{17,9... | collective-permute-start | bytes 786440 | tf_op jit(solution)/shard_map/ppermute | solution.py:572
  50.4 39.2 %all-to-all-start.1 = ((bf16[32,96,128]{2,1,0:T(8,128)(2,1)}), bf16[32,96,128]{2,1,0:T(8,128)(2,1)S(1)}, u32[]{:S(2)}, u32[]{:S(2)}) async-start(bf16[32,96,128]{2,1,0:T(8,128)(2,1)} %attn_head.1), calls=%async_computation.1 | async-start | bytes 1572864 | tf_op jit(solution)/shard_map/all_to_all | solution.py:615
  67.5 5.0 %collective-permute-start.10 = (bf16[64,1024]{1,0:T(8,128)(2,1)S(1)}, bf16[64,1024]{1,0:T(8,128)(2,1)S(1)}, u32[]{:S(2)}, u32[]{:S(2)}) collective-permute-start(bf16[64,1024]{1,0:T(8,128)(2,1)S(1)} %get-tuple-element.107), channel_id=1, source_target_pairs={{0,1},{1,0},{2,3},{3,2},{4,5},{5,4},{6,7},{7,6},{8,9},{9,8},{10,11... | collective-permute-start | bytes 393224 | tf_op jit(solution)/shard_map/ppermute | solution.py:576
  67.6 8.9 %collective-permute-start.11 = (bf16[64,1024]{1,0:T(8,128)(2,1)S(1)}, bf16[64,1024]{1,0:T(8,128)(2,1)S(1)}, u32[]{:S(2)}, u32[]{:S(2)}) collective-permute-start(bf16[64,1024]{1,0:T(8,128)(2,1)S(1)} %get-tuple-element.109), channel_id=1, source_target_pairs={{0,2},{1,3},{2,0},{3,1},{4,6},{5,7},{6,4},{7,5},{8,10},{9,11},{10,... | collective-permute-start | bytes 393224 | tf_op jit(solution)/shard_map/ppermute | solution.py:576
  69.3 8.3 %collective-permute-start.12 = (bf16[64,1024]{1,0:T(8,128)(2,1)S(1)}, bf16[64,1024]{1,0:T(8,128)(2,1)S(1)}, u32[]{:S(2)}, u32[]{:S(2)}) collective-permute-start(bf16[64,1024]{1,0:T(8,128)(2,1)S(1)} %get-tuple-element.110), channel_id=1, source_target_pairs={{0,3},{1,2},{2,1},{3,0},{4,7},{5,6},{6,5},{7,4},{8,11},{9,10},{10,... | collective-permute-start | bytes 393224 | tf_op jit(solution)/shard_map/ppermute | solution.py:576
  69.4 4.1 %collective-permute-start.8 = (f32[64,128]{1,0:T(8,128)S(1)}, f32[64,128]{1,0:T(8,128)S(1)}, u32[]{:S(2)}, u32[]{:S(2)}) collective-permute-start(f32[64,128]{1,0:T(8,128)S(1)} %conv_filter_grad.1), channel_id=1, source_target_pairs={{0,8},{1,9},{2,10},{3,11},{4,12},{5,13},{6,14},{7,15},{8,0},{9,1},... | collective-permute-start | bytes 98312 | tf_op jit(solution)/shard_map/ppermute | solution.py:576
  71.0 9.0 %collective-permute-start.13 = (bf16[64,1024]{1,0:T(8,128)(2,1)S(1)}, bf16[64,1024]{1,0:T(8,128)(2,1)S(1)}, u32[]{:S(2)}, u32[]{:S(2)}) collective-permute-start(bf16[64,1024]{1,0:T(8,128)(2,1)S(1)} %get-tuple-element.117), channel_id=1, source_target_pairs={{0,4},{1,5},{2,6},{3,7},{4,0},{5,1},{6,2},{7,3},{8,12},{9,13},{10,... | collective-permute-start | bytes 393224 | tf_op jit(solution)/shard_map/ppermute | solution.py:576
  72.5 12.9 %collective-permute-start.14 = (bf16[64,1024]{1,0:T(8,128)(2,1)S(1)}, bf16[64,1024]{1,0:T(8,128)(2,1)S(1)}, u32[]{:S(2)}, u32[]{:S(2)}) collective-permute-start(bf16[64,1024]{1,0:T(8,128)(2,1)S(1)} %get-tuple-element.118), channel_id=1, source_target_pairs={{0,5},{1,4},{2,7},{3,6},{4,1},{5,0},{6,3},{7,2},{8,13},{9,12},{10,... | collective-permute-start | bytes 393224 | tf_op jit(solution)/shard_map/ppermute | solution.py:576
  73.5 11.9 %collective-permute-start.15 = (bf16[64,1024]{1,0:T(8,128)(2,1)S(1)}, bf16[64,1024]{1,0:T(8,128)(2,1)S(1)}, u32[]{:S(2)}, u32[]{:S(2)}) collective-permute-start(bf16[64,1024]{1,0:T(8,128)(2,1)S(1)} %get-tuple-element.119), channel_id=1, source_target_pairs={{0,6},{1,7},{2,4},{3,5},{4,2},{5,3},{6,0},{7,1},{8,14},{9,15},{10,... | collective-permute-start | bytes 393224 | tf_op jit(solution)/shard_map/ppermute | solution.py:576
  76.5 8.9 %collective-permute-start.16 = (bf16[64,1024]{1,0:T(8,128)(2,1)S(1)}, bf16[64,1024]{1,0:T(8,128)(2,1)S(1)}, u32[]{:S(2)}, u32[]{:S(2)}) collective-permute-start(bf16[64,1024]{1,0:T(8,128)(2,1)S(1)} %get-tuple-element.120), channel_id=1, source_target_pairs={{0,7},{1,6},{2,5},{3,4},{4,3},{5,2},{6,1},{7,0},{8,15},{9,14},{10,... | collective-permute-start | bytes 393224 | tf_op jit(solution)/shard_map/ppermute | solution.py:576
  77.5 7.8 %collective-permute-start.17 = (f32[64,128]{1,0:T(8,128)S(1)}, f32[64,128]{1,0:T(8,128)S(1)}, u32[]{:S(2)}, u32[]{:S(2)}) collective-permute-start(f32[64,128]{1,0:T(8,128)S(1)} %add.10), channel_id=1, source_target_pairs={{0,16},{1,17},{2,18},{3,19},{4,20},{5,21},{6,22},{7,23},{8,24},{9,... | collective-permute-start | bytes 98312 | tf_op jit(solution)/shard_map/ppermute | solution.py:576
  85.6 3.9 %collective-permute-start.18 = (f32[64,128]{1,0:T(8,128)S(1)}, f32[64,128]{1,0:T(8,128)S(1)}, u32[]{:S(2)}, u32[]{:S(2)}) collective-permute-start(f32[64,128]{1,0:T(8,128)S(1)} %pad_maximum_fusion.1.mine_ref), channel_id=1, source_target_pairs={{0,4},{1,5},{2,6},{3,7},{4,0},{5,1},{6,2},{7,3},{8,12},{9,13},{10,... | collective-permute-start | bytes 98312 | tf_op jit(solution)/shard_map/ppermute | solution.py:576
  (10 other events, 58.8 us)
